TPU v7x, 32 devices: a whole 2x2x4 slice. The times are simulated.
32 devices in a mesh: slab: 4 (over y, x), row: 2 (over core), col: 4 (over z).
Axes of the slice: x: 2, y: 2, z: 4, core: 2. Of those that a mesh axis runs over, the one named last changes fastest.
Arguments:
- sources: float32 [4, 4, 2, 1536, 256], P('slab', 'col', 'row'), may hold values from -6 to 6
- tr_vals: float32 [4, 4, 2, 24, 12, 128, 128], P('slab', 'col', 'row'), may hold values from -0.09375 to 0.09375
- tr_cols: int32 [4, 4, 2, 24, 12], P('slab', 'col', 'row'), may hold values from 0 to 47, as said below
- rf_vals: float32 [4, 4, 2, 24, 12, 128, 128], P('slab', 'col', 'row'), may hold values from -0.078125 to 0.078125
- rf_cols: int32 [4, 4, 2, 24, 12], P('slab', 'col', 'row'), may hold values from 0 to 47, as said below
Outputs:
- total_traces: float32 [4, 4, 2, 1536, 256], P('slab', 'col', 'row')
Inputs may be any that keep to these rules, and one draw needn't show every extreme that they name: `tr_cols`: each block row lists 12 different column blocks of its column group. `rf_cols`: each block row lists 12 different column blocks of its column group.
All inputs are finite; a program needn't handle non-finite values.
Results may differ from a plain program's by a relative error of at most 0.0001.
Values sent between devices are 32-bit elements; how exact they have to be, the bound alone decides.
No kernel may reach another device: no remote copies, remote signals or barrier semaphores. Data moves between devices by JAX's collectives and lax.ppermute only.
A program may use at most 192 MiB of HBM per device.

v0:
```python
import jax
import jax.numpy as jnp
from jax import lax
from jax.sharding import PartitionSpec as P


def passed_along(value, axis, steps):
    count = lax.axis_size(axis)
    initial, last = (max(0, -steps), min(count, count - steps))
    return lax.ppermute(value, axis, [(source, source + steps) for source in range(initial, last)])


def local_product(values, columns, gathered, span):
    block_size = values.shape[-1]
    tiles = gathered.reshape(-1, block_size, span)
    picked = tiles[columns]
    result = jnp.einsum("rkab,rkbw->raw", values, picked, precision=lax.Precision.HIGHEST)
    return result.reshape(-1, span)


def shards(sources, tr_vals, tr_cols, rf_vals, rf_cols):
    source_part = sources[0, 0, 0]
    trans_values = tr_vals[0, 0, 0]
    trans_index = tr_cols[0, 0, 0]
    refl_values = rf_vals[0, 0, 0]
    refl_index = rf_cols[0, 0, 0]
    piece_rows = source_part.shape[0]
    columns_total = source_part.shape[1]
    batch_count = 2
    span = columns_total // batch_count
    length = lax.axis_size("slab")
    position = lax.axis_index("slab")
    carry = jnp.zeros((piece_rows, span), jnp.float32)
    down_store = jnp.zeros_like(source_part)
    refl_store = jnp.zeros_like(source_part)
    for moment in range(length + batch_count - 1):
        incoming = passed_along(carry, "slab", 1)
        which = moment - position
        valid = (which >= 0) & (which < batch_count)
        offset = jnp.clip(which, 0, batch_count - 1) * span
        incident = incoming + lax.dynamic_slice_in_dim(source_part, offset, span, 1)
        gathered = lax.all_gather(incident, "col", axis=0, tiled=True)
        trans_part = local_product(trans_values, trans_index, gathered, span)
        refl_part = local_product(refl_values, refl_index, gathered, span)
        moved, reflected = (
            lax.psum_scatter(trans_part, "row", scatter_dimension=0, tiled=True),
            lax.psum_scatter(refl_part, "row", scatter_dimension=0, tiled=True),
        )
        down_store = jnp.where(
            valid, lax.dynamic_update_slice_in_dim(down_store, moved, offset, 1), down_store
        )
        refl_store = jnp.where(
            valid, lax.dynamic_update_slice_in_dim(refl_store, reflected, offset, 1), refl_store
        )
        carry = moved
    carry = jnp.zeros((piece_rows, span), jnp.float32)
    up_store = jnp.zeros_like(source_part)
    for moment in range(length + batch_count - 1):
        incoming = passed_along(carry, "slab", -1)
        which = moment - (length - 1 - position)
        valid = (which >= 0) & (which < batch_count)
        offset = jnp.clip(which, 0, batch_count - 1) * span
        incident = incoming + lax.dynamic_slice_in_dim(refl_store, offset, span, 1)
        gathered = lax.all_gather(incident, "col", axis=0, tiled=True)
        trans_part = local_product(trans_values, trans_index, gathered, span)
        moved = lax.psum_scatter(trans_part, "row", scatter_dimension=0, tiled=True)
        up_store = jnp.where(
            valid, lax.dynamic_update_slice_in_dim(up_store, moved, offset, 1), up_store
        )
        carry = moved
    return (down_store + up_store)[None, None, None]


def solution(mesh):
    placed = (
        P("slab", "col", "row", None, None),
        P("slab", "col", "row", None, None, None, None),
        P("slab", "col", "row", None, None),
        P("slab", "col", "row", None, None, None, None),
        P("slab", "col", "row", None, None),
    )
    return jax.shard_map(
        shards,
        mesh=mesh,
        in_specs=placed,
        out_specs=P("slab", "col", "row", None, None),
        check_vma=False,
    )
```

profile of v0, /device:TPU:0, one launch (start us, length us, event | category | flops | bytes accessed | tf_op | source)
XLA Modules:
  0.0 1450.8 jit_solution(11580355453208857878)
XLA Ops:
  31.3 64.9 %all-gather.11.cloned.1.call-done = f32[6144,128]{1,0:T(8,128)} async-done(((f32[1536,128]{1,0:T(8,128)}), f32[6144,128]{1,0:T(8,128)}) %all-gather.11.cloned.1.call-update) | async-done | bytes 3145744 | tf_op jit(solution)/shard_map/all_gather | solution.py:42
  111.5 25.7 %fusion.28 = f32[24,128,128,1]{1,2,3,0:T(8,128)} fusion(f32[24,12,128,128]{3,2,1,0:T(8,128)} %bitcast.203, f32[1,1,1,24,12,128,128]{6,5,4,3,2,1,0:T(8,128)} %param.6), kind=kOutput, calls=%fused_computation.43 | convolution fusion | flops 7247757312 | bytes 39321600 | tf_op jit(solution)/shard_map/rkab,rkbw->raw/dot_general | solution.py:17
  167.7 65.0 %all-gather.13.cloned.1.call-done = f32[6144,128]{1,0:T(8,128)} async-done(((f32[1536,128]{1,0:T(8,128)}), f32[6144,128]{1,0:T(8,128)}) %all-gather.13.cloned.1.call-update) | async-done | bytes 3145744 | tf_op jit(solution)/shard_map/all_gather | solution.py:42
  247.9 25.6 %fusion.26 = f32[24,128,128,1]{1,2,3,0:T(8,128)} fusion(f32[24,12,128,128]{3,2,1,0:T(8,128)} %bitcast.204, f32[1,1,1,24,12,128,128]{6,5,4,3,2,1,0:T(8,128)} %param.6), kind=kOutput, calls=%fused_computation.41 | convolution fusion | flops 7247757312 | bytes 39321600 | tf_op jit(solution)/shard_map/rkab,rkbw->raw/dot_general | solution.py:17
  303.7 65.3 %all-gather.15.cloned.1.call-done = f32[6144,128]{1,0:T(8,128)} async-done(((f32[1536,128]{1,0:T(8,128)}), f32[6144,128]{1,0:T(8,128)}) %all-gather.15.cloned.1.call-update) | async-done | bytes 3145744 | tf_op jit(solution)/shard_map/all_gather | solution.py:42
  384.2 25.6 %fusion.24 = f32[24,128,128,1]{1,2,3,0:T(8,128)} fusion(f32[24,12,128,128]{3,2,1,0:T(8,128)} %bitcast.205, f32[1,1,1,24,12,128,128]{6,5,4,3,2,1,0:T(8,128)} %param.6), kind=kOutput, calls=%fused_computation.39 | convolution fusion | flops 7247757312 | bytes 39321600 | tf_op jit(solution)/shard_map/rkab,rkbw->raw/dot_general | solution.py:17
  440.1 65.2 %all-gather.17.cloned.1.call-done = f32[6144,128]{1,0:T(8,128)} async-done(((f32[1536,128]{1,0:T(8,128)}), f32[6144,128]{1,0:T(8,128)}) %all-gather.17.cloned.1.call-update) | async-done | bytes 3145744 | tf_op jit(solution)/shard_map/all_gather | solution.py:42
  520.6 25.7 %fusion.22 = f32[24,128,128,1]{1,2,3,0:T(8,128)} fusion(f32[24,12,128,128]{3,2,1,0:T(8,128)} %bitcast.206, f32[1,1,1,24,12,128,128]{6,5,4,3,2,1,0:T(8,128)} %param.6), kind=kOutput, calls=%fused_computation.37 | convolution fusion | flops 7247757312 | bytes 39321600 | tf_op jit(solution)/shard_map/rkab,rkbw->raw/dot_general | solution.py:17
  586.7 26.2 %fusion.8 = f32[24,128,128,1]{1,2,3,0:T(8,128)} fusion(f32[24,12,128,128]{3,2,1,0:T(8,128)} %bitcast.193, f32[1,1,1,24,12,128,128]{6,5,4,3,2,1,0:T(8,128)} %param.8), kind=kOutput, calls=%fused_computation.23 | convolution fusion | flops 7247757312 | bytes 39321600 | tf_op jit(solution)/shard_map/rkab,rkbw->raw/dot_general | solution.py:17
  621.4 25.8 %fusion.6 = f32[24,128,128,1]{1,2,3,0:T(8,128)} fusion(f32[24,12,128,128]{3,2,1,0:T(8,128)} %bitcast.194, f32[1,1,1,24,12,128,128]{6,5,4,3,2,1,0:T(8,128)} %param.8), kind=kOutput, calls=%fused_computation.21 | convolution fusion | flops 7247757312 | bytes 39321600 | tf_op jit(solution)/shard_map/rkab,rkbw->raw/dot_general | solution.py:17
  656.1 25.7 %fusion.4 = f32[24,128,128,1]{1,2,3,0:T(8,128)} fusion(f32[24,12,128,128]{3,2,1,0:T(8,128)} %bitcast.195, f32[1,1,1,24,12,128,128]{6,5,4,3,2,1,0:T(8,128)} %param.8), kind=kOutput, calls=%fused_computation.19 | convolution fusion | flops 7247757312 | bytes 39321600 | tf_op jit(solution)/shard_map/rkab,rkbw->raw/dot_general | solution.py:17
  690.7 25.9 %fusion.2 = f32[24,128,128,1]{1,2,3,0:T(8,128)} fusion(f32[24,12,128,128]{3,2,1,0:T(8,128)} %bitcast.196, f32[1,1,1,24,12,128,128]{6,5,4,3,2,1,0:T(8,128)} %param.8), kind=kOutput, calls=%fused_computation.17 | convolution fusion | flops 7247757312 | bytes 39321600 | tf_op jit(solution)/shard_map/rkab,rkbw->raw/dot_general | solution.py:17
  732.3 25.7 %fusion = f32[24,128,128,1]{1,2,3,0:T(8,128)} fusion(f32[24,12,128,128]{3,2,1,0:T(8,128)} %bitcast.197, f32[1,1,1,24,12,128,128]{6,5,4,3,2,1,0:T(8,128)} %param.8), kind=kOutput, calls=%fused_computation.15 | convolution fusion | flops 7247757312 | bytes 39321600 | tf_op jit(solution)/shard_map/rkab,rkbw->raw/dot_general | solution.py:17
  780.9 64.6 %all-gather.21.cloned.1.call-done = f32[6144,128]{1,0:T(8,128)} async-done(((f32[1536,128]{1,0:T(8,128)}), f32[6144,128]{1,0:T(8,128)}) %all-gather.21.cloned.1.call-update) | async-done | bytes 3145744 | tf_op jit(solution)/shard_map/all_gather | solution.py:64
  860.7 25.6 %fusion.18 = f32[24,128,128,1]{1,2,3,0:T(8,128)} fusion(f32[24,12,128,128]{3,2,1,0:T(8,128)} %bitcast.198, f32[1,1,1,24,12,128,128]{6,5,4,3,2,1,0:T(8,128)} %param.6), kind=kOutput, calls=%fused_computation.33 | convolution fusion | flops 7247757312 | bytes 39321600 | tf_op jit(solution)/shard_map/rkab,rkbw->raw/dot_general | solution.py:17
  917.2 64.6 %all-gather.23.cloned.1.call-done = f32[6144,128]{1,0:T(8,128)} async-done(((f32[1536,128]{1,0:T(8,128)}), f32[6144,128]{1,0:T(8,128)}) %all-gather.23.cloned.1.call-update) | async-done | bytes 3145744 | tf_op jit(solution)/shard_map/all_gather | solution.py:64
  997.0 25.6 %fusion.16 = f32[24,128,128,1]{1,2,3,0:T(8,128)} fusion(f32[24,12,128,128]{3,2,1,0:T(8,128)} %bitcast.199, f32[1,1,1,24,12,128,128]{6,5,4,3,2,1,0:T(8,128)} %param.6), kind=kOutput, calls=%fused_computation.31 | convolution fusion | flops 7247757312 | bytes 39321600 | tf_op jit(solution)/shard_map/rkab,rkbw->raw/dot_general | solution.py:17
  1053.7 64.4 %all-gather.25.cloned.1.call-done = f32[6144,128]{1,0:T(8,128)} async-done(((f32[1536,128]{1,0:T(8,128)}), f32[6144,128]{1,0:T(8,128)}) %all-gather.25.cloned.1.call-update) | async-done | bytes 3145744 | tf_op jit(solution)/shard_map/all_gather | solution.py:64
  1133.3 25.6 %fusion.14 = f32[24,128,128,1]{1,2,3,0:T(8,128)} fusion(f32[24,12,128,128]{3,2,1,0:T(8,128)} %bitcast.200, f32[1,1,1,24,12,128,128]{6,5,4,3,2,1,0:T(8,128)} %param.6), kind=kOutput, calls=%fused_computation.29 | convolution fusion | flops 7247757312 | bytes 39321600 | tf_op jit(solution)/shard_map/rkab,rkbw->raw/dot_general | solution.py:17
  1189.8 64.7 %all-gather.27.cloned.1.call-done = f32[6144,128]{1,0:T(8,128)} async-done(((f32[1536,128]{1,0:T(8,128)}), f32[6144,128]{1,0:T(8,128)}) %all-gather.27.cloned.1.call-update) | async-done | bytes 3145744 | tf_op jit(solution)/shard_map/all_gather | solution.py:64
  1269.6 25.7 %fusion.12 = f32[24,128,128,1]{1,2,3,0:T(8,128)} fusion(f32[24,12,128,128]{3,2,1,0:T(8,128)} %bitcast.201, f32[1,1,1,24,12,128,128]{6,5,4,3,2,1,0:T(8,128)} %param.6), kind=kOutput, calls=%fused_computation.27 | convolution fusion | flops 7247757312 | bytes 39321600 | tf_op jit(solution)/shard_map/rkab,rkbw->raw/dot_general | solution.py:17
  1336.3 26.0 %fusion.20 = f32[24,128,128,1]{1,2,3,0:T(8,128)} fusion(f32[24,12,128,128]{3,2,1,0:T(8,128)} %bitcast.202, f32[1,1,1,24,12,128,128]{6,5,4,3,2,1,0:T(8,128)} %param.6), kind=kOutput, calls=%fused_computation.35 | convolution fusion | flops 7247757312 | bytes 39321600 | tf_op jit(solution)/shard_map/rkab,rkbw->raw/dot_general | solution.py:17
  1363.0 29.4 %all-gather.29.cloned.1.call-done = f32[6144,128]{1,0:T(8,128)} async-done(((f32[1536,128]{1,0:T(8,128)}), f32[6144,128]{1,0:T(8,128)}) %all-gather.29.cloned.1.call-update) | async-done | bytes 3145744 | tf_op jit(solution)/shard_map/all_gather | solution.py:64
  1407.6 25.7 %fusion.10 = f32[24,128,128,1]{1,2,3,0:T(8,128)} fusion(f32[24,12,128,128]{3,2,1,0:T(8,128)} %bitcast.192, f32[1,1,1,24,12,128,128]{6,5,4,3,2,1,0:T(8,128)} %param.6), kind=kOutput, calls=%fused_computation.25 | convolution fusion | flops 7247757312 | bytes 39321600 | tf_op jit(solution)/shard_map/rkab,rkbw->raw/dot_general | solution.py:17
  (168 shorter events, 502.1 us)
Async XLA Ops:
  6.5 89.7 %all-gather.11.cloned.1.call-start = ((), (), s32[]{:S(2)}) async-start(), calls=%async_computation.15 | async-start | bytes 3932160 | tf_op jit(solution)/shard_map/all_gather | solution.py:42
  30.4 114.7 %reduce-scatter.16.cloned.1.call-start = ((), (), s32[]{:S(2)}) async-start(), calls=%async_computation.16 | async-start | bytes 2359296 | tf_op jit(solution)/shard_map/reduce_scatter | solution.py:46
  137.2 95.5 %all-gather.13.cloned.1.call-start = ((), (), s32[]{:S(2)}) async-start(), calls=%async_computation.17 | async-start | bytes 3932160 | tf_op jit(solution)/shard_map/all_gather | solution.py:42
  167.2 114.2 %reduce-scatter.18.cloned.1.call-start = ((), (), s32[]{:S(2)}) async-start(), calls=%async_computation.18 | async-start | bytes 2359296 | tf_op jit(solution)/shard_map/reduce_scatter | solution.py:46
  273.5 95.5 %all-gather.15.cloned.1.call-start = ((), (), s32[]{:S(2)}) async-start(), calls=%async_computation.19 | async-start | bytes 3932160 | tf_op jit(solution)/shard_map/all_gather | solution.py:42
  303.5 114.2 %reduce-scatter.20.cloned.1.call-start = ((), (), s32[]{:S(2)}) async-start(), calls=%async_computation.20 | async-start | bytes 2359296 | tf_op jit(solution)/shard_map/reduce_scatter | solution.py:46
  409.8 95.5 %all-gather.17.cloned.1.call-start = ((), (), s32[]{:S(2)}) async-start(), calls=%async_computation.21 | async-start | bytes 3932160 | tf_op jit(solution)/shard_map/all_gather | solution.py:42
  439.9 114.3 %reduce-scatter.22.cloned.1.call-start = ((), (), s32[]{:S(2)}) async-start(), calls=%async_computation.22 | async-start | bytes 2359296 | tf_op jit(solution)/shard_map/reduce_scatter | solution.py:46
  546.3 170.8 %all-gather.19.cloned.1.call-start = ((), (), s32[]{:S(2)}) async-start(), calls=%async_computation.23 | async-start | bytes 3932160 | tf_op jit(solution)/shard_map/all_gather | solution.py:42
  577.7 181.8 %reduce-scatter.26.cloned.1.call-start = ((), (), s32[]{:S(2)}) async-start(), calls=%async_computation.25 | async-start | bytes 2359296 | tf_op jit(solution)/shard_map/reduce_scatter | solution.py:47
  612.9 147.9 %reduce-scatter.28.cloned.1.call-start = ((), (), s32[]{:S(2)}) async-start(), calls=%async_computation.26 | async-start | bytes 2359296 | tf_op jit(solution)/shard_map/reduce_scatter | solution.py:47
  647.2 114.9 %reduce-scatter.30.cloned.1.call-start = ((), (), s32[]{:S(2)}) async-start(), calls=%async_computation.27 | async-start | bytes 2359296 | tf_op jit(solution)/shard_map/reduce_scatter | solution.py:47
  681.8 80.5 %reduce-scatter.32.cloned.1.call-start = ((), (), s32[]{:S(2)}) async-start(), calls=%async_computation.28 | async-start | bytes 2359296 | tf_op jit(solution)/shard_map/reduce_scatter | solution.py:47
  758.0 87.5 %all-gather.21.cloned.1.call-start = ((), (), s32[]{:S(2)}) async-start(), calls=%async_computation.30 | async-start | bytes 3932160 | tf_op jit(solution)/shard_map/all_gather | solution.py:64
  780.7 113.5 %reduce-scatter.36.cloned.1.call-start = ((), (), s32[]{:S(2)}) async-start(), calls=%async_computation.31 | async-start | bytes 2359296 | tf_op jit(solution)/shard_map/reduce_scatter | solution.py:66
  886.3 95.5 %all-gather.23.cloned.1.call-start = ((), (), s32[]{:S(2)}) async-start(), calls=%async_computation.32 | async-start | bytes 3932160 | tf_op jit(solution)/shard_map/all_gather | solution.py:64
  917.0 113.5 %reduce-scatter.38.cloned.1.call-start = ((), (), s32[]{:S(2)}) async-start(), calls=%async_computation.33 | async-start | bytes 2359296 | tf_op jit(solution)/shard_map/reduce_scatter | solution.py:66
  1022.6 95.5 %all-gather.25.cloned.1.call-start = ((), (), s32[]{:S(2)}) async-start(), calls=%async_computation.34 | async-start | bytes 3932160 | tf_op jit(solution)/shard_map/all_gather | solution.py:64
  1053.3 113.5 %reduce-scatter.40.cloned.1.call-start = ((), (), s32[]{:S(2)}) async-start(), calls=%async_computation.35 | async-start | bytes 2359296 | tf_op jit(solution)/shard_map/reduce_scatter | solution.py:66
  1158.9 95.5 %all-gather.27.cloned.1.call-start = ((), (), s32[]{:S(2)}) async-start(), calls=%async_computation.36 | async-start | bytes 3932160 | tf_op jit(solution)/shard_map/all_gather | solution.py:64
  1189.6 113.7 %reduce-scatter.42.cloned.1.call-start = ((), (), s32[]{:S(2)}) async-start(), calls=%async_computation.37 | async-start | bytes 2359296 | tf_op jit(solution)/shard_map/reduce_scatter | solution.py:66
  1295.4 97.0 %all-gather.29.cloned.1.call-start = ((), (), s32[]{:S(2)}) async-start(), calls=%async_computation.38 | async-start | bytes 3932160 | tf_op jit(solution)/shard_map/all_gather | solution.py:64
  1327.5 106.1 %reduce-scatter.24.cloned.1.call-start = ((), (), s32[]{:S(2)}) async-start(), calls=%async_computation.24 | async-start | bytes 2359296 | tf_op jit(solution)/shard_map/reduce_scatter | solution.py:46
  1362.3 78.8 %reduce-scatter.44.cloned.1.call-start = ((), (), s32[]{:S(2)}) async-start(), calls=%async_computation.39 | async-start | bytes 2359296 | tf_op jit(solution)/shard_map/reduce_scatter | solution.py:66
  (26 other events, 1759.2 us)
Sparse Core Ops, SparseCore 0:
  30.5 65.7 all-gather.10
  137.3 7.6 reduce-scatter.15
  167.3 65.3 all-gather.12
  303.6 65.3 all-gather.14
  410.0 7.6 reduce-scatter.19
  440.0 65.3 all-gather.16
  546.4 7.6 reduce-scatter.21
  577.8 65.4 all-gather.18
  645.4 7.7 reduce-scatter.25
  655.5 10.2 reduce-scatter.27
  681.9 10.8 reduce-scatter.29
  716.7 10.7 reduce-scatter.31
  758.2 10.7 reduce-scatter.33
  780.8 64.6 all-gather.20
  886.4 7.6 reduce-scatter.35
  917.1 64.6 all-gather.22
  1022.7 7.6 reduce-scatter.37
  1053.4 64.6 all-gather.24
  1159.0 7.6 reduce-scatter.39
  1189.7 64.7 all-gather.26
  1295.5 7.6 reduce-scatter.41
  1327.7 64.6 all-gather.28
  1394.6 7.6 reduce-scatter.23
  1433.4 7.6 reduce-scatter.43
  (1 shorter events, 7.6 us)
where the time goes:
time: 1460 us; the launch traced here: 1450 us
  waiting for transfers between devices  802 us (55%)
  matrix products  386 us (26%)
  local copies, waits for them, and re-layouts  195 us (13%)
  starting transfers between devices  31.7 us (2%)
  other arithmetic  22.1 us (2%)
    all_gather x10, waiting for transfers between devices, shards(): gathered = lax.all_gather(incident, 'col', axis=0, tiled=True)  548 us
    dot_general x15, matrix products, local_product(): jnp.einsum('rkab,rkbw->raw', values, picked, precision=lax.Precision.HIGH...  386 us
    gather x15, local copies, waits for them, and re-layouts, local_product(): picked = tiles[columns]  194 us
    ppermute x10, waiting for transfers between devices, passed_along(): lax.ppermute(value, axis, [(source, source + steps) for source in range(i...  179 us
    reduce_scatter x5, waiting for transfers between devices, shards(): moved = lax.psum_scatter(trans_part, 'row', scatter_dimension=0, tiled=True)  36.8 us
    reduce_scatter x5, waiting for transfers between devices, shards(): lax.psum_scatter(trans_part, 'row', scatter_dimension=0, tiled=True)  31.2 us
  transfers between devices with their start and end apart: 35, of which 29 were waited for; matrix products, arithmetic and copies ran while one was open for 18% of the time, Pallas kernels for 0%

commit v1 on v0

v1 whole, which is shorter than its diff:
```python
import functools

import jax
import jax.numpy as jnp
from jax import lax
from jax.experimental import pallas as pl
from jax.experimental.pallas import tpu as pltpu
from jax.sharding import PartitionSpec as P

BATCHES = 8
DELAY = 2


def divisor_up_to(number, limit):
    return max(n for n in range(1, limit + 1) if number % n == 0)


def passed_along(value, axis, steps):
    count = lax.axis_size(axis)
    initial, last = (max(0, -steps), min(count, count - steps))
    return lax.ppermute(value, axis, [(source, source + steps) for source in range(initial, last)])


def split_kernel(values_ref, parts_ref):
    for k in range(values_ref.shape[1]):
        value = values_ref[0, k]
        high = value.astype(jnp.bfloat16)
        size = value.shape[0]
        parts_ref[0, k, :size] = high
        parts_ref[0, k, size:] = (value - high.astype(jnp.float32)).astype(jnp.bfloat16)


def split_operator(values):
    rows, picks, size, depth = values.shape
    return pl.pallas_call(
        split_kernel,
        grid=(rows,),
        in_specs=[pl.BlockSpec((1, picks, size, depth), lambda i: (i, 0, 0, 0))],
        out_specs=pl.BlockSpec((1, picks, 2 * size, depth), lambda i: (i, 0, 0, 0)),
        out_shape=jax.ShapeDtypeStruct((rows, picks, 2 * size, depth), jnp.bfloat16),
        compiler_params=pltpu.CompilerParams(vmem_limit_bytes=24 * 2**20),
        cost_estimate=pl.CostEstimate(flops=0, bytes_accessed=8 * values.size, transcendentals=0),
        name="split_operator",
    )(values)


def apply_kernel(half, index_ref, place_ref, parts_ref, gathered_ref, own_ref, other_ref, tiles):
    step = pl.program_id(0)
    rows, picks, _, size = parts_ref.shape
    pieces, span, piece_rows = gathered_ref.shape
    per_piece = piece_rows // size

    @pl.when(step == 0)
    def _():
        for piece in range(pieces):
            for j in range(per_piece):
                tile = gathered_ref[piece, :, j * size : (j + 1) * size]
                high = tile.astype(jnp.bfloat16).astype(jnp.float32)
                both = jnp.concatenate([high, tile - high], axis=0)
                tiles[piece * per_piece + j] = both.T.astype(jnp.bfloat16)

    place = place_ref[0]
    first = jnp.where(step < half, (1 - place) * half + step, place * half + step - half) * rows
    found = []
    for i in range(rows):
        base = (first + i) * picks
        picked = jnp.concatenate([tiles[index_ref[base + k]] for k in range(picks)], axis=0)
        block = jnp.concatenate([parts_ref[i, k] for k in range(picks)], axis=1)
        product = jnp.dot(block, picked, preferred_element_type=jnp.float32)
        both = (product[:size] + product[size:]).T
        found.append(both[:span] + both[span:])
    result = jnp.concatenate(found, axis=1)

    @pl.when(step < half)
    def _():
        other_ref[...] = result

    @pl.when(step >= half)
    def _():
        own_ref[...] = result


def apply_operator(parts, index, place, gathered):
    block_rows, picks, twice, size = parts.shape
    pieces, span, piece_rows = gathered.shape
    out_rows = block_rows // 2 * size
    rows = divisor_up_to(block_rows // 2, 4)
    half = block_rows // 2 // rows

    def block_of(step, index_ref, place_ref):
        place = place_ref[0]
        return (jnp.where(step < half, (1 - place) * half + step, place * half + step - half), 0, 0, 0)

    spec = pltpu.PrefetchScalarGridSpec(
        num_scalar_prefetch=2,
        grid=(2 * half,),
        in_specs=[
            pl.BlockSpec((rows, picks, twice, size), block_of),
            pl.BlockSpec((pieces, span, piece_rows), lambda step, *_: (0, 0, 0)),
        ],
        out_specs=[
            pl.BlockSpec((span, rows * size), lambda step, *_: (0, jnp.maximum(step - half, 0))),
            pl.BlockSpec((span, rows * size), lambda step, *_: (0, jnp.minimum(step, half - 1))),
        ],
        scratch_shapes=[pltpu.VMEM((pieces * piece_rows // size, size, 2 * span), jnp.bfloat16)],
    )
    return pl.pallas_call(
        functools.partial(apply_kernel, half),
        grid_spec=spec,
        out_shape=[jax.ShapeDtypeStruct((span, out_rows), jnp.float32)] * 2,
        compiler_params=pltpu.CompilerParams(vmem_limit_bytes=32 * 2**20),
        cost_estimate=pl.CostEstimate(
            flops=2 * parts.size * 2 * span,
            bytes_accessed=2 * parts.size + 4 * gathered.size,
            transcendentals=0,
        ),
        name="apply_operator",
    )(index, place, parts, gathered)


def shards(sources, tr_vals, tr_cols, rf_vals, rf_cols):
    source = sources[0, 0, 0]
    piece_rows, columns = source.shape
    batches, delay = BATCHES, DELAY
    span = columns // batches
    length = lax.axis_size("slab")
    position = lax.axis_index("slab")
    place = lax.axis_index("row").reshape(1)
    source = source.T.reshape(batches, span, piece_rows)
    trans = split_operator(tr_vals[0, 0, 0])
    refl = split_operator(rf_vals[0, 0, 0])
    trans_index = tr_cols.reshape(-1)
    refl_index = rf_cols.reshape(-1)
    swap = [(0, 1), (1, 0)]

    def applied(parts, index, gathered):
        own, other = apply_operator(parts, index, place, gathered)
        return own + lax.ppermute(other, "row", swap)

    def batch_at(store, which, start):
        return lax.dynamic_index_in_dim(store, jnp.clip(which, 0, batches - 1) + start, 0, keepdims=False)

    moments = batches + delay * (length - 1)
    zero = jnp.zeros((span, piece_rows), jnp.float32)
    downs, refls, ups = [], [], []
    for moment in range(moments):
        incident = batch_at(source, moment - delay * position, 0)
        if moment >= delay:
            incident = incident + passed_along(downs[moment - delay], "slab", 1)
        gathered = lax.all_gather(incident, "col", axis=0, tiled=False)
        downs.append(applied(trans, trans_index, gathered))
        refls.append(applied(refl, refl_index, gathered))
    reflected = jnp.stack(refls)
    for moment in range(moments):
        incident = batch_at(reflected, moment - delay * (length - 1 - position), delay * position)
        if moment >= delay:
            incident = incident + passed_along(ups[moment - delay], "slab", -1)
        gathered = lax.all_gather(incident, "col", axis=0, tiled=False)
        ups.append(applied(trans, trans_index, gathered))
    down = lax.dynamic_slice_in_dim(jnp.stack(downs), delay * position, batches, 0)
    up = lax.dynamic_slice_in_dim(jnp.stack(ups), delay * (length - 1 - position), batches, 0)
    total = (down + up).reshape(columns, piece_rows).T
    return total[None, None, None]


def solution(mesh):
    placed = (
        P("slab", "col", "row", None, None),
        P("slab", "col", "row", None, None, None, None),
        P("slab", "col", "row", None, None),
        P("slab", "col", "row", None, None, None, None),
        P("slab", "col", "row", None, None),
    )
    return jax.shard_map(
        shards,
        mesh=mesh,
        in_specs=placed,
        out_specs=P("slab", "col", "row", None, None),
        check_vma=False,
    )
```

time: 1460 us -> 1250 us (0.86)
  waiting for transfers between devices: 802 us -> 101 us
  blocking collectives: 0 us -> 510 us
  matrix products: 386 us -> 0 us
  Pallas kernels: 0 us -> 344 us
  starting transfers between devices: 31.7 us -> 77.1 us
    all_gather x10 -> x0, waiting for transfers between devices: 548 us -> none  [shards(): gathered = lax.all_gather(incident, 'col', axis=0, tiled=True)]
    all_gather x0 -> x28, blocking collectives: none -> 510 us  [shards(): gathered = lax.all_gather(incident, 'col', axis=0, tiled=False)]
    dot_general x15 -> x0, matrix products: 386 us -> none  [local_product(): jnp.einsum('rkab,rkbw->raw', values, picked, precision=lax.Precision.HIGH...]
    pallas_call x0 -> x44, Pallas kernels: none -> 344 us  [the longest x42 312 us: apply_operator(): pl.pallas_call(functools.partial(apply_kernel, half), grid_spec=spec, out...]
    gather x15 -> x0, local copies, waits for them, and re-layouts: 194 us -> none  [local_product(): picked = tiles[columns]]
    unnamed x30 -> x74, local copies, waits for them, and re-layouts: 0.06 us -> 185 us
    ppermute x10 -> x24, waiting for transfers between devices: 179 us -> 83.6 us  [passed_along(): lax.ppermute(value, axis, [(source, source + steps) for source in range(i...]
    reduce_scatter x15 -> x0, waiting for transfers between devices: 74.5 us -> none  [the longest x5 36.8 us: shards(): moved = lax.psum_scatter(trans_part, 'row', scatter_dimension=0, tiled=True)]
  transfers between devices with their start and end apart: 35 -> 66, of which waited for: 29 -> 32; matrix products, arithmetic and copies ran while one was open for 18% -> 1% of each run, Pallas kernels for 0% -> 16%
where the time goes in v1:
time: 1250 us; the launch traced here: 1240 us
  blocking collectives  510 us (41%)
  Pallas kernels  344 us (28%)
  local copies, waits for them, and re-layouts  188 us (15%)
  waiting for transfers between devices  101 us (8%)
  starting transfers between devices  77.1 us (6%)
  other arithmetic  14.3 us (1%)
    all_gather x28, blocking collectives, shards(): gathered = lax.all_gather(incident, 'col', axis=0, tiled=False)  510 us
    pallas_call x42, Pallas kernels, apply_operator(): pl.pallas_call(functools.partial(apply_kernel, half), grid_spec=spec, out...  312 us
    unnamed x74, local copies, waits for them, and re-layouts  185 us
    ppermute x24, waiting for transfers between devices, passed_along(): lax.ppermute(value, axis, [(source, source + steps) for source in range(i...  83.6 us
    ppermute x24, starting transfers between devices, passed_along(): lax.ppermute(value, axis, [(source, source + steps) for source in range(i...  70.4 us
    pallas_call x2, Pallas kernels, split_operator(): pl.pallas_call(split_kernel, grid=(rows,), in_specs=[pl.BlockSpec((1, pic...  31.1 us
  transfers between devices with their start and end apart: 66, of which 32 were waited for; matrix products, arithmetic and copies ran while one was open for 1% of the time, Pallas kernels for 16%

profile of v1, /device:TPU:0, one launch (start us, length us, event | category | flops | bytes accessed | tf_op | source)
XLA Modules:
  0.0 1235.7 jit_solution(424209933479396084)
XLA Ops:
  23.4 21.3 %all_gather.160.gathered_ref = f32[4,32,1536]{2,1,0:T(8,128)S(1)} all-gather(f32[1,32,1536]{2,1,0:T(8,128)S(1)} %get-tuple-element.248), channel_id=1, replica_groups=mesh['slab'=4,'row'=2,'col'=4] {'col'}, dimensions={0}, use_global_device_ids=true | all-gather | bytes 983040 | tf_op jit(solution)/shard_map/all_gather | solution.py:150
  82.3 18.0 %all_gather.161.gathered_ref = f32[4,32,1536]{2,1,0:T(8,128)S(1)} all-gather(f32[1,32,1536]{2,1,0:T(8,128)S(1)} %get-tuple-element.247), channel_id=1, replica_groups=mesh['slab'=4,'row'=2,'col'=4] {'col'}, dimensions={0}, use_global_device_ids=true | all-gather | bytes 983040 | tf_op jit(solution)/shard_map/all_gather | solution.py:150
  143.1 18.1 %all-gather = f32[128,1536]{1,0:T(8,128)S(1)} all-gather(f32[32,1536]{1,0:T(8,128)S(1)} %get-tuple-element.246), channel_id=2, replica_groups=mesh['slab'=4,'row'=2,'col'=4] {'col'}, dimensions={0}, use_global_device_ids=true | all-gather | bytes 983040 | tf_op jit(solution)/shard_map/all_gather | solution.py:150
  188.9 18.2 %all-gather.1 = f32[128,1536]{1,0:T(8,128)S(1)} all-gather(f32[32,1536]{1,0:T(8,128)S(1)} %get-tuple-element.245), channel_id=3, replica_groups=mesh['slab'=4,'row'=2,'col'=4] {'col'}, dimensions={0}, use_global_device_ids=true | all-gather | bytes 983040 | tf_op jit(solution)/shard_map/all_gather | solution.py:150
  249.9 18.2 %all-gather.2 = f32[128,1536]{1,0:T(8,128)S(1)} all-gather(f32[32,1536]{1,0:T(8,128)S(1)} %get-tuple-element.244), channel_id=4, replica_groups=mesh['slab'=4,'row'=2,'col'=4] {'col'}, dimensions={0}, use_global_device_ids=true | all-gather | bytes 983040 | tf_op jit(solution)/shard_map/all_gather | solution.py:150
  295.8 18.0 %all-gather.3 = f32[128,1536]{1,0:T(8,128)S(1)} all-gather(f32[32,1536]{1,0:T(8,128)S(1)} %get-tuple-element.243), channel_id=5, replica_groups=mesh['slab'=4,'row'=2,'col'=4] {'col'}, dimensions={0}, use_global_device_ids=true | all-gather | bytes 983040 | tf_op jit(solution)/shard_map/all_gather | solution.py:150
  357.3 18.2 %all-gather.4 = f32[128,1536]{1,0:T(8,128)S(1)} all-gather(f32[32,1536]{1,0:T(8,128)S(1)} %get-tuple-element.242), channel_id=6, replica_groups=mesh['slab'=4,'row'=2,'col'=4] {'col'}, dimensions={0}, use_global_device_ids=true | all-gather | bytes 983040 | tf_op jit(solution)/shard_map/all_gather | solution.py:150
  403.2 18.0 %all-gather.5 = f32[128,1536]{1,0:T(8,128)S(1)} all-gather(f32[32,1536]{1,0:T(8,128)S(1)} %get-tuple-element.241), channel_id=7, replica_groups=mesh['slab'=4,'row'=2,'col'=4] {'col'}, dimensions={0}, use_global_device_ids=true | all-gather | bytes 983040 | tf_op jit(solution)/shard_map/all_gather | solution.py:150
  510.6 18.4 %all-gather.7 = f32[128,1536]{1,0:T(8,128)S(1)} all-gather(f32[32,1536]{1,0:T(8,128)S(1)} %get-tuple-element.239), channel_id=9, replica_groups=mesh['slab'=4,'row'=2,'col'=4] {'col'}, dimensions={0}, use_global_device_ids=true | all-gather | bytes 983040 | tf_op jit(solution)/shard_map/all_gather | solution.py:150
  680.5 18.1 %all-gather.10 = f32[128,1536]{1,0:T(8,128)S(1)} all-gather(f32[32,1536]{1,0:T(8,128)S(1)} %get-tuple-element.236), channel_id=12, replica_groups=mesh['slab'=4,'row'=2,'col'=4] {'col'}, dimensions={0}, use_global_device_ids=true | all-gather | bytes 983040 | tf_op jit(solution)/shard_map/all_gather | solution.py:150
  739.4 18.2 %all_gather.186.gathered_ref = f32[4,32,1536]{2,1,0:T(8,128)S(1)} all-gather(f32[1,32,1536]{2,1,0:T(8,128)S(1)} %get-tuple-element.234), channel_id=1, replica_groups=mesh['slab'=4,'row'=2,'col'=4] {'col'}, dimensions={0}, use_global_device_ids=true | all-gather | bytes 983040 | tf_op jit(solution)/shard_map/all_gather | solution.py:158
  771.6 18.2 %all_gather.187.gathered_ref = f32[4,32,1536]{2,1,0:T(8,128)S(1)} all-gather(f32[1,32,1536]{2,1,0:T(8,128)S(1)} %get-tuple-element.233), channel_id=1, replica_groups=mesh['slab'=4,'row'=2,'col'=4] {'col'}, dimensions={0}, use_global_device_ids=true | all-gather | bytes 983040 | tf_op jit(solution)/shard_map/all_gather | solution.py:158
  814.6 18.1 %all-gather.12 = f32[128,1536]{1,0:T(8,128)S(1)} all-gather(f32[32,1536]{1,0:T(8,128)S(1)} %get-tuple-element.232), channel_id=14, replica_groups=mesh['slab'=4,'row'=2,'col'=4] {'col'}, dimensions={0}, use_global_device_ids=true | all-gather | bytes 983040 | tf_op jit(solution)/shard_map/all_gather | solution.py:158
  846.6 18.1 %all-gather.13 = f32[128,1536]{1,0:T(8,128)S(1)} all-gather(f32[32,1536]{1,0:T(8,128)S(1)} %get-tuple-element.231), channel_id=15, replica_groups=mesh['slab'=4,'row'=2,'col'=4] {'col'}, dimensions={0}, use_global_device_ids=true | all-gather | bytes 983040 | tf_op jit(solution)/shard_map/all_gather | solution.py:158
  890.1 18.3 %all-gather.14 = f32[128,1536]{1,0:T(8,128)S(1)} all-gather(f32[32,1536]{1,0:T(8,128)S(1)} %get-tuple-element.230), channel_id=16, replica_groups=mesh['slab'=4,'row'=2,'col'=4] {'col'}, dimensions={0}, use_global_device_ids=true | all-gather | bytes 983040 | tf_op jit(solution)/shard_map/all_gather | solution.py:158
  922.4 18.1 %all-gather.15 = f32[128,1536]{1,0:T(8,128)S(1)} all-gather(f32[32,1536]{1,0:T(8,128)S(1)} %get-tuple-element.229), channel_id=17, replica_groups=mesh['slab'=4,'row'=2,'col'=4] {'col'}, dimensions={0}, use_global_device_ids=true | all-gather | bytes 983040 | tf_op jit(solution)/shard_map/all_gather | solution.py:158
  964.9 18.2 %all-gather.16 = f32[128,1536]{1,0:T(8,128)S(1)} all-gather(f32[32,1536]{1,0:T(8,128)S(1)} %get-tuple-element.228), channel_id=18, replica_groups=mesh['slab'=4,'row'=2,'col'=4] {'col'}, dimensions={0}, use_global_device_ids=true | all-gather | bytes 983040 | tf_op jit(solution)/shard_map/all_gather | solution.py:158
  997.0 18.1 %all-gather.17 = f32[128,1536]{1,0:T(8,128)S(1)} all-gather(f32[32,1536]{1,0:T(8,128)S(1)} %get-tuple-element.227), channel_id=19, replica_groups=mesh['slab'=4,'row'=2,'col'=4] {'col'}, dimensions={0}, use_global_device_ids=true | all-gather | bytes 983040 | tf_op jit(solution)/shard_map/all_gather | solution.py:158
  1043.4 18.4 %all-gather.18 = f32[128,1536]{1,0:T(8,128)S(1)} all-gather(f32[32,1536]{1,0:T(8,128)S(1)} %get-tuple-element.226), channel_id=20, replica_groups=mesh['slab'=4,'row'=2,'col'=4] {'col'}, dimensions={0}, use_global_device_ids=true | all-gather | bytes 983040 | tf_op jit(solution)/shard_map/all_gather | solution.py:158
  1069.3 18.2 %all-gather.19 = f32[128,1536]{1,0:T(8,128)S(1)} all-gather(f32[32,1536]{1,0:T(8,128)S(1)} %get-tuple-element.225), channel_id=21, replica_groups=mesh['slab'=4,'row'=2,'col'=4] {'col'}, dimensions={0}, use_global_device_ids=true | all-gather | bytes 983040 | tf_op jit(solution)/shard_map/all_gather | solution.py:158
  1112.6 18.1 %all-gather.20 = f32[128,1536]{1,0:T(8,128)S(1)} all-gather(f32[32,1536]{1,0:T(8,128)S(1)} %get-tuple-element.224), channel_id=22, replica_groups=mesh['slab'=4,'row'=2,'col'=4] {'col'}, dimensions={0}, use_global_device_ids=true | all-gather | bytes 983040 | tf_op jit(solution)/shard_map/all_gather | solution.py:158
  1138.3 18.1 %all-gather.21 = f32[128,1536]{1,0:T(8,128)S(1)} all-gather(f32[32,1536]{1,0:T(8,128)S(1)} %get-tuple-element.223), channel_id=23, replica_groups=mesh['slab'=4,'row'=2,'col'=4] {'col'}, dimensions={0}, use_global_device_ids=true | all-gather | bytes 983040 | tf_op jit(solution)/shard_map/all_gather | solution.py:158
  1180.7 18.1 %all-gather.22 = f32[128,1536]{1,0:T(8,128)S(1)} all-gather(f32[32,1536]{1,0:T(8,128)S(1)} %get-tuple-element.222), channel_id=24, replica_groups=mesh['slab'=4,'row'=2,'col'=4] {'col'}, dimensions={0}, use_global_device_ids=true | all-gather | bytes 983040 | tf_op jit(solution)/shard_map/all_gather | solution.py:158
  1206.4 18.1 %all-gather.23 = f32[128,1536]{1,0:T(8,128)S(1)} all-gather(f32[32,1536]{1,0:T(8,128)S(1)} %get-tuple-element.221), channel_id=25, replica_groups=mesh['slab'=4,'row'=2,'col'=4] {'col'}, dimensions={0}, use_global_device_ids=true | all-gather | bytes 983040 | tf_op jit(solution)/shard_map/all_gather | solution.py:158
  (315 shorter events, 795.2 us)
Async XLA Ops:
  58.5 79.1 %collective-permute-start.26 = (f32[32,1536]{1,0:T(8,128)S(1)}, f32[32,1536]{1,0:T(8,128)}, u32[]{:S(2)}, u32[]{:S(2)}) collective-permute-start(f32[32,1536]{1,0:T(8,128)S(1)} %get-tuple-element.118), channel_id=1, source_target_pairs={{0,4},{4,0},{1,5},{5,1},{2,6},{6,2},{3,7},{7,3},{8,12},{12,8},{9,1... | collective-permute-start | bytes 589832 | tf_op jit(solution)/shard_map/ppermute | solution.py:138
  81.8 46.9 %collective-permute-start = (f32[32,1536]{1,0:T(8,128)S(1)}, f32[32,1536]{1,0:T(8,128)S(1)}, u32[]{:S(2)}, u32[]{:S(2)}) collective-permute-start(f32[32,1536]{1,0:T(8,128)S(1)} %get-tuple-element.90), channel_id=1, source_target_pairs={{0,4},{4,0},{1,5},{5,1},{2,6},{6,2},{3,7},{7,3},{8,12},{12,8},{9,1... | collective-permute-start | bytes 589832 | tf_op jit(solution)/shard_map/ppermute | solution.py:138
  188.8 56.7 %collective-permute-start.28 = (f32[32,1536]{1,0:T(8,128)S(1)}, f32[32,1536]{1,0:T(8,128)S(1)}, u32[]{:S(2)}, u32[]{:S(2)}) collective-permute-start(f32[32,1536]{1,0:T(8,128)S(1)} %get-tuple-element.122), channel_id=1, source_target_pairs={{0,4},{4,0},{1,5},{5,1},{2,6},{6,2},{3,7},{7,3},{8,12},{12,8},{9,1... | collective-permute-start | bytes 589832 | tf_op jit(solution)/shard_map/ppermute | solution.py:138
  207.1 28.3 %collective-permute-start.3 = (f32[32,1536]{1,0:T(8,128)S(1)}, f32[32,1536]{1,0:T(8,128)S(1)}, u32[]{:S(2)}, u32[]{:S(2)}) collective-permute-start(f32[32,1536]{1,0:T(8,128)S(1)} %get-tuple-element.94), channel_id=1, source_target_pairs={{0,4},{4,0},{1,5},{5,1},{2,6},{6,2},{3,7},{7,3},{8,12},{12,8},{9,1... | collective-permute-start | bytes 589832 | tf_op jit(solution)/shard_map/ppermute | solution.py:138
  295.7 57.3 %collective-permute-start.30 = (f32[32,1536]{1,0:T(8,128)S(1)}, f32[32,1536]{1,0:T(8,128)S(1)}, u32[]{:S(2)}, u32[]{:S(2)}) collective-permute-start(f32[32,1536]{1,0:T(8,128)S(1)} %get-tuple-element.126), channel_id=1, source_target_pairs={{0,4},{4,0},{1,5},{5,1},{2,6},{6,2},{3,7},{7,3},{8,12},{12,8},{9,1... | collective-permute-start | bytes 589832 | tf_op jit(solution)/shard_map/ppermute | solution.py:138
  313.8 28.3 %collective-permute-start.7 = (f32[32,1536]{1,0:T(8,128)S(1)}, f32[32,1536]{1,0:T(8,128)S(1)}, u32[]{:S(2)}, u32[]{:S(2)}) collective-permute-start(f32[32,1536]{1,0:T(8,128)S(1)} %get-tuple-element.98), channel_id=1, source_target_pairs={{0,4},{4,0},{1,5},{5,1},{2,6},{6,2},{3,7},{7,3},{8,12},{12,8},{9,1... | collective-permute-start | bytes 589832 | tf_op jit(solution)/shard_map/ppermute | solution.py:138
  403.1 57.8 %collective-permute-start.32 = (f32[32,1536]{1,0:T(8,128)S(1)}, f32[32,1536]{1,0:T(8,128)S(1)}, u32[]{:S(2)}, u32[]{:S(2)}) collective-permute-start(f32[32,1536]{1,0:T(8,128)S(1)} %get-tuple-element.130), channel_id=1, source_target_pairs={{0,4},{4,0},{1,5},{5,1},{2,6},{6,2},{3,7},{7,3},{8,12},{12,8},{9,1... | collective-permute-start | bytes 589832 | tf_op jit(solution)/shard_map/ppermute | solution.py:138
  421.1 28.3 %collective-permute-start.11 = (f32[32,1536]{1,0:T(8,128)S(1)}, f32[32,1536]{1,0:T(8,128)S(1)}, u32[]{:S(2)}, u32[]{:S(2)}) collective-permute-start(f32[32,1536]{1,0:T(8,128)S(1)} %get-tuple-element.102), channel_id=1, source_target_pairs={{0,4},{4,0},{1,5},{5,1},{2,6},{6,2},{3,7},{7,3},{8,12},{12,8},{9,1... | collective-permute-start | bytes 589832 | tf_op jit(solution)/shard_map/ppermute | solution.py:138
  435.0 25.9 %collective-permute-start.33 = (f32[32,1536]{1,0:T(8,128)S(1)}, f32[32,1536]{1,0:T(8,128)S(1)}, u32[]{:S(2)}, u32[]{:S(2)}) collective-permute-start(f32[32,1536]{1,0:T(8,128)S(1)} %get-tuple-element.132), channel_id=1, source_target_pairs={{0,4},{4,0},{1,5},{5,1},{2,6},{6,2},{3,7},{7,3},{8,12},{12,8},{9,1... | collective-permute-start | bytes 589832 | tf_op jit(solution)/shard_map/ppermute | solution.py:138
  510.5 58.2 %collective-permute-start.34 = (f32[32,1536]{1,0:T(8,128)S(1)}, f32[32,1536]{1,0:T(8,128)S(1)}, u32[]{:S(2)}, u32[]{:S(2)}) collective-permute-start(f32[32,1536]{1,0:T(8,128)S(1)} %get-tuple-element.134), channel_id=1, source_target_pairs={{0,4},{4,0},{1,5},{5,1},{2,6},{6,2},{3,7},{7,3},{8,12},{12,8},{9,1... | collective-permute-start | bytes 589832 | tf_op jit(solution)/shard_map/ppermute | solution.py:138
  529.0 28.3 %collective-permute-start.15 = (f32[32,1536]{1,0:T(8,128)S(1)}, f32[32,1536]{1,0:T(8,128)S(1)}, u32[]{:S(2)}, u32[]{:S(2)}) collective-permute-start(f32[32,1536]{1,0:T(8,128)S(1)} %get-tuple-element.106), channel_id=1, source_target_pairs={{0,4},{4,0},{1,5},{5,1},{2,6},{6,2},{3,7},{7,3},{8,12},{12,8},{9,1... | collective-permute-start | bytes 589832 | tf_op jit(solution)/shard_map/ppermute | solution.py:138
  542.8 25.9 %collective-permute-start.35 = (f32[32,1536]{1,0:T(8,128)S(1)}, f32[32,1536]{1,0:T(8,128)S(1)}, u32[]{:S(2)}, u32[]{:S(2)}) collective-permute-start(f32[32,1536]{1,0:T(8,128)S(1)} %get-tuple-element.136), channel_id=1, source_target_pairs={{0,4},{4,0},{1,5},{5,1},{2,6},{6,2},{3,7},{7,3},{8,12},{12,8},{9,1... | collective-permute-start | bytes 589832 | tf_op jit(solution)/shard_map/ppermute | solution.py:138
  618.4 57.8 %collective-permute-start.36 = (f32[32,1536]{1,0:T(8,128)S(1)}, f32[32,1536]{1,0:T(8,128)S(1)}, u32[]{:S(2)}, u32[]{:S(2)}) collective-permute-start(f32[32,1536]{1,0:T(8,128)S(1)} %get-tuple-element.138), channel_id=1, source_target_pairs={{0,4},{4,0},{1,5},{5,1},{2,6},{6,2},{3,7},{7,3},{8,12},{12,8},{9,1... | collective-permute-start | bytes 589832 | tf_op jit(solution)/shard_map/ppermute | solution.py:138
  636.5 28.3 %collective-permute-start.19 = (f32[32,1536]{1,0:T(8,128)S(1)}, f32[32,1536]{1,0:T(8,128)S(1)}, u32[]{:S(2)}, u32[]{:S(2)}) collective-permute-start(f32[32,1536]{1,0:T(8,128)S(1)} %get-tuple-element.110), channel_id=1, source_target_pairs={{0,4},{4,0},{1,5},{5,1},{2,6},{6,2},{3,7},{7,3},{8,12},{12,8},{9,1... | collective-permute-start | bytes 589832 | tf_op jit(solution)/shard_map/ppermute | solution.py:138
  650.3 26.0 %collective-permute-start.37 = (f32[32,1536]{1,0:T(8,128)S(1)}, f32[32,1536]{1,0:T(8,128)S(1)}, u32[]{:S(2)}, u32[]{:S(2)}) collective-permute-start(f32[32,1536]{1,0:T(8,128)S(1)} %get-tuple-element.140), channel_id=1, source_target_pairs={{0,4},{4,0},{1,5},{5,1},{2,6},{6,2},{3,7},{7,3},{8,12},{12,8},{9,1... | collective-permute-start | bytes 589832 | tf_op jit(solution)/shard_map/ppermute | solution.py:138
  771.5 25.8 %collective-permute-start.40 = (f32[32,1536]{1,0:T(8,128)S(1)}, f32[32,1536]{1,0:T(8,128)S(1)}, u32[]{:S(2)}, u32[]{:S(2)}) collective-permute-start(f32[32,1536]{1,0:T(8,128)S(1)} %get-tuple-element.146), channel_id=1, source_target_pairs={{0,4},{4,0},{1,5},{5,1},{2,6},{6,2},{3,7},{7,3},{8,12},{12,8},{9,1... | collective-permute-start | bytes 589832 | tf_op jit(solution)/shard_map/ppermute | solution.py:138
  846.5 25.7 %collective-permute-start.43 = (f32[32,1536]{1,0:T(8,128)S(1)}, f32[32,1536]{1,0:T(8,128)S(1)}, u32[]{:S(2)}, u32[]{:S(2)}) collective-permute-start(f32[32,1536]{1,0:T(8,128)S(1)} %get-tuple-element.150), channel_id=1, source_target_pairs={{0,4},{4,0},{1,5},{5,1},{2,6},{6,2},{3,7},{7,3},{8,12},{12,8},{9,1... | collective-permute-start | bytes 589832 | tf_op jit(solution)/shard_map/ppermute | solution.py:138
  922.3 25.7 %collective-permute-start.47 = (f32[32,1536]{1,0:T(8,128)S(1)}, f32[32,1536]{1,0:T(8,128)S(1)}, u32[]{:S(2)}, u32[]{:S(2)}) collective-permute-start(f32[32,1536]{1,0:T(8,128)S(1)} %get-tuple-element.154), channel_id=1, source_target_pairs={{0,4},{4,0},{1,5},{5,1},{2,6},{6,2},{3,7},{7,3},{8,12},{12,8},{9,1... | collective-permute-start | bytes 589832 | tf_op jit(solution)/shard_map/ppermute | solution.py:138
  996.9 25.7 %collective-permute-start.51 = (f32[32,1536]{1,0:T(8,128)S(1)}, f32[32,1536]{1,0:T(8,128)S(1)}, u32[]{:S(2)}, u32[]{:S(2)}) collective-permute-start(f32[32,1536]{1,0:T(8,128)S(1)} %get-tuple-element.158), channel_id=1, source_target_pairs={{0,4},{4,0},{1,5},{5,1},{2,6},{6,2},{3,7},{7,3},{8,12},{12,8},{9,1... | collective-permute-start | bytes 589832 | tf_op jit(solution)/shard_map/ppermute | solution.py:138
  1034.2 64.9 %collective-permute-start.23 = (f32[32,1536]{1,0:T(8,128)S(1)}, f32[32,1536]{1,0:T(8,128)S(1)}, u32[]{:S(2)}, u32[]{:S(2)}) collective-permute-start(f32[32,1536]{1,0:T(8,128)S(1)} %get-tuple-element.114), channel_id=1, source_target_pairs={{0,4},{4,0},{1,5},{5,1},{2,6},{6,2},{3,7},{7,3},{8,12},{12,8},{9,1... | collective-permute-start | bytes 589832 | tf_op jit(solution)/shard_map/ppermute | solution.py:138
  1041.9 126.1 %collective-permute-start.25 = (f32[32,1536]{1,0:T(8,128)S(1)}, f32[32,1536]{1,0:T(8,128)S(1)}, u32[]{:S(2)}, u32[]{:S(2)}) collective-permute-start(f32[32,1536]{1,0:T(8,128)S(1)} %get-tuple-element.116), channel_id=1, source_target_pairs={{0,4},{4,0},{1,5},{5,1},{2,6},{6,2},{3,7},{7,3},{8,12},{12,8},{9,1... | collective-permute-start | bytes 589832 | tf_op jit(solution)/shard_map/ppermute | solution.py:138
  1069.3 25.8 %collective-permute-start.55 = (f32[32,1536]{1,0:T(8,128)S(1)}, f32[32,1536]{1,0:T(8,128)S(1)}, u32[]{:S(2)}, u32[]{:S(2)}) collective-permute-start(f32[32,1536]{1,0:T(8,128)S(1)} %get-tuple-element.162), channel_id=1, source_target_pairs={{0,4},{4,0},{1,5},{5,1},{2,6},{6,2},{3,7},{7,3},{8,12},{12,8},{9,1... | collective-permute-start | bytes 589832 | tf_op jit(solution)/shard_map/ppermute | solution.py:138
  1138.2 25.7 %collective-permute-start.59 = (f32[32,1536]{1,0:T(8,128)S(1)}, f32[32,1536]{1,0:T(8,128)S(1)}, u32[]{:S(2)}, u32[]{:S(2)}) collective-permute-start(f32[32,1536]{1,0:T(8,128)S(1)} %get-tuple-element.166), channel_id=1, source_target_pairs={{0,4},{4,0},{1,5},{5,1},{2,6},{6,2},{3,7},{7,3},{8,12},{12,8},{9,1... | collective-permute-start | bytes 589832 | tf_op jit(solution)/shard_map/ppermute | solution.py:138
  1206.3 25.7 %collective-permute-start.63 = (f32[32,1536]{1,0:T(8,128)S(1)}, f32[32,1536]{1,0:T(8,128)S(1)}, u32[]{:S(2)}, u32[]{:S(2)}) collective-permute-start(f32[32,1536]{1,0:T(8,128)S(1)} %get-tuple-element.170), channel_id=1, source_target_pairs={{0,4},{4,0},{1,5},{5,1},{2,6},{6,2},{3,7},{7,3},{8,12},{12,8},{9,1... | collective-permute-start | bytes 589832 | tf_op jit(solution)/shard_map/ppermute | solution.py:138
  (78 other events, 706.7 us)

commit v2 on v0

v2 whole, which is shorter than its diff:
```python
import jax
import jax.numpy as jnp
from jax import lax
from jax.experimental import pallas as pl
from jax.experimental.pallas import tpu as pltpu
from jax.sharding import PartitionSpec as P

BATCHES = 8
DELAY = 2


def divisor_up_to(number, limit):
    return max(n for n in range(1, limit + 1) if number % n == 0)


def passed_along(value, axis, steps):
    count = lax.axis_size(axis)
    initial, last = (max(0, -steps), min(count, count - steps))
    return lax.ppermute(value, axis, [(source, source + steps) for source in range(initial, last)])


def split_kernel(place_ref, own_ref, other_ref, parts_ref):
    picks, size = own_ref.shape[1:3]

    def split(values_ref, start):
        for k in range(picks):
            value = values_ref[0, k]
            high = value.astype(jnp.bfloat16)
            parts_ref[0, start + k, :size] = high
            parts_ref[0, start + k, size:] = (value - high.astype(jnp.float32)).astype(jnp.bfloat16)

    @pl.when(place_ref[0] == 0)
    def _():
        split(own_ref, 0)
        split(other_ref, picks)

    @pl.when(place_ref[0] != 0)
    def _():
        split(other_ref, 0)
        split(own_ref, picks)


def split_operator(values, other, place):
    _, picks, size, depth = values.shape
    rows = other.shape[0]
    spec = pltpu.PrefetchScalarGridSpec(
        num_scalar_prefetch=1,
        grid=(rows,),
        in_specs=[
            pl.BlockSpec((1, picks, size, depth), lambda i, place_ref: (place_ref[0] * rows + i, 0, 0, 0)),
            pl.BlockSpec((1, picks, size, depth), lambda i, place_ref: (i, 0, 0, 0)),
        ],
        out_specs=pl.BlockSpec((1, 2 * picks, 2 * size, depth), lambda i, place_ref: (i, 0, 0, 0)),
    )
    return pl.pallas_call(
        split_kernel,
        grid_spec=spec,
        out_shape=jax.ShapeDtypeStruct((rows, 2 * picks, 2 * size, depth), jnp.bfloat16),
        compiler_params=pltpu.CompilerParams(vmem_limit_bytes=44 * 2**20),
        name="split_operator",
    )(place, values, other)


def apply_kernel(index_ref, parts_ref, gathered_ref, *refs):
    result_ref, tiles = refs[-2:]
    step = pl.program_id(0)
    rows, picks, _, size = parts_ref.shape
    pieces, groups, span, piece_rows = gathered_ref.shape
    per_piece = piece_rows // size

    @pl.when(step == 0)
    def _():
        for group in range(groups):
            for piece in range(pieces):
                for j in range(per_piece):
                    tile = gathered_ref[piece, group, :, j * size : (j + 1) * size]
                    high = tile.astype(jnp.bfloat16).astype(jnp.float32)
                    both = jnp.concatenate([high, tile - high], axis=0)
                    tiles[(group * pieces + piece) * per_piece + j] = both.T.astype(jnp.bfloat16)

    found = []
    for i in range(rows):
        base = (step * rows + i) * picks
        picked = jnp.concatenate([tiles[index_ref[base + k]] for k in range(picks)], axis=0)
        block = jnp.concatenate([parts_ref[i, k] for k in range(picks)], axis=1)
        product = jnp.dot(block, picked, preferred_element_type=jnp.float32)
        both = (product[:size] + product[size:]).T
        found.append(both[:span] + both[span:])
    result_ref[...] = jnp.concatenate(found, axis=1)


def apply_operator(parts, index, gathered, *after):
    block_rows, picks, twice, size = parts.shape
    pieces, groups, span, piece_rows = gathered.shape
    rows = divisor_up_to(block_rows, 2)
    spec = pltpu.PrefetchScalarGridSpec(
        num_scalar_prefetch=1,
        grid=(block_rows // rows,),
        in_specs=[
            pl.BlockSpec((rows, picks, twice, size), lambda step, *_: (step, 0, 0, 0)),
            pl.BlockSpec((pieces, groups, span, piece_rows), lambda step, *_: (0, 0, 0, 0)),
        ]
        + [pl.BlockSpec(memory_space=pl.ANY)] * len(after),
        out_specs=pl.BlockSpec((span, rows * size), lambda step, *_: (0, step)),
        scratch_shapes=[pltpu.VMEM((groups * pieces * piece_rows // size, size, 2 * span), jnp.bfloat16)],
    )
    return pl.pallas_call(
        apply_kernel,
        grid_spec=spec,
        out_shape=jax.ShapeDtypeStruct((span, block_rows * size), jnp.float32),
        compiler_params=pltpu.CompilerParams(vmem_limit_bytes=44 * 2**20),
        cost_estimate=pl.CostEstimate(flops=0, bytes_accessed=gathered.size, transcendentals=0),
        name="apply_operator",
    )(index, parts, gathered, *after)


def sum_kernel(which_ref, arrived_ref, store_ref, *refs):
    refs[-1][...] = arrived_ref[...] + store_ref[0]


def sum_with(arrived, store, which, *after):
    spec = pltpu.PrefetchScalarGridSpec(
        num_scalar_prefetch=1,
        grid=(1,),
        in_specs=[
            pl.BlockSpec(arrived.shape, lambda i, which_ref: (0, 0)),
            pl.BlockSpec((1,) + arrived.shape, lambda i, which_ref: (which_ref[0], 0, 0)),
        ]
        + [pl.BlockSpec(memory_space=pl.ANY)] * len(after),
        out_specs=pl.BlockSpec(arrived.shape, lambda i, which_ref: (0, 0)),
    )
    return pl.pallas_call(
        sum_kernel,
        grid_spec=spec,
        out_shape=jax.ShapeDtypeStruct(arrived.shape, arrived.dtype),
        compiler_params=pltpu.CompilerParams(vmem_limit_bytes=44 * 2**20),
        name="sum_with",
    )(which.reshape(1), arrived, store, *after)


def shards(sources, tr_vals, tr_cols, rf_vals, rf_cols):
    source = sources[0, 0, 0]
    piece_rows, columns = source.shape
    batches, delay = BATCHES, DELAY
    span = columns // batches
    length = lax.axis_size("slab")
    position = lax.axis_index("slab")
    place = lax.axis_index("row")
    source = source.T.reshape(batches, span, piece_rows)
    group_blocks = lax.axis_size("col") * piece_rows // tr_vals.shape[-1]

    def halves(values, columns):
        half = values.shape[0] // 2
        swap = [(0, 1), (1, 0)]

        def other_half(array):
            return lax.ppermute(lax.dynamic_slice_in_dim(array, (1 - place) * half, half, 0), "row", swap)

        own = lax.dynamic_slice_in_dim(columns, place * half, half, 0)
        other = other_half(columns)
        first = jnp.where(place == 0, own, other)
        second = jnp.where(place == 0, other, own) + group_blocks
        index = jnp.concatenate([first, second], axis=1).reshape(-1)
        return split_operator(values, other_half(values), place.reshape(1)), index

    trans = halves(tr_vals[0, 0, 0], tr_cols[0, 0, 0])
    refl = halves(rf_vals[0, 0, 0], rf_cols[0, 0, 0])

    def gather(piece):
        return lax.all_gather(piece, ("col", "row"), axis=0).reshape((-1, 2) + piece.shape)

    moments = batches + delay * (length - 1)

    def sweep(first, start, steps, reflect):
        def incident_of(moment):
            offset = position if steps > 0 else length - 1 - position
            which = jnp.clip(moment - delay * offset, 0, batches - 1) + start
            if moment < delay:
                return lax.dynamic_index_in_dim(first, which, 0, keepdims=False)
            arrived = passed_along(moved[moment - delay], "slab", steps)
            return sum_with(arrived, first, which, *reflected[moment - delay : moment - delay + 1])

        moved, reflected = [], []
        incident = incident_of(0)
        gathered = gather(incident)
        for moment in range(moments):
            if moment + 1 < moments:
                incident = incident_of(moment + 1)
                coming = gather(incident)
            moved.append(apply_operator(*trans, gathered, incident, *reflected[-1:]))
            if reflect:
                reflected.append(apply_operator(*refl, gathered, moved[-1]))
            gathered = coming
        return jnp.stack(moved), jnp.stack(reflected) if reflect else None

    downs, reflected = sweep(source, 0, 1, True)
    ups, _ = sweep(reflected, delay * position, -1, False)
    down = lax.dynamic_slice_in_dim(downs, delay * position, batches, 0)
    up = lax.dynamic_slice_in_dim(ups, delay * (length - 1 - position), batches, 0)
    total = (down + up).reshape(columns, piece_rows).T
    return total[None, None, None]


def solution(mesh):
    placed = (
        P("slab", "col", "row", None, None),
        P("slab", "col", "row", None, None, None, None),
        P("slab", "col", "row", None, None),
        P("slab", "col", "row", None, None, None, None),
        P("slab", "col", "row", None, None),
    )
    return jax.shard_map(
        shards,
        mesh=mesh,
        in_specs=placed,
        out_specs=P("slab", "col", "row", None, None),
        check_vma=False,
    )
```

time: 1460 us -> 900 us (0.62)
  waiting for transfers between devices: 802 us -> 142 us
  Pallas kernels: 0 us -> 527 us
  matrix products: 386 us -> 0 us
  local copies, waits for them, and re-layouts: 195 us -> 150 us
  other arithmetic: 22.1 us -> 1.81 us
  starting transfers between devices: 31.7 us -> 48.5 us
    pallas_call x0 -> x65, Pallas kernels: none -> 527 us  [the longest x39 463 us: apply_operator(): pl.pallas_call(apply_kernel, grid_spec=spec, out_shape=jax.ShapeDtypeStru...]
    all_gather x10 -> x28, waiting for transfers between devices: 548 us -> 51.1 us  [gather(): lax.all_gather(piece, ('col', 'row'), axis=0).reshape((-1, 2) + piece.shape)]
    dot_general x15 -> x0, matrix products: 386 us -> none  [local_product(): jnp.einsum('rkab,rkbw->raw', values, picked, precision=lax.Precision.HIGH...]
    gather x15 -> x0, local copies, waits for them, and re-layouts: 194 us -> none  [local_product(): picked = tiles[columns]]
    unnamed x30 -> x260, local copies, waits for them, and re-layouts: 0.06 us -> 92.3 us
    ppermute x10 -> x24, waiting for transfers between devices: 179 us -> 86.4 us  [passed_along(): lax.ppermute(value, axis, [(source, source + steps) for source in range(i...]
    reduce_scatter x15 -> x0, waiting for transfers between devices: 74.5 us -> none  [the longest x5 36.8 us: shards(): moved = lax.psum_scatter(trans_part, 'row', scatter_dimension=0, tiled=True)]
    pallas_call x0 -> x3, local copies, waits for them, and re-layouts: none -> 37.6 us  [apply_operator(): pl.pallas_call(apply_kernel, grid_spec=spec, out_shape=jax.ShapeDtypeStru...]
  transfers between devices with their start and end apart: 35 -> 56, of which waited for: 29 -> 25; matrix products, arithmetic and copies ran while one was open for 18% -> 6% of each run, Pallas kernels for 0% -> 58%
where the time goes in v2:
time: 900 us; the launch traced here: 886 us
  Pallas kernels  527 us (59%)
  local copies, waits for them, and re-layouts  150 us (17%)
  waiting for transfers between devices  142 us (16%)
  starting transfers between devices  48.5 us (5%)
  between operations  15.9 us (2%)
    pallas_call x39, Pallas kernels, apply_operator(): pl.pallas_call(apply_kernel, grid_spec=spec, out_shape=jax.ShapeDtypeStru...  463 us
    unnamed x260, local copies, waits for them, and re-layouts  92.3 us
    ppermute x24, waiting for transfers between devices, passed_along(): lax.ppermute(value, axis, [(source, source + steps) for source in range(i...  86.4 us
    all_gather x28, waiting for transfers between devices, gather(): lax.all_gather(piece, ('col', 'row'), axis=0).reshape((-1, 2) + piece.shape)  51.1 us
    ppermute x24, starting transfers between devices, passed_along(): lax.ppermute(value, axis, [(source, source + steps) for source in range(i...  44.1 us
    pallas_call x3, local copies, waits for them, and re-layouts, apply_operator(): pl.pallas_call(apply_kernel, grid_spec=spec, out_shape=jax.ShapeDtypeStru...  37.6 us
    pallas_call x2, Pallas kernels, split_operator(): pl.pallas_call(split_kernel, grid_spec=spec, out_shape=jax.ShapeDtypeStru...  34.1 us
    pallas_call x24, Pallas kernels, sum_with(): pl.pallas_call(sum_kernel, grid_spec=spec, out_shape=jax.ShapeDtypeStruct...  29.5 us
  transfers between devices with their start and end apart: 56, of which 25 were waited for; matrix products, arithmetic and copies ran while one was open for 6% of the time, Pallas kernels for 58%

profile of v2, /device:TPU:0, one launch (start us, length us, event | category | flops | bytes accessed | tf_op | source)
XLA Modules:
  0.0 885.6 jit_solution(3158582943492991413)
XLA Ops:
  31.6 17.1 %split_operator.2.parts_ref = bf16[12,24,256,128]{3,2,1,0:T(8,128)(2,1)} custom-call(s32[1]{0:T(128)} %bitcast.2.place_ref, f32[24,12,128,128]{3,2,1,0:T(8,128)} %bitcast.220, f32[12,12,128,128]{3,2,1,0:T(8,128)} %collective-permute-done.1.other_ref), custom_call_target="tpu_custom_call" | custom-call | tf_op jit(solution)/shard_map/split_operator/pallas_call | solution.py:55
  71.0 17.1 %split_operator.3.parts_ref = bf16[12,24,256,128]{3,2,1,0:T(8,128)(2,1)} custom-call(s32[1]{0:T(128)} %bitcast.2.place_ref, f32[24,12,128,128]{3,2,1,0:T(8,128)} %bitcast.221, f32[12,12,128,128]{3,2,1,0:T(8,128)} %collective-permute-done.4.other_ref), custom_call_target="tpu_custom_call" | custom-call | tf_op jit(solution)/shard_map/split_operator/pallas_call | solution.py:55
  101.9 12.4 %apply_operator.44.refs_0_ = f32[32,1536]{1,0:T(8,128)} custom-call(s32[288]{0:T(512)S(1)} %reshape.178.index_ref, bf16[12,24,256,128]{3,2,1,0:T(8,128)(2,1)} %split_operator.2.parts_ref, f32[4,2,32,1536]{3,2,1,0:T(8,128)S(1)} %bitcast.178, f32[32,1536]{1,0:T(8,128)} %sum_with.24.refs_0_, f32[32,1536]{1,0:T(8,128)S(1)} %apply_operator.43.refs_0_.refs_1_), custom_call_target="tpu_custom_call" | custom-call | bytes 393216 | tf_op jit(solution)/shard_map/apply_operator/pallas_call | solution.py:107
  133.7 12.3 %apply_operator.46.refs_0_ = f32[32,1536]{1,0:T(8,128)} custom-call(s32[288]{0:T(512)S(1)} %reshape.178.index_ref, bf16[12,24,256,128]{3,2,1,0:T(8,128)(2,1)} %split_operator.2.parts_ref, f32[4,2,32,1536]{3,2,1,0:T(8,128)S(1)} %bitcast.188, f32[32,1536]{1,0:T(8,128)} %sum_with.25.refs_0_, f32[32,1536]{1,0:T(8,128)S(1)} %apply_operator.45.refs_0_.refs_1_), custom_call_target="tpu_custom_call" | custom-call | bytes 393216 | tf_op jit(solution)/shard_map/apply_operator/pallas_call | solution.py:107
  165.9 12.3 %apply_operator.48.refs_0_ = f32[32,1536]{1,0:T(8,128)} custom-call(s32[288]{0:T(512)S(1)} %reshape.178.index_ref, bf16[12,24,256,128]{3,2,1,0:T(8,128)(2,1)} %split_operator.2.parts_ref, f32[4,2,32,1536]{3,2,1,0:T(8,128)S(1)} %bitcast.190, f32[32,1536]{1,0:T(8,128)} %sum_with.26.refs_0_, f32[32,1536]{1,0:T(8,128)S(1)} %copy-done.31), custom_call_target="tpu_custom_call" | custom-call | bytes 393216 | tf_op jit(solution)/shard_map/apply_operator/pallas_call | solution.py:107
  196.8 12.4 %apply_operator.50.refs_0_ = f32[32,1536]{1,0:T(8,128)} custom-call(s32[288]{0:T(512)S(1)} %reshape.178.index_ref, bf16[12,24,256,128]{3,2,1,0:T(8,128)(2,1)} %split_operator.2.parts_ref, f32[4,2,32,1536]{3,2,1,0:T(8,128)S(1)} %bitcast.192, f32[32,1536]{1,0:T(8,128)} %sum_with.27.refs_0_, f32[32,1536]{1,0:T(8,128)S(1)} %copy-done.34), custom_call_target="tpu_custom_call" | custom-call | bytes 393216 | tf_op jit(solution)/shard_map/apply_operator/pallas_call | solution.py:107
  227.8 12.4 %apply_operator.52.refs_0_ = f32[32,1536]{1,0:T(8,128)} custom-call(s32[288]{0:T(512)S(1)} %reshape.178.index_ref, bf16[12,24,256,128]{3,2,1,0:T(8,128)(2,1)} %split_operator.2.parts_ref, f32[4,2,32,1536]{3,2,1,0:T(8,128)S(1)} %bitcast.194, f32[32,1536]{1,0:T(8,128)} %sum_with.28.refs_0_, f32[32,1536]{1,0:T(8,128)S(1)} %copy-done.37), custom_call_target="tpu_custom_call" | custom-call | bytes 393216 | tf_op jit(solution)/shard_map/apply_operator/pallas_call | solution.py:107
  258.6 12.4 %apply_operator.54.refs_0_ = f32[32,1536]{1,0:T(8,128)} custom-call(s32[288]{0:T(512)S(1)} %reshape.178.index_ref, bf16[12,24,256,128]{3,2,1,0:T(8,128)(2,1)} %split_operator.2.parts_ref, f32[4,2,32,1536]{3,2,1,0:T(8,128)S(1)} %bitcast.196, f32[32,1536]{1,0:T(8,128)} %sum_with.29.refs_0_, f32[32,1536]{1,0:T(8,128)S(1)} %copy-done.40), custom_call_target="tpu_custom_call" | custom-call | bytes 393216 | tf_op jit(solution)/shard_map/apply_operator/pallas_call | solution.py:107
  289.4 12.4 %apply_operator.56.refs_0_ = f32[32,1536]{1,0:T(8,128)} custom-call(s32[288]{0:T(512)S(1)} %reshape.178.index_ref, bf16[12,24,256,128]{3,2,1,0:T(8,128)(2,1)} %split_operator.2.parts_ref, f32[4,2,32,1536]{3,2,1,0:T(8,128)S(1)} %bitcast.198, f32[32,1536]{1,0:T(8,128)} %sum_with.30.refs_0_, f32[32,1536]{1,0:T(8,128)S(1)} %copy-done.42), custom_call_target="tpu_custom_call" | custom-call | bytes 393216 | tf_op jit(solution)/shard_map/apply_operator/pallas_call | solution.py:107
  320.4 12.4 %apply_operator.58.refs_0_ = f32[32,1536]{1,0:T(8,128)} custom-call(s32[288]{0:T(512)S(1)} %reshape.178.index_ref, bf16[12,24,256,128]{3,2,1,0:T(8,128)(2,1)} %split_operator.2.parts_ref, f32[4,2,32,1536]{3,2,1,0:T(8,128)S(1)} %bitcast.200, f32[32,1536]{1,0:T(8,128)} %sum_with.31.refs_0_, f32[32,1536]{1,0:T(8,128)S(1)} %copy-done.45), custom_call_target="tpu_custom_call" | custom-call | bytes 393216 | tf_op jit(solution)/shard_map/apply_operator/pallas_call | solution.py:107
  351.2 12.4 %apply_operator.60.refs_0_ = f32[32,1536]{1,0:T(8,128)} custom-call(s32[288]{0:T(512)S(1)} %reshape.178.index_ref, bf16[12,24,256,128]{3,2,1,0:T(8,128)(2,1)} %split_operator.2.parts_ref, f32[4,2,32,1536]{3,2,1,0:T(8,128)S(1)} %bitcast.202, f32[32,1536]{1,0:T(8,128)} %sum_with.32.refs_0_, f32[32,1536]{1,0:T(8,128)S(1)} %copy-done.48), custom_call_target="tpu_custom_call" | custom-call | bytes 393216 | tf_op jit(solution)/shard_map/apply_operator/pallas_call | solution.py:107
  382.0 11.8 %apply_operator.62.refs_0_ = f32[32,1536]{1,0:T(8,128)S(1)} custom-call(s32[288]{0:T(512)S(1)} %reshape.178.index_ref, bf16[12,24,256,128]{3,2,1,0:T(8,128)(2,1)} %split_operator.2.parts_ref, f32[4,2,32,1536]{3,2,1,0:T(8,128)S(1)} %bitcast.184, f32[32,1536]{1,0:T(8,128)} %sum_with.33.refs_0_, f32[32,1536]{1,0:T(8,128)S(1)} %copy-done.51), custom_call_target="tpu_custom_call" | custom-call | bytes 393216 | tf_op jit(solution)/shard_map/apply_operator/pallas_call | solution.py:107
  413.2 11.8 %apply_operator.64.refs_0_ = f32[32,1536]{1,0:T(8,128)S(1)} custom-call(s32[288]{0:T(512)S(1)} %reshape.178.index_ref, bf16[12,24,256,128]{3,2,1,0:T(8,128)(2,1)} %split_operator.2.parts_ref, f32[4,2,32,1536]{3,2,1,0:T(8,128)S(1)} %bitcast.182, f32[32,1536]{1,0:T(8,128)S(1)} %copy-done.68, f32[32,1536]{1,0:T(8,128)S(1)} %copy-done.54), custom_call_target="tpu_custom_call" | custom-call | bytes 393216 | tf_op jit(solution)/shard_map/apply_operator/pallas_call | solution.py:107
  444.5 11.9 %apply_operator.66.refs_0_ = f32[32,1536]{1,0:T(8,128)S(1)} custom-call(s32[288]{0:T(512)S(1)} %reshape.178.index_ref, bf16[12,24,256,128]{3,2,1,0:T(8,128)(2,1)} %split_operator.2.parts_ref, f32[4,2,32,1536]{3,2,1,0:T(8,128)S(1)} %bitcast.186, f32[32,1536]{1,0:T(8,128)S(1)} %copy-done.57, f32[32,1536]{1,0:T(8,128)S(1)} %copy-done.60), custom_call_target="tpu_custom_call" | custom-call | bytes 393216 | tf_op jit(solution)/shard_map/apply_operator/pallas_call | solution.py:107
  494.6 21.9 %all-gather.57.cloned.1.call-done = f32[8,32,1536]{2,1,0:T(8,128)} async-done(((f32[1,32,1536]{2,1,0:T(8,128)}), f32[8,32,1536]{2,1,0:T(8,128)}) %all-gather.57.cloned.1.call-update) | async-done | bytes 1572880 | tf_op jit(solution)/shard_map/all_gather | solution.py:170
  518.8 11.8 %apply_operator.69 = f32[32,1536]{1,0:T(8,128)S(1)} custom-call(s32[288]{0:T(512)S(1)} %reshape.178.index_ref, bf16[12,24,256,128]{3,2,1,0:T(8,128)(2,1)} %split_operator.2.parts_ref, f32[4,2,32,1536]{3,2,1,0:T(8,128)S(1)} %bitcast.219, f32[32,1536]{1,0:T(8,128)S(1)} %bitcast.207), custom_call_target="tpu_custom_call" | custom-call | bytes 393216 | tf_op jit(solution)/shard_map/apply_operator/pallas_call | solution.py:107
  544.0 11.7 %apply_operator.70 = f32[32,1536]{1,0:T(8,128)S(1)} custom-call(s32[288]{0:T(512)S(1)} %reshape.178.index_ref, bf16[12,24,256,128]{3,2,1,0:T(8,128)(2,1)} %split_operator.2.parts_ref, f32[4,2,32,1536]{3,2,1,0:T(8,128)S(1)} %bitcast.212, f32[32,1536]{1,0:T(8,128)} %sum_with.36.refs_0_), custom_call_target="tpu_custom_call" | custom-call | bytes 393216 | tf_op jit(solution)/shard_map/apply_operator/pallas_call | solution.py:107
  596.2 11.7 %apply_operator.72 = f32[32,1536]{1,0:T(8,128)S(1)} custom-call(s32[288]{0:T(512)S(1)} %reshape.178.index_ref, bf16[12,24,256,128]{3,2,1,0:T(8,128)(2,1)} %split_operator.2.parts_ref, f32[4,2,32,1536]{3,2,1,0:T(8,128)S(1)} %bitcast.214, f32[32,1536]{1,0:T(8,128)} %sum_with.38.refs_0_), custom_call_target="tpu_custom_call" | custom-call | bytes 393216 | tf_op jit(solution)/shard_map/apply_operator/pallas_call | solution.py:107
  674.9 11.7 %apply_operator.75 = f32[32,1536]{1,0:T(8,128)S(1)} custom-call(s32[288]{0:T(512)S(1)} %reshape.178.index_ref, bf16[12,24,256,128]{3,2,1,0:T(8,128)(2,1)} %split_operator.2.parts_ref, f32[4,2,32,1536]{3,2,1,0:T(8,128)S(1)} %bitcast.218, f32[32,1536]{1,0:T(8,128)} %sum_with.41.refs_0_), custom_call_target="tpu_custom_call" | custom-call | bytes 393216 | tf_op jit(solution)/shard_map/apply_operator/pallas_call | solution.py:107
  701.1 11.7 %apply_operator.76 = f32[32,1536]{1,0:T(8,128)S(1)} custom-call(s32[288]{0:T(512)S(1)} %reshape.178.index_ref, bf16[12,24,256,128]{3,2,1,0:T(8,128)(2,1)} %split_operator.2.parts_ref, f32[4,2,32,1536]{3,2,1,0:T(8,128)S(1)} %bitcast.217, f32[32,1536]{1,0:T(8,128)} %sum_with.42.refs_0_), custom_call_target="tpu_custom_call" | custom-call | bytes 393216 | tf_op jit(solution)/shard_map/apply_operator/pallas_call | solution.py:107
  758.3 11.8 %apply_operator.78 = f32[32,1536]{1,0:T(8,128)S(1)} custom-call(s32[288]{0:T(512)S(1)} %reshape.178.index_ref, bf16[12,24,256,128]{3,2,1,0:T(8,128)(2,1)} %split_operator.2.parts_ref, f32[4,2,32,1536]{3,2,1,0:T(8,128)S(1)} %bitcast.208, f32[32,1536]{1,0:T(8,128)} %sum_with.44.refs_0_), custom_call_target="tpu_custom_call" | custom-call | bytes 393216 | tf_op jit(solution)/shard_map/apply_operator/pallas_call | solution.py:107
  815.6 11.9 %apply_operator.80 = f32[32,1536]{1,0:T(8,128)S(1)} custom-call(s32[288]{0:T(512)S(1)} %reshape.178.index_ref, bf16[12,24,256,128]{3,2,1,0:T(8,128)(2,1)} %split_operator.2.parts_ref, f32[4,2,32,1536]{3,2,1,0:T(8,128)S(1)} %bitcast.211, f32[32,1536]{1,0:T(8,128)} %sum_with.46.refs_0_), custom_call_target="tpu_custom_call" | custom-call | bytes 393216 | tf_op jit(solution)/shard_map/apply_operator/pallas_call | solution.py:107
  842.7 13.0 %apply_operator.82 = f32[14,32,1536]{2,1,0:T(8,128)} fusion(f32[14,32,1536]{2,1,0:T(8,128)} %bitcast_dynamic-update-slice_fusion.2, s32[288]{0:T(512)S(1)} %reshape.178.index_ref, bf16[12,24,256,128]{3,2,1,0:T(8,128)(2,1)} %split_operator.2.parts_ref, f32[4,2,32,1536]{3,2,1,0:T(8,128)} %bitcast.224, f32[32,1536]{1,0:T(8,128)} %sum_with.47), kind=kCustom, calls=%fused_computation.4 | custom fusion | bytes 20841600 | tf_op jit(solution)/shard_map/apply_operator/pallas_call | solution.py:107
  862.0 13.0 %apply_operator.81 = f32[14,32,1536]{2,1,0:T(8,128)} fusion(f32[14,32,1536]{2,1,0:T(8,128)} %apply_operator.82, s32[288]{0:T(512)S(1)} %reshape.178.index_ref, bf16[12,24,256,128]{3,2,1,0:T(8,128)(2,1)} %split_operator.2.parts_ref, f32[4,2,32,1536]{3,2,1,0:T(8,128)} %bitcast.225, f32[32,1536]{1,0:T(8,128)} %sum_with.47), kind=kCustom, calls=%fused_computation.3 | custom fusion | bytes 20841600 | tf_op jit(solution)/shard_map/apply_operator/pallas_call | solution.py:107
  (459 shorter events, 558.6 us)
Async XLA Ops:
  26.6 73.9 %all-gather.55.cloned.1.call-start = ((), (), s32[]{:S(2)}) async-start(), calls=%async_computation.1 | async-start | bytes 1769472 | tf_op jit(solution)/shard_map/all_gather | solution.py:170
  27.3 104.9 %all-gather.61.cloned.1.call-start = ((), (), s32[]{:S(2)}) async-start(), calls=%async_computation.4 | async-start | bytes 1769472 | tf_op jit(solution)/shard_map/all_gather | solution.py:170
  100.4 63.1 %all-gather.63.cloned.1.call-start = ((), (), s32[]{:S(2)}) async-start(), calls=%async_computation.5 | async-start | bytes 1769472 | tf_op jit(solution)/shard_map/all_gather | solution.py:170
  131.7 62.7 %all-gather.65.cloned.1.call-start = ((), (), s32[]{:S(2)}) async-start(), calls=%async_computation.6 | async-start | bytes 1769472 | tf_op jit(solution)/shard_map/all_gather | solution.py:170
  163.5 62.0 %all-gather.67.cloned.1.call-start = ((), (), s32[]{:S(2)}) async-start(), calls=%async_computation.7 | async-start | bytes 1769472 | tf_op jit(solution)/shard_map/all_gather | solution.py:170
  194.4 61.9 %all-gather.69.cloned.1.call-start = ((), (), s32[]{:S(2)}) async-start(), calls=%async_computation.8 | async-start | bytes 1769472 | tf_op jit(solution)/shard_map/all_gather | solution.py:170
  225.2 61.8 %all-gather.71.cloned.1.call-start = ((), (), s32[]{:S(2)}) async-start(), calls=%async_computation.9 | async-start | bytes 1769472 | tf_op jit(solution)/shard_map/all_gather | solution.py:170
  256.2 61.8 %all-gather.73.cloned.1.call-start = ((), (), s32[]{:S(2)}) async-start(), calls=%async_computation.10 | async-start | bytes 1769472 | tf_op jit(solution)/shard_map/all_gather | solution.py:170
  287.0 61.9 %all-gather.75.cloned.1.call-start = ((), (), s32[]{:S(2)}) async-start(), calls=%async_computation.11 | async-start | bytes 1769472 | tf_op jit(solution)/shard_map/all_gather | solution.py:170
  317.7 61.9 %all-gather.77.cloned.1.call-start = ((), (), s32[]{:S(2)}) async-start(), calls=%async_computation.12 | async-start | bytes 1769472 | tf_op jit(solution)/shard_map/all_gather | solution.py:170
  348.8 61.1 %all-gather.79.cloned.1.call-start = ((), (), s32[]{:S(2)}) async-start(), calls=%async_computation.13 | async-start | bytes 1769472 | tf_op jit(solution)/shard_map/all_gather | solution.py:170
  379.6 61.7 %all-gather.81.cloned.1.call-start = ((), (), s32[]{:S(2)}) async-start(), calls=%async_computation.14 | async-start | bytes 1769472 | tf_op jit(solution)/shard_map/all_gather | solution.py:170
  408.3 59.8 %all-gather.83.cloned.1.call-start = ((), (), s32[]{:S(2)}) async-start(), calls=%async_computation.15 | async-start | bytes 1769472 | tf_op jit(solution)/shard_map/all_gather | solution.py:170
  440.1 76.4 %all-gather.57.cloned.1.call-start = ((), (), s32[]{:S(2)}) async-start(), calls=%async_computation.2 | async-start | bytes 1769472 | tf_op jit(solution)/shard_map/all_gather | solution.py:170
  494.3 74.3 %all-gather.85.cloned.1.call-start = ((), (), s32[]{:S(2)}) async-start(), calls=%async_computation.16 | async-start | bytes 1769472 | tf_op jit(solution)/shard_map/all_gather | solution.py:170
  566.5 54.6 %all-gather.89.cloned.1.call-start = ((), (), s32[]{:S(2)}) async-start(), calls=%async_computation.18 | async-start | bytes 1769472 | tf_op jit(solution)/shard_map/all_gather | solution.py:170
  592.6 54.6 %all-gather.91.cloned.1.call-start = ((), (), s32[]{:S(2)}) async-start(), calls=%async_computation.19 | async-start | bytes 1769472 | tf_op jit(solution)/shard_map/all_gather | solution.py:170
  618.7 54.8 %all-gather.93.cloned.1.call-start = ((), (), s32[]{:S(2)}) async-start(), calls=%async_computation.20 | async-start | bytes 1769472 | tf_op jit(solution)/shard_map/all_gather | solution.py:170
  644.9 54.8 %all-gather.95.cloned.1.call-start = ((), (), s32[]{:S(2)}) async-start(), calls=%async_computation.21 | async-start | bytes 1769472 | tf_op jit(solution)/shard_map/all_gather | solution.py:170
  671.0 54.9 %all-gather.97.cloned.1.call-start = ((), (), s32[]{:S(2)}) async-start(), calls=%async_computation.22 | async-start | bytes 1769472 | tf_op jit(solution)/shard_map/all_gather | solution.py:170
  697.3 59.6 %all-gather.99.cloned.1.call-start = ((), (), s32[]{:S(2)}) async-start(), calls=%async_computation.23 | async-start | bytes 1769472 | tf_op jit(solution)/shard_map/all_gather | solution.py:170
  723.7 61.8 %all-gather.101.cloned.1.call-start = ((), (), s32[]{:S(2)}) async-start(), calls=%async_computation.24 | async-start | bytes 1769472 | tf_op jit(solution)/shard_map/all_gather | solution.py:170
  748.8 65.4 %all-gather.103.cloned.1.call-start = ((), (), s32[]{:S(2)}) async-start(), calls=%async_computation.25 | async-start | bytes 1769472 | tf_op jit(solution)/shard_map/all_gather | solution.py:170
  779.9 62.8 %all-gather.105.cloned.1.call-start = ((), (), s32[]{:S(2)}) async-start(), calls=%async_computation.26 | async-start | bytes 1769472 | tf_op jit(solution)/shard_map/all_gather | solution.py:170
  (141 other events, 1725.9 us)
Sparse Core Ops, SparseCore 0:
  26.7 27.4 all-gather.52
  55.8 24.5 all-gather.54
  100.6 23.7 all-gather.60
  131.8 23.0 all-gather.62
  163.6 22.9 all-gather.64
  194.5 22.7 all-gather.66
  225.3 22.7 all-gather.68
  256.3 22.7 all-gather.70
  287.1 22.7 all-gather.72
  317.9 22.7 all-gather.74
  379.7 22.7 all-gather.78
  518.0 24.5 all-gather.58
  544.1 24.5 all-gather.84
  570.2 24.5 all-gather.86
  596.4 24.5 all-gather.88
  622.6 24.5 all-gather.90
  648.8 24.5 all-gather.92
  675.1 24.5 all-gather.94
  701.3 24.5 all-gather.96
  727.5 24.5 all-gather.98
  753.7 24.5 all-gather.100
  780.0 24.8 all-gather.102
  808.9 25.0 all-gather.104
  836.8 25.1 all-gather.106
  (4 shorter events, 90.4 us)

commit v3 on v2

v3 whole, which is shorter than its diff:
```python
import jax
import jax.numpy as jnp
from jax import lax
from jax.experimental import pallas as pl
from jax.experimental.pallas import tpu as pltpu
from jax.sharding import PartitionSpec as P

LANES = 128
DELAY = 2
SLOTS = 4
VMEM_BYTES = 44 * 2**20
TOKEN = jax.ShapeDtypeStruct((8, LANES), jnp.float32)
TOKEN_SPEC = pl.BlockSpec(TOKEN.shape, lambda *_: (0, 0))


def passed_along(value, axis, steps):
    count = lax.axis_size(axis)
    initial, last = (max(0, -steps), min(count, count - steps))
    return lax.ppermute(value, axis, [(source, source + steps) for source in range(initial, last)])


def pack_kernel(rows_ref, packed_ref):
    batches, _, size, lanes = packed_ref.shape
    pack = rows_ref.shape[0] // size
    span = lanes // pack
    for batch in range(batches):
        found = [rows_ref[q * size : (q + 1) * size, batch * span : (batch + 1) * span] for q in range(pack)]
        packed_ref[batch, 0] = jnp.concatenate(found, axis=1)


def unpack_kernel(packed_ref, rows_ref):
    batches, _, size, lanes = packed_ref.shape
    pack = rows_ref.shape[0] // size
    span = lanes // pack
    for q in range(pack):
        found = [packed_ref[batch, 0, :, q * span : (q + 1) * span] for batch in range(batches)]
        rows_ref[q * size : (q + 1) * size, :] = jnp.concatenate(found, axis=1)


def packed_trace(rows, batches, pack, size):
    groups = rows.shape[0] // (pack * size)
    return pl.pallas_call(
        pack_kernel,
        grid=(groups,),
        in_specs=[pl.BlockSpec((pack * size, rows.shape[1]), lambda i: (i, 0))],
        out_specs=pl.BlockSpec((batches, 1, size, LANES), lambda i: (0, i, 0, 0)),
        out_shape=jax.ShapeDtypeStruct((batches, groups, size, LANES), rows.dtype),
        compiler_params=pltpu.CompilerParams(vmem_limit_bytes=VMEM_BYTES),
        name="pack_trace",
    )(rows)


def unpacked_trace(packed, pack):
    batches, groups, size, lanes = packed.shape
    columns = batches * (lanes // pack)
    return pl.pallas_call(
        unpack_kernel,
        grid=(groups,),
        in_specs=[pl.BlockSpec((batches, 1, size, lanes), lambda i: (0, i, 0, 0))],
        out_specs=pl.BlockSpec((pack * size, columns), lambda i: (i, 0)),
        out_shape=jax.ShapeDtypeStruct((groups * pack * size, columns), packed.dtype),
        compiler_params=pltpu.CompilerParams(vmem_limit_bytes=VMEM_BYTES),
        name="unpack_trace",
    )(packed)


def split_kernel(place_ref, own_ref, other_ref, parts_ref):
    picks, size = own_ref.shape[1:3]
    for start, values_ref in ((0, own_ref), (picks, other_ref)):
        for k in range(picks):
            value = values_ref[0, k]
            high = value.astype(jnp.bfloat16)
            parts_ref[0, start + k, :size] = high
            parts_ref[0, start + k, size:] = (value - high.astype(jnp.float32)).astype(jnp.bfloat16)


def split_operator(values, other, place):
    _, picks, size, depth = values.shape
    rows = other.shape[0]
    spec = pltpu.PrefetchScalarGridSpec(
        num_scalar_prefetch=1,
        grid=(rows,),
        in_specs=[
            pl.BlockSpec((1, picks, size, depth), lambda i, place_ref: (place_ref[0] * rows + i, 0, 0, 0)),
            pl.BlockSpec((1, picks, size, depth), lambda i, place_ref: (i, 0, 0, 0)),
        ],
        out_specs=pl.BlockSpec((1, 2 * picks, 2 * size, depth), lambda i, place_ref: (i, 0, 0, 0)),
    )
    return pl.pallas_call(
        split_kernel,
        grid_spec=spec,
        out_shape=jax.ShapeDtypeStruct((rows, 2 * picks, 2 * size, depth), jnp.bfloat16),
        compiler_params=pltpu.CompilerParams(vmem_limit_bytes=VMEM_BYTES),
        name="split_operator",
    )(place, values, other)


def apply_kernel(pack, index_ref, parts_ref, own_ref, other_ref, *refs):
    result_ref, token_ref, slots, tiles, arrived = refs[-5:]
    row, rows = pl.program_id(0), pl.num_programs(0)
    count, picks, twice, _ = slots.shape
    size = twice // 2
    pieces, groups, _, lanes = own_ref.shape
    span = lanes // pack

    def fetch(which):
        slot = lax.rem(which, count)
        return pltpu.make_async_copy(parts_ref.at[which], slots.at[slot], arrived.at[slot])

    @pl.when(row == 0)
    def _():
        for ahead in range(min(count - 1, parts_ref.shape[0])):
            fetch(ahead).start()

    @pl.when(row + count - 1 < rows)
    def _():
        fetch(row + count - 1).start()

    @pl.when(row == 0)
    def _():
        token_ref[...] = jnp.zeros_like(token_ref)
        lane = lax.broadcasted_iota(jnp.int32, (size, 2 * lanes), 1) % lanes // span
        masks = [(lane == q).astype(jnp.float32).astype(jnp.bfloat16) for q in range(pack)]
        for start, ref in ((0, own_ref), (pieces * groups, other_ref)):
            for piece in range(pieces):
                for group in range(groups):
                    tile = ref[piece, group]
                    high = tile.astype(jnp.bfloat16)
                    low = (tile - high.astype(jnp.float32)).astype(jnp.bfloat16)
                    both = jnp.concatenate([high, low], axis=1)
                    base = (start + piece * groups + group) * pack
                    for q in range(pack):
                        tiles[base + q] = both * masks[q] if pack > 1 else both

    fetch(row).wait()
    slot = lax.rem(row, count)
    picked = jnp.concatenate([tiles[index_ref[row * picks + k]] for k in range(picks)], axis=0)
    block = jnp.concatenate([slots[slot, k] for k in range(picks)], axis=1)
    product = jnp.dot(block, picked, preferred_element_type=jnp.float32)
    total = product[:size] + product[size:]
    total = total[:, :lanes] + total[:, lanes:]
    shift = span
    while shift < lanes:
        total = total + pltpu.roll(total, shift, 1)
        shift *= 2
    if pack == 1:
        result_ref[0] = total
    else:
        lane = lax.broadcasted_iota(jnp.int32, total.shape, 1)
        result_ref[0] = jnp.where(lane < lax.rem(row, pack) * span, result_ref[0], total)


def apply_operator(parts, index, pack, own, other, *after):
    rows, picks, twice, depth = parts.shape
    pieces, groups, size, lanes = own.shape
    whole = pl.BlockSpec(own.shape, lambda row, *_: (0, 0, 0, 0))
    spec = pltpu.PrefetchScalarGridSpec(
        num_scalar_prefetch=1,
        grid=(rows,),
        in_specs=[pl.BlockSpec(memory_space=pl.ANY), whole, whole]
        + [pl.BlockSpec(memory_space=pl.ANY)] * len(after),
        out_specs=[pl.BlockSpec((1, size, lanes), lambda row, *_: (row // pack, 0, 0)), TOKEN_SPEC],
        scratch_shapes=[
            pltpu.VMEM((SLOTS, picks, twice, depth), jnp.bfloat16),
            pltpu.VMEM((2 * pieces * groups * pack, size, 2 * lanes), jnp.bfloat16),
            pltpu.SemaphoreType.DMA((SLOTS,)),
        ],
    )

    def kernel(*refs):
        apply_kernel(pack, *refs)

    return pl.pallas_call(
        kernel,
        grid_spec=spec,
        out_shape=[jax.ShapeDtypeStruct((groups, size, lanes), jnp.float32), TOKEN],
        compiler_params=pltpu.CompilerParams(vmem_limit_bytes=VMEM_BYTES),
        cost_estimate=pl.CostEstimate(flops=0, bytes_accessed=own.size, transcendentals=0),
        name="apply_operator",
    )(index, parts, own, other, *after)


def sum_kernel(which_ref, arrived_ref, store_ref, *refs):
    copies_ref, token_ref = refs[-2:]
    total = arrived_ref[...] + store_ref[0]
    for copy in range(copies_ref.shape[0]):
        copies_ref[copy] = total
    token_ref[...] = jnp.zeros_like(token_ref)


def sum_with(copies, arrived, store, which, *after):
    spec = pltpu.PrefetchScalarGridSpec(
        num_scalar_prefetch=1,
        grid=(1,),
        in_specs=[
            pl.BlockSpec(arrived.shape, lambda i, which_ref: (0, 0, 0)),
            pl.BlockSpec((1,) + arrived.shape, lambda i, which_ref: (which_ref[0], 0, 0, 0)),
        ]
        + [pl.BlockSpec(memory_space=pl.ANY)] * len(after),
        out_specs=[
            pl.BlockSpec((copies,) + arrived.shape, lambda i, which_ref: (0, 0, 0, 0)),
            TOKEN_SPEC,
        ],
    )
    return pl.pallas_call(
        sum_kernel,
        grid_spec=spec,
        out_shape=[jax.ShapeDtypeStruct((copies,) + arrived.shape, arrived.dtype), TOKEN],
        compiler_params=pltpu.CompilerParams(vmem_limit_bytes=VMEM_BYTES),
        name="sum_with",
    )(which.reshape(1), arrived, store, *after)


def shards(sources, tr_vals, tr_cols, rf_vals, rf_cols):
    source = sources[0, 0, 0]
    piece_rows, columns = source.shape
    size = tr_vals.shape[-1]
    blocks = piece_rows // size
    pack = next(n for n in (4, 2, 1) if blocks % n == 0)
    batches, delay = columns // (LANES // pack), DELAY
    length, pieces = lax.axis_size("slab"), lax.axis_size("col")
    position = lax.axis_index("slab")
    place = lax.axis_index("row")
    swap = [(0, 1), (1, 0)]
    source = packed_trace(source, batches, pack, size)

    def halves(values, columns):
        half = values.shape[0] // 2

        def other_half(array):
            return lax.ppermute(lax.dynamic_slice_in_dim(array, (1 - place) * half, half, 0), "row", swap)

        own = lax.dynamic_slice_in_dim(columns, place * half, half, 0)
        index = jnp.concatenate([own, other_half(columns) + pieces * blocks], axis=1).reshape(-1)
        return split_operator(values, other_half(values), place.reshape(1)), index, pack

    trans = halves(tr_vals[0, 0, 0], tr_cols[0, 0, 0])
    refl = halves(rf_vals[0, 0, 0], rf_cols[0, 0, 0])

    def gather(copies):
        gathered = lax.all_to_all(copies, "col", 0, 0)
        return gathered, lax.ppermute(gathered, "row", swap)

    moments = batches + delay * (length - 1)

    def sweep(first, start, steps, reflect):
        def incident_of(moment):
            offset = position if steps > 0 else length - 1 - position
            which = jnp.clip(moment - delay * offset, 0, batches - 1) + start
            if moment < delay:
                piece = lax.dynamic_index_in_dim(first, which, 0, keepdims=False)
                return jnp.broadcast_to(piece[None], (pieces,) + piece.shape), None
            arrived = passed_along(moved[moment - delay], "slab", steps)
            return sum_with(pieces, arrived, first, which, *tokens[moment - delay : moment - delay + 1])

        moved, reflected, tokens = [], [], []
        incident, _ = incident_of(0)
        gathered = gather(incident)
        for moment in range(moments):
            after = tokens[-1:]
            if moment + 1 < moments:
                incident, token = incident_of(moment + 1)
                coming = gather(incident)
                after = after + ([] if token is None else [token])
            product, token = apply_operator(*trans, *gathered, *after)
            moved.append(product)
            if reflect:
                product, token = apply_operator(*refl, *gathered, token)
                reflected.append(product)
                tokens.append(token)
            gathered = coming
        return jnp.stack(moved), jnp.stack(reflected) if reflect else None

    downs, reflected = sweep(source, 0, 1, True)
    ups, _ = sweep(reflected, delay * position, -1, False)
    down = lax.dynamic_slice_in_dim(downs, delay * position, batches, 0)
    up = lax.dynamic_slice_in_dim(ups, delay * (length - 1 - position), batches, 0)
    return unpacked_trace(down + up, pack)[None, None, None]


def solution(mesh):
    placed = (
        P("slab", "col", "row", None, None),
        P("slab", "col", "row", None, None, None, None),
        P("slab", "col", "row", None, None),
        P("slab", "col", "row", None, None, None, None),
        P("slab", "col", "row", None, None),
    )
    return jax.shard_map(
        shards,
        mesh=mesh,
        in_specs=placed,
        out_specs=P("slab", "col", "row", None, None),
        check_vma=False,
    )
```

time: 900 us -> 1070 us (1.19)
  starting transfers between devices: 48.5 us -> 175 us
  blocking collectives: 0 us -> 50.7 us
  waiting for transfers between devices: 142 us -> 171 us
  local copies, waits for them, and re-layouts: 150 us -> 130 us
  between operations: 15.9 us -> 2.39 us
    all_to_all x0 -> x26, starting transfers between devices: none -> 130 us  [gather(): gathered = lax.all_to_all(copies, 'col', 0, 0)]
    all_gather x28 -> x0, waiting for transfers between devices: 51.1 us -> none  [gather(): lax.all_gather(piece, ('col', 'row'), axis=0).reshape((-1, 2) + piece.shape)]
    all_to_all x0 -> x2, blocking collectives: none -> 50.7 us  [gather(): gathered = lax.all_to_all(copies, 'col', 0, 0)]
    ppermute x0 -> x28, waiting for transfers between devices: none -> 45.3 us  [gather(): return (gathered, lax.ppermute(gathered, 'row', swap))]
    pallas_call x3 -> x0, local copies, waits for them, and re-layouts: 37.6 us -> none  [apply_operator(): pl.pallas_call(apply_kernel, grid_spec=spec, out_shape=jax.ShapeDtypeStru...]
    all_to_all x0 -> x26, waiting for transfers between devices: none -> 25 us  [gather(): gathered = lax.all_to_all(copies, 'col', 0, 0)]
    unnamed x260 -> x257, local copies, waits for them, and re-layouts: 92.3 us -> 108 us
    ppermute x24, waiting for transfers between devices: 86.4 us -> 99.5 us  [passed_along(): lax.ppermute(value, axis, [(source, source + steps) for source in range(i...]
  transfers between devices with their start and end apart: 56 -> 82, of which waited for: 25 -> 35; matrix products, arithmetic and copies ran while one was open for 6% -> 6% of each run, Pallas kernels for 58% -> 46%
where the time goes in v3:
time: 1070 us; the launch traced here: 1060 us
  Pallas kernels  526 us (49%)
  starting transfers between devices  175 us (16%)
  waiting for transfers between devices  171 us (16%)
  local copies, waits for them, and re-layouts  130 us (12%)
  blocking collectives  50.7 us (5%)
    pallas_call x42, Pallas kernels, apply_operator(): pl.pallas_call(kernel, grid_spec=spec, out_shape=[jax.ShapeDtypeStruct((g...  479 us
    all_to_all x26, starting transfers between devices, gather(): gathered = lax.all_to_all(copies, 'col', 0, 0)  130 us
    unnamed x257, local copies, waits for them, and re-layouts  108 us
    ppermute x24, waiting for transfers between devices, passed_along(): lax.ppermute(value, axis, [(source, source + steps) for source in range(i...  99.5 us
    all_to_all x2, blocking collectives, gather(): gathered = lax.all_to_all(copies, 'col', 0, 0)  50.7 us
    ppermute x28, waiting for transfers between devices, gather(): return (gathered, lax.ppermute(gathered, 'row', swap))  45.3 us
    ppermute x24, starting transfers between devices, passed_along(): lax.ppermute(value, axis, [(source, source + steps) for source in range(i...  42.9 us
    pallas_call x2, Pallas kernels, split_operator(): pl.pallas_call(split_kernel, grid_spec=spec, out_shape=jax.ShapeDtypeStru...  33.9 us
  transfers between devices with their start and end apart: 82, of which 35 were waited for; matrix products, arithmetic and copies ran while one was open for 6% of the time, Pallas kernels for 46%

profile of v3, /device:TPU:0, one launch (start us, length us, event | category | flops | bytes accessed | tf_op | source)
XLA Modules:
  0.0 1056.5 jit_solution(14240984390588366518)
XLA Ops:
  19.7 26.5 %all_to_all.140.refs_2_ = f32[4,3,128,128]{3,2,1,0:T(8,128)S(1)} all-to-all(f32[4,3,128,128]{3,2,1,0:T(8,128)S(1)} %broadcast_in_dim.36), channel_id=1, replica_groups=mesh['slab'=4,'row'=2,'col'=4] {'col'}, dimensions={0} | all-to-all | bytes 1572864 | tf_op jit(solution)/shard_map/all_to_all | solution.py:241
  53.3 16.9 %split_operator.2.refs_1_ = bf16[12,24,256,128]{3,2,1,0:T(8,128)(2,1)} custom-call(s32[1]{0:T(128)} %bitcast.2.place_ref, f32[24,12,128,128]{3,2,1,0:T(8,128)} %bitcast.130, f32[12,12,128,128]{3,2,1,0:T(8,128)} %collective-permute-done.1.other_ref), custom_call_target="tpu_custom_call" | custom-call | tf_op jit(solution)/shard_map/split_operator/pallas_call | solution.py:89
  70.2 12.0 %apply_operator.42 = (f32[3,128,128]{2,1,0:T(8,128)S(1)}, f32[8,128]{1,0:T(8,128)S(1)}) custom-call(s32[288]{0:T(512)S(1)} %reshape.88.refs_0_, bf16[12,24,256,128]{3,2,1,0:T(8,128)(2,1)} %split_operator.2.refs_1_, f32[4,3,128,128]{3,2,1,0:T(8,128)S(1)} %all_to_all.140.refs_2_, f32[4,3,128,128]{3,2,1,0:T(8,128)} %collective-permute-done.2.refs_3_), custom_call_target="tpu_custom_call" | custom-call | bytes 196608 | tf_op jit(solution)/shard_map/apply_operator/pallas_call | solution.py:173
  87.9 16.9 %split_operator.3.refs_1_ = bf16[12,24,256,128]{3,2,1,0:T(8,128)(2,1)} custom-call(s32[1]{0:T(128)} %bitcast.2.place_ref, f32[24,12,128,128]{3,2,1,0:T(8,128)} %bitcast.131, f32[12,12,128,128]{3,2,1,0:T(8,128)} %collective-permute-done.5.other_ref), custom_call_target="tpu_custom_call" | custom-call | tf_op jit(solution)/shard_map/split_operator/pallas_call | solution.py:89
  104.8 12.1 %apply_operator.43 = (f32[3,128,128]{2,1,0:T(8,128)S(1)}, f32[8,128]{1,0:T(8,128)S(1)}) custom-call(s32[288]{0:T(512)S(1)} %reshape.90.refs_0_, bf16[12,24,256,128]{3,2,1,0:T(8,128)(2,1)} %split_operator.3.refs_1_, f32[4,3,128,128]{3,2,1,0:T(8,128)S(1)} %all_to_all.140.refs_2_, f32[4,3,128,128]{3,2,1,0:T(8,128)} %collective-permute-done.2.refs_3_, ...), custom_call_target="tpu_custom_call" | custom-call | bytes 196608 | tf_op jit(solution)/shard_map/apply_operator/pallas_call | solution.py:173
  480.9 12.3 %apply_operator.64 = (f32[3,128,128]{2,1,0:T(8,128)S(1)}, f32[8,128]{1,0:T(8,128)S(1)}) custom-call(s32[288]{0:T(512)S(1)} %reshape.88.refs_0_, bf16[12,24,256,128]{3,2,1,0:T(8,128)(2,1)} %split_operator.2.refs_1_, f32[4,3,128,128]{3,2,1,0:T(8,128)} %all-to-all-done.11.refs_2_, f32[4,3,128,128]{3,2,1,0:T(8,128)} %collective-permute-done.25.refs_3_, ...), custom_call_target="tpu_custom_call" | custom-call | bytes 196608 | tf_op jit(solution)/shard_map/apply_operator/pallas_call | solution.py:173
  495.1 12.3 %apply_operator.65 = (f32[3,128,128]{2,1,0:T(8,128)S(1)}, f32[8,128]{1,0:T(8,128)S(1)}) custom-call(s32[288]{0:T(512)S(1)} %reshape.90.refs_0_, bf16[12,24,256,128]{3,2,1,0:T(8,128)(2,1)} %split_operator.3.refs_1_, f32[4,3,128,128]{3,2,1,0:T(8,128)} %all-to-all-done.11.refs_2_, f32[4,3,128,128]{3,2,1,0:T(8,128)} %collective-permute-done.25.refs_3_, ...), custom_call_target="tpu_custom_call" | custom-call | bytes 196608 | tf_op jit(solution)/shard_map/apply_operator/pallas_call | solution.py:173
  519.9 14.5 %all-to-all-done.13.refs_2_ = f32[4,3,128,128]{3,2,1,0:T(8,128)} async-done(((f32[4,3,128,128]{3,2,1,0:T(8,128)}), f32[4,3,128,128]{3,2,1,0:T(8,128)}, u32[]{:S(2)}, u32[]{:S(2)}) %all-to-all-start.13) | async-done | bytes 786464 | tf_op jit(solution)/shard_map/all_to_all | solution.py:241
  537.3 12.1 %apply_operator.66 = (f32[3,128,128]{2,1,0:T(8,128)S(1)}, f32[8,128]{1,0:T(8,128)S(1)}) custom-call(s32[288]{0:T(512)S(1)} %reshape.88.refs_0_, bf16[12,24,256,128]{3,2,1,0:T(8,128)(2,1)} %split_operator.2.refs_1_, f32[4,3,128,128]{3,2,1,0:T(8,128)S(1)} %all-to-all-done.12.refs_2_, f32[4,3,128,128]{3,2,1,0:T(8,128)} %collective-permute-done.27.refs_3_, ...), custom_call_target="tpu_custom_call" | custom-call | bytes 196608 | tf_op jit(solution)/shard_map/apply_operator/pallas_call | solution.py:173
  550.0 12.1 %apply_operator.67 = (f32[3,128,128]{2,1,0:T(8,128)S(1)}, f32[8,128]{1,0:T(8,128)S(1)}) custom-call(s32[288]{0:T(512)S(1)} %reshape.90.refs_0_, bf16[12,24,256,128]{3,2,1,0:T(8,128)(2,1)} %split_operator.3.refs_1_, f32[4,3,128,128]{3,2,1,0:T(8,128)S(1)} %all-to-all-done.12.refs_2_, f32[4,3,128,128]{3,2,1,0:T(8,128)} %collective-permute-done.27.refs_3_, ...), custom_call_target="tpu_custom_call" | custom-call | bytes 196608 | tf_op jit(solution)/shard_map/apply_operator/pallas_call | solution.py:173
  562.1 12.1 %apply_operator.68 = (f32[3,128,128]{2,1,0:T(8,128)S(1)}, f32[8,128]{1,0:T(8,128)S(1)}) custom-call(s32[288]{0:T(512)S(1)} %reshape.88.refs_0_, bf16[12,24,256,128]{3,2,1,0:T(8,128)(2,1)} %split_operator.2.refs_1_, f32[4,3,128,128]{3,2,1,0:T(8,128)} %all-to-all-done.13.refs_2_, f32[4,3,128,128]{3,2,1,0:T(8,128)S(1)} %collective-permute-done.29.refs_3_, ...), custom_call_target="tpu_custom_call" | custom-call | bytes 196608 | tf_op jit(solution)/shard_map/apply_operator/pallas_call | solution.py:173
  574.9 12.1 %apply_operator.69 = (f32[3,128,128]{2,1,0:T(8,128)S(1)}, f32[8,128]{1,0:T(8,128)}) custom-call(s32[288]{0:T(512)S(1)} %reshape.90.refs_0_, bf16[12,24,256,128]{3,2,1,0:T(8,128)(2,1)} %split_operator.3.refs_1_, f32[4,3,128,128]{3,2,1,0:T(8,128)} %all-to-all-done.13.refs_2_, f32[4,3,128,128]{3,2,1,0:T(8,128)S(1)} %collective-permute-done.29.refs_3_, ...), custom_call_target="tpu_custom_call" | custom-call | bytes 196608 | tf_op jit(solution)/shard_map/apply_operator/pallas_call | solution.py:173
  587.1 24.1 %all_to_all.141.refs_2_ = f32[4,3,128,128]{3,2,1,0:T(8,128)} all-to-all(f32[4,3,128,128]{3,2,1,0:T(8,128)S(1)} %broadcast_in_dim.40), channel_id=1, replica_groups=mesh['slab'=4,'row'=2,'col'=4] {'col'}, dimensions={0} | all-to-all | bytes 1572864 | tf_op jit(solution)/shard_map/all_to_all | solution.py:241
  619.4 11.6 %apply_operator.70 = (f32[3,128,128]{2,1,0:T(8,128)}, f32[8,128]{1,0:T(8,128)}) custom-call(s32[288]{0:T(512)S(1)} %reshape.88.refs_0_, bf16[12,24,256,128]{3,2,1,0:T(8,128)(2,1)} %split_operator.2.refs_1_, f32[4,3,128,128]{3,2,1,0:T(8,128)S(1)} %copy-done.26, f32[4,3,128,128]{3,2,1,0:T(8,128)S(1)} %collective-permute-done.30.refs_3_), custom_call_target="tpu_custom_call" | custom-call | bytes 196608 | tf_op jit(solution)/shard_map/apply_operator/pallas_call | solution.py:173
  651.6 11.7 %apply_operator.71 = (f32[3,128,128]{2,1,0:T(8,128)}, f32[8,128]{1,0:T(8,128)}) custom-call(s32[288]{0:T(512)S(1)} %reshape.88.refs_0_, bf16[12,24,256,128]{3,2,1,0:T(8,128)(2,1)} %split_operator.2.refs_1_, f32[4,3,128,128]{3,2,1,0:T(8,128)S(1)} %copy-done.25, f32[4,3,128,128]{3,2,1,0:T(8,128)S(1)} %collective-permute-done.31.refs_3_, ...), custom_call_target="tpu_custom_call" | custom-call | bytes 196608 | tf_op jit(solution)/shard_map/apply_operator/pallas_call | solution.py:173
  682.0 11.7 %apply_operator.72 = (f32[3,128,128]{2,1,0:T(8,128)}, f32[8,128]{1,0:T(8,128)}) custom-call(s32[288]{0:T(512)S(1)} %reshape.88.refs_0_, bf16[12,24,256,128]{3,2,1,0:T(8,128)(2,1)} %split_operator.2.refs_1_, f32[4,3,128,128]{3,2,1,0:T(8,128)S(1)} %all-to-all-done.16.refs_2_, f32[4,3,128,128]{3,2,1,0:T(8,128)S(1)} %collective-permute-done.33.refs_3_, ...), custom_call_target="tpu_custom_call" | custom-call | bytes 196608 | tf_op jit(solution)/shard_map/apply_operator/pallas_call | solution.py:173
  711.5 12.8 %apply_operator.73 = (f32[3,128,128]{2,1,0:T(8,128)}, f32[8,128]{1,0:T(8,128)}) custom-call(s32[288]{0:T(512)S(1)} %reshape.88.refs_0_, bf16[12,24,256,128]{3,2,1,0:T(8,128)(2,1)} %split_operator.2.refs_1_, f32[4,3,128,128]{3,2,1,0:T(8,128)} %all-to-all-done.17.refs_2_, f32[4,3,128,128]{3,2,1,0:T(8,128)S(1)} %collective-permute-done.35.refs_3_, ...), custom_call_target="tpu_custom_call" | custom-call | bytes 196608 | tf_op jit(solution)/shard_map/apply_operator/pallas_call | solution.py:173
  743.6 11.6 %apply_operator.74 = (f32[3,128,128]{2,1,0:T(8,128)}, f32[8,128]{1,0:T(8,128)}) custom-call(s32[288]{0:T(512)S(1)} %reshape.88.refs_0_, bf16[12,24,256,128]{3,2,1,0:T(8,128)(2,1)} %split_operator.2.refs_1_, f32[4,3,128,128]{3,2,1,0:T(8,128)S(1)} %all-to-all-done.18.refs_2_, f32[4,3,128,128]{3,2,1,0:T(8,128)S(1)} %collective-permute-done.37.refs_3_, ...), custom_call_target="tpu_custom_call" | custom-call | bytes 196608 | tf_op jit(solution)/shard_map/apply_operator/pallas_call | solution.py:173
  773.7 12.8 %apply_operator.75 = (f32[3,128,128]{2,1,0:T(8,128)}, f32[8,128]{1,0:T(8,128)}) custom-call(s32[288]{0:T(512)S(1)} %reshape.88.refs_0_, bf16[12,24,256,128]{3,2,1,0:T(8,128)(2,1)} %split_operator.2.refs_1_, f32[4,3,128,128]{3,2,1,0:T(8,128)} %all-to-all-done.19.refs_2_, f32[4,3,128,128]{3,2,1,0:T(8,128)S(1)} %collective-permute-done.39.refs_3_, ...), custom_call_target="tpu_custom_call" | custom-call | bytes 196608 | tf_op jit(solution)/shard_map/apply_operator/pallas_call | solution.py:173
  808.0 11.6 %apply_operator.76 = (f32[3,128,128]{2,1,0:T(8,128)}, f32[8,128]{1,0:T(8,128)}) custom-call(s32[288]{0:T(512)S(1)} %reshape.88.refs_0_, bf16[12,24,256,128]{3,2,1,0:T(8,128)(2,1)} %split_operator.2.refs_1_, f32[4,3,128,128]{3,2,1,0:T(8,128)S(1)} %copy-done.23, f32[4,3,128,128]{3,2,1,0:T(8,128)S(1)} %collective-permute-done.41.refs_3_, ...), custom_call_target="tpu_custom_call" | custom-call | bytes 196608 | tf_op jit(solution)/shard_map/apply_operator/pallas_call | solution.py:173
  839.0 11.6 %apply_operator.77 = (f32[3,128,128]{2,1,0:T(8,128)}, f32[8,128]{1,0:T(8,128)}) custom-call(s32[288]{0:T(512)S(1)} %reshape.88.refs_0_, bf16[12,24,256,128]{3,2,1,0:T(8,128)(2,1)} %split_operator.2.refs_1_, f32[4,3,128,128]{3,2,1,0:T(8,128)S(1)} %all-to-all-done.21.refs_2_, f32[4,3,128,128]{3,2,1,0:T(8,128)S(1)} %collective-permute-done.43.refs_3_, ...), custom_call_target="tpu_custom_call" | custom-call | bytes 196608 | tf_op jit(solution)/shard_map/apply_operator/pallas_call | solution.py:173
  869.1 12.8 %apply_operator.78 = (f32[3,128,128]{2,1,0:T(8,128)}, f32[8,128]{1,0:T(8,128)}) custom-call(s32[288]{0:T(512)S(1)} %reshape.88.refs_0_, bf16[12,24,256,128]{3,2,1,0:T(8,128)(2,1)} %split_operator.2.refs_1_, f32[4,3,128,128]{3,2,1,0:T(8,128)} %all-to-all-done.22.refs_2_, f32[4,3,128,128]{3,2,1,0:T(8,128)S(1)} %collective-permute-done.45.refs_3_, ...), custom_call_target="tpu_custom_call" | custom-call | bytes 196608 | tf_op jit(solution)/shard_map/apply_operator/pallas_call | solution.py:173
  978.2 12.1 %apply_operator.81 = (f32[3,128,128]{2,1,0:T(8,128)S(1)}, f32[8,128]{1,0:T(8,128)}) custom-call(s32[288]{0:T(512)S(1)} %reshape.88.refs_0_, bf16[12,24,256,128]{3,2,1,0:T(8,128)(2,1)} %split_operator.2.refs_1_, f32[4,3,128,128]{3,2,1,0:T(8,128)} %all-to-all-done.25.refs_2_, f32[4,3,128,128]{3,2,1,0:T(8,128)S(1)} %collective-permute-done.51.refs_3_, ...), custom_call_target="tpu_custom_call" | custom-call | bytes 196608 | tf_op jit(solution)/shard_map/apply_operator/pallas_call | solution.py:173
  1030.8 11.2 %apply_operator.82 = (f32[3,128,128]{2,1,0:T(8,128)S(1)}, f32[8,128]{1,0:T(8,128)}) custom-call(s32[288]{0:T(512)S(1)} %reshape.88.refs_0_, bf16[12,24,256,128]{3,2,1,0:T(8,128)(2,1)} %split_operator.2.refs_1_, f32[4,3,128,128]{3,2,1,0:T(8,128)S(1)} %all-to-all-done.26.refs_2_, f32[4,3,128,128]{3,2,1,0:T(8,128)S(1)} %collective-permute-done.53.refs_3_, ...), custom_call_target="tpu_custom_call" | custom-call | bytes 196608 | tf_op jit(solution)/shard_map/apply_operator/pallas_call | solution.py:173
  (488 shorter events, 726.7 us)
Async XLA Ops:
  8.7 44.5 %collective-permute-start.1 = (f32[12,12,128,128]{3,2,1,0:T(8,128)}, f32[12,12,128,128]{3,2,1,0:T(8,128)}, u32[]{:S(2)}, u32[]{:S(2)}) collective-permute-start(f32[12,12,128,128]{3,2,1,0:T(8,128)} %dynamic-slice_bitcast_fusion.1), channel_id=1, source_target_pairs={{0,4},{4,0},{1,5},{5,1},{2,6},{6,2},{3,7},{7,3},{8,12},{12,8},{9,1... | collective-permute-start | bytes 28311560 | tf_op jit(solution)/shard_map/ppermute | solution.py:231
  17.9 70.0 %collective-permute-start.5 = (f32[12,12,128,128]{3,2,1,0:T(8,128)}, f32[12,12,128,128]{3,2,1,0:T(8,128)}, u32[]{:S(2)}, u32[]{:S(2)}) collective-permute-start(f32[12,12,128,128]{3,2,1,0:T(8,128)} %dynamic-slice_bitcast_fusion), channel_id=1, source_target_pairs={{0,4},{4,0},{1,5},{5,1},{2,6},{6,2},{3,7},{7,3},{8,12},{12,8},{9,1... | collective-permute-start | bytes 28311560 | tf_op jit(solution)/shard_map/ppermute | solution.py:231
  47.2 71.3 %all-to-all-start.1 = ((f32[4,3,128,128]{3,2,1,0:T(8,128)}), f32[4,3,128,128]{3,2,1,0:T(8,128)S(1)}, u32[]{:S(2)}, u32[]{:S(2)}) async-start(f32[4,3,128,128]{3,2,1,0:T(8,128)} %broadcast_in_dim.38), calls=%async_computation.1 | async-start | bytes 1572864 | tf_op jit(solution)/shard_map/all_to_all | solution.py:241
  52.2 33.5 %collective-permute-start.4 = (s32[12,12]{1,0:T(8,128)}, s32[12,12]{1,0:T(8,128)}, u32[]{:S(2)}, u32[]{:S(2)}) collective-permute-start(s32[12,12]{1,0:T(8,128)} %bitcast.10), channel_id=1, source_target_pairs={{0,4},{4,0},{1,5},{5,1},{2,6},{6,2},{3,7},{7,3},{8,12},{12,8},{9,1... | collective-permute-start | bytes 1736 | tf_op jit(solution)/shard_map/ppermute | solution.py:231
  82.2 35.3 %collective-permute-start.6 = (f32[3,128,128]{2,1,0:T(8,128)S(1)}, f32[3,128,128]{2,1,0:T(8,128)S(1)}, u32[]{:S(2)}, u32[]{:S(2)}) collective-permute-start(f32[3,128,128]{2,1,0:T(8,128)S(1)} %get-tuple-element.122), channel_id=1, source_target_pairs={{0,8},{8,16},{16,24},{1,9},{9,17},{17,25},{2,10},{10,18},{18,26},{... | collective-permute-start | bytes 589832 | tf_op jit(solution)/shard_map/ppermute | solution.py:19
  118.5 36.6 %all-to-all-start.2 = ((f32[4,3,128,128]{3,2,1,0:T(8,128)}), f32[4,3,128,128]{3,2,1,0:T(8,128)S(1)}, u32[]{:S(2)}, u32[]{:S(2)}) async-start(f32[4,3,128,128]{3,2,1,0:T(8,128)} %copy-done.31), calls=%async_computation.2 | async-start | bytes 1572864 | tf_op jit(solution)/shard_map/all_to_all | solution.py:241
  155.1 36.7 %all-to-all-start.3 = ((f32[4,3,128,128]{3,2,1,0:T(8,128)}), f32[4,3,128,128]{3,2,1,0:T(8,128)S(1)}, u32[]{:S(2)}, u32[]{:S(2)}) async-start(f32[4,3,128,128]{3,2,1,0:T(8,128)} %copy-done.32), calls=%async_computation.3 | async-start | bytes 1572864 | tf_op jit(solution)/shard_map/all_to_all | solution.py:241
  191.8 35.5 %all-to-all-start.4 = ((f32[4,3,128,128]{3,2,1,0:T(8,128)}), f32[4,3,128,128]{3,2,1,0:T(8,128)S(1)}, u32[]{:S(2)}, u32[]{:S(2)}) async-start(f32[4,3,128,128]{3,2,1,0:T(8,128)} %copy-done.33), calls=%async_computation.4 | async-start | bytes 1572864 | tf_op jit(solution)/shard_map/all_to_all | solution.py:241
  227.3 35.2 %all-to-all-start.5 = ((f32[4,3,128,128]{3,2,1,0:T(8,128)}), f32[4,3,128,128]{3,2,1,0:T(8,128)S(1)}, u32[]{:S(2)}, u32[]{:S(2)}) async-start(f32[4,3,128,128]{3,2,1,0:T(8,128)} %copy-done.34), calls=%async_computation.5 | async-start | bytes 1572864 | tf_op jit(solution)/shard_map/all_to_all | solution.py:241
  262.5 35.2 %all-to-all-start.6 = ((f32[4,3,128,128]{3,2,1,0:T(8,128)}), f32[4,3,128,128]{3,2,1,0:T(8,128)S(1)}, u32[]{:S(2)}, u32[]{:S(2)}) async-start(f32[4,3,128,128]{3,2,1,0:T(8,128)} %copy-done.35), calls=%async_computation.6 | async-start | bytes 1572864 | tf_op jit(solution)/shard_map/all_to_all | solution.py:241
  297.6 35.2 %all-to-all-start.7 = ((f32[4,3,128,128]{3,2,1,0:T(8,128)}), f32[4,3,128,128]{3,2,1,0:T(8,128)S(1)}, u32[]{:S(2)}, u32[]{:S(2)}) async-start(f32[4,3,128,128]{3,2,1,0:T(8,128)} %copy-done.36), calls=%async_computation.7 | async-start | bytes 1572864 | tf_op jit(solution)/shard_map/all_to_all | solution.py:241
  332.8 35.7 %all-to-all-start.8 = ((f32[4,3,128,128]{3,2,1,0:T(8,128)}), f32[4,3,128,128]{3,2,1,0:T(8,128)S(1)}, u32[]{:S(2)}, u32[]{:S(2)}) async-start(f32[4,3,128,128]{3,2,1,0:T(8,128)} %copy-done.37), calls=%async_computation.8 | async-start | bytes 1572864 | tf_op jit(solution)/shard_map/all_to_all | solution.py:241
  368.5 35.2 %all-to-all-start.9 = ((f32[4,3,128,128]{3,2,1,0:T(8,128)}), f32[4,3,128,128]{3,2,1,0:T(8,128)S(1)}, u32[]{:S(2)}, u32[]{:S(2)}) async-start(f32[4,3,128,128]{3,2,1,0:T(8,128)} %copy-done.38), calls=%async_computation.9 | async-start | bytes 1572864 | tf_op jit(solution)/shard_map/all_to_all | solution.py:241
  403.7 35.2 %all-to-all-start.10 = ((f32[4,3,128,128]{3,2,1,0:T(8,128)}), f32[4,3,128,128]{3,2,1,0:T(8,128)S(1)}, u32[]{:S(2)}, u32[]{:S(2)}) async-start(f32[4,3,128,128]{3,2,1,0:T(8,128)} %copy-done.39), calls=%async_computation.10 | async-start | bytes 1572864 | tf_op jit(solution)/shard_map/all_to_all | solution.py:241
  438.9 34.1 %all-to-all-start.11 = ((f32[4,3,128,128]{3,2,1,0:T(8,128)}), f32[4,3,128,128]{3,2,1,0:T(8,128)}, u32[]{:S(2)}, u32[]{:S(2)}) async-start(f32[4,3,128,128]{3,2,1,0:T(8,128)} %get-tuple-element.172), calls=%async_computation.11 | async-start | bytes 1572864 | tf_op jit(solution)/shard_map/all_to_all | solution.py:241
  472.9 36.2 %all-to-all-start.12 = ((f32[4,3,128,128]{3,2,1,0:T(8,128)}), f32[4,3,128,128]{3,2,1,0:T(8,128)S(1)}, u32[]{:S(2)}, u32[]{:S(2)}) async-start(f32[4,3,128,128]{3,2,1,0:T(8,128)} %get-tuple-element.177), calls=%async_computation.12 | async-start | bytes 1572864 | tf_op jit(solution)/shard_map/all_to_all | solution.py:241
  643.0 31.3 %all-to-all-start.16 = ((f32[4,3,128,128]{3,2,1,0:T(8,128)}), f32[4,3,128,128]{3,2,1,0:T(8,128)S(1)}, u32[]{:S(2)}, u32[]{:S(2)}) async-start(f32[4,3,128,128]{3,2,1,0:T(8,128)} %copy-done.40), calls=%async_computation.16 | async-start | bytes 1572864 | tf_op jit(solution)/shard_map/all_to_all | solution.py:241
  704.0 32.3 %all-to-all-start.18 = ((f32[4,3,128,128]{3,2,1,0:T(8,128)}), f32[4,3,128,128]{3,2,1,0:T(8,128)S(1)}, u32[]{:S(2)}, u32[]{:S(2)}) async-start(f32[4,3,128,128]{3,2,1,0:T(8,128)} %copy-done.42), calls=%async_computation.18 | async-start | bytes 1572864 | tf_op jit(solution)/shard_map/all_to_all | solution.py:241
  766.2 32.4 %all-to-all-start.20 = ((f32[4,3,128,128]{3,2,1,0:T(8,128)}), f32[4,3,128,128]{3,2,1,0:T(8,128)S(1)}, u32[]{:S(2)}, u32[]{:S(2)}) async-start(f32[4,3,128,128]{3,2,1,0:T(8,128)} %copy-done.47), calls=%async_computation.20 | async-start | bytes 1572864 | tf_op jit(solution)/shard_map/all_to_all | solution.py:241
  799.4 32.2 %all-to-all-start.21 = ((f32[4,3,128,128]{3,2,1,0:T(8,128)}), f32[4,3,128,128]{3,2,1,0:T(8,128)S(1)}, u32[]{:S(2)}, u32[]{:S(2)}) async-start(f32[4,3,128,128]{3,2,1,0:T(8,128)} %copy-done.44), calls=%async_computation.21 | async-start | bytes 1572864 | tf_op jit(solution)/shard_map/all_to_all | solution.py:241
  861.5 32.3 %all-to-all-start.23 = ((f32[4,3,128,128]{3,2,1,0:T(8,128)}), f32[4,3,128,128]{3,2,1,0:T(8,128)S(1)}, u32[]{:S(2)}, u32[]{:S(2)}) async-start(f32[4,3,128,128]{3,2,1,0:T(8,128)} %copy-done.46), calls=%async_computation.23 | async-start | bytes 1572864 | tf_op jit(solution)/shard_map/all_to_all | solution.py:241
  894.7 35.1 %all-to-all-start.24 = ((f32[4,3,128,128]{3,2,1,0:T(8,128)}), f32[4,3,128,128]{3,2,1,0:T(8,128)S(1)}, u32[]{:S(2)}, u32[]{:S(2)}) async-start(f32[4,3,128,128]{3,2,1,0:T(8,128)} %copy-done.28), calls=%async_computation.24 | async-start | bytes 1572864 | tf_op jit(solution)/shard_map/all_to_all | solution.py:241
  929.8 35.3 %all-to-all-start.25 = ((f32[4,3,128,128]{3,2,1,0:T(8,128)}), f32[4,3,128,128]{3,2,1,0:T(8,128)}, u32[]{:S(2)}, u32[]{:S(2)}) async-start(f32[4,3,128,128]{3,2,1,0:T(8,128)} %copy-done.30), calls=%async_computation.25 | async-start | bytes 1572864 | tf_op jit(solution)/shard_map/all_to_all | solution.py:241
  965.1 36.3 %all-to-all-start.26 = ((f32[4,3,128,128]{3,2,1,0:T(8,128)}), f32[4,3,128,128]{3,2,1,0:T(8,128)S(1)}, u32[]{:S(2)}, u32[]{:S(2)}) async-start(f32[4,3,128,128]{3,2,1,0:T(8,128)} %copy-done.29), calls=%async_computation.26 | async-start | bytes 1572864 | tf_op jit(solution)/shard_map/all_to_all | solution.py:241
  (165 other events, 1620.9 us)

commit v4 on v3

--- a/solution.py
+++ b/solution.py
@@ -7,7 +7,7 @@
 
 LANES = 128
 DELAY = 2
-SLOTS = 4
+SLOTS = 8
 VMEM_BYTES = 44 * 2**20
 TOKEN = jax.ShapeDtypeStruct((8, LANES), jnp.float32)
 TOKEN_SPEC = pl.BlockSpec(TOKEN.shape, lambda *_: (0, 0))
@@ -119,18 +119,21 @@
     @pl.when(row == 0)
     def _():
         token_ref[...] = jnp.zeros_like(token_ref)
-        lane = lax.broadcasted_iota(jnp.int32, (size, 2 * lanes), 1) % lanes // span
-        masks = [(lane == q).astype(jnp.float32).astype(jnp.bfloat16) for q in range(pack)]
+        left = lax.broadcasted_iota(jnp.int32, (size, lanes), 1) < span
         for start, ref in ((0, own_ref), (pieces * groups, other_ref)):
             for piece in range(pieces):
                 for group in range(groups):
                     tile = ref[piece, group]
-                    high = tile.astype(jnp.bfloat16)
-                    low = (tile - high.astype(jnp.float32)).astype(jnp.bfloat16)
-                    both = jnp.concatenate([high, low], axis=1)
+                    high = tile.astype(jnp.bfloat16).astype(jnp.float32)
+                    low = tile - high
                     base = (start + piece * groups + group) * pack
-                    for q in range(pack):
-                        tiles[base + q] = both * masks[q] if pack > 1 else both
+                    if pack == 1:
+                        tiles[base] = jnp.concatenate([high, low], axis=1).astype(jnp.bfloat16)
+                    else:
+                        first = jnp.where(left, high, pltpu.roll(low, span, 1))
+                        second = jnp.where(left, pltpu.roll(high, span, 1), low)
+                        tiles[base] = first.astype(jnp.bfloat16)
+                        tiles[base + 1] = second.astype(jnp.bfloat16)
 
     fetch(row).wait()
     slot = lax.rem(row, count)
@@ -138,14 +141,10 @@
     block = jnp.concatenate([slots[slot, k] for k in range(picks)], axis=1)
     product = jnp.dot(block, picked, preferred_element_type=jnp.float32)
     total = product[:size] + product[size:]
-    total = total[:, :lanes] + total[:, lanes:]
-    shift = span
-    while shift < lanes:
-        total = total + pltpu.roll(total, shift, 1)
-        shift *= 2
     if pack == 1:
-        result_ref[0] = total
+        result_ref[0] = total[:, :lanes] + total[:, lanes:]
     else:
+        total = total + pltpu.roll(total, span, 1)
         lane = lax.broadcasted_iota(jnp.int32, total.shape, 1)
         result_ref[0] = jnp.where(lane < lax.rem(row, pack) * span, result_ref[0], total)
 
@@ -162,7 +161,7 @@
         out_specs=[pl.BlockSpec((1, size, lanes), lambda row, *_: (row // pack, 0, 0)), TOKEN_SPEC],
         scratch_shapes=[
             pltpu.VMEM((SLOTS, picks, twice, depth), jnp.bfloat16),
-            pltpu.VMEM((2 * pieces * groups * pack, size, 2 * lanes), jnp.bfloat16),
+            pltpu.VMEM((2 * pieces * groups * pack, size, 2 * lanes // pack), jnp.bfloat16),
             pltpu.SemaphoreType.DMA((SLOTS,)),
         ],
     )
@@ -181,14 +180,12 @@
 
 
 def sum_kernel(which_ref, arrived_ref, store_ref, *refs):
-    copies_ref, token_ref = refs[-2:]
-    total = arrived_ref[...] + store_ref[0]
-    for copy in range(copies_ref.shape[0]):
-        copies_ref[copy] = total
+    total_ref, token_ref = refs[-2:]
+    total_ref[...] = arrived_ref[...] + store_ref[0]
     token_ref[...] = jnp.zeros_like(token_ref)
 
 
-def sum_with(copies, arrived, store, which, *after):
+def sum_with(arrived, store, which, *after):
     spec = pltpu.PrefetchScalarGridSpec(
         num_scalar_prefetch=1,
         grid=(1,),
@@ -198,14 +195,14 @@
         ]
         + [pl.BlockSpec(memory_space=pl.ANY)] * len(after),
         out_specs=[
-            pl.BlockSpec((copies,) + arrived.shape, lambda i, which_ref: (0, 0, 0, 0)),
+            pl.BlockSpec(arrived.shape, lambda i, which_ref: (0, 0, 0)),
             TOKEN_SPEC,
         ],
     )
     return pl.pallas_call(
         sum_kernel,
         grid_spec=spec,
-        out_shape=[jax.ShapeDtypeStruct((copies,) + arrived.shape, arrived.dtype), TOKEN],
+        out_shape=[jax.ShapeDtypeStruct(arrived.shape, arrived.dtype), TOKEN],
         compiler_params=pltpu.CompilerParams(vmem_limit_bytes=VMEM_BYTES),
         name="sum_with",
     )(which.reshape(1), arrived, store, *after)
@@ -216,7 +213,7 @@
     piece_rows, columns = source.shape
     size = tr_vals.shape[-1]
     blocks = piece_rows // size
-    pack = next(n for n in (4, 2, 1) if blocks % n == 0)
+    pack = 2 if blocks % 2 == 0 else 1
     batches, delay = columns // (LANES // pack), DELAY
     length, pieces = lax.axis_size("slab"), lax.axis_size("col")
     position = lax.axis_index("slab")
@@ -237,8 +234,8 @@
     trans = halves(tr_vals[0, 0, 0], tr_cols[0, 0, 0])
     refl = halves(rf_vals[0, 0, 0], rf_cols[0, 0, 0])
 
-    def gather(copies):
-        gathered = lax.all_to_all(copies, "col", 0, 0)
+    def gather(piece):
+        gathered = lax.all_gather(piece, "col", axis=0)
         return gathered, lax.ppermute(gathered, "row", swap)
 
     moments = batches + delay * (length - 1)
@@ -248,10 +245,9 @@
             offset = position if steps > 0 else length - 1 - position
             which = jnp.clip(moment - delay * offset, 0, batches - 1) + start
             if moment < delay:
-                piece = lax.dynamic_index_in_dim(first, which, 0, keepdims=False)
-                return jnp.broadcast_to(piece[None], (pieces,) + piece.shape), None
+                return lax.dynamic_index_in_dim(first, which, 0, keepdims=False), None
             arrived = passed_along(moved[moment - delay], "slab", steps)
-            return sum_with(pieces, arrived, first, which, *tokens[moment - delay : moment - delay + 1])
+            return sum_with(arrived, first, which, *tokens[moment - delay : moment - delay + 1])
 
         moved, reflected, tokens = [], [], []
         incident, _ = incident_of(0)

time: 1070 us -> 915 us (0.86)
  waiting for transfers between devices: 171 us -> 345 us
  Pallas kernels: 526 us -> 368 us
  starting transfers between devices: 175 us -> 45.8 us
  blocking collectives: 50.7 us -> 0 us
  between operations: 2.39 us -> 15.1 us
    all_gather x0 -> x20, waiting for transfers between devices: none -> 195 us  [gather(): gathered = lax.all_gather(piece, 'col', axis=0)]
    pallas_call x42 -> x30, Pallas kernels: 479 us -> 310 us  [apply_operator(): pl.pallas_call(kernel, grid_spec=spec, out_shape=[jax.ShapeDtypeStruct((g...]
    all_to_all x26 -> x0, starting transfers between devices: 130 us -> none  [gather(): gathered = lax.all_to_all(copies, 'col', 0, 0)]
    all_to_all x2 -> x0, blocking collectives: 50.7 us -> none  [gather(): gathered = lax.all_to_all(copies, 'col', 0, 0)]
    all_to_all x26 -> x0, waiting for transfers between devices: 25 us -> none  [gather(): gathered = lax.all_to_all(copies, 'col', 0, 0)]
    pallas_call x24 -> x16, Pallas kernels: 8.74 us -> 20.9 us  [sum_with(): pl.pallas_call(sum_kernel, grid_spec=spec, out_shape=[jax.ShapeDtypeStruc...]
    ppermute x28 -> x20, waiting for transfers between devices: 45.3 us -> 54.1 us  [gather(): return (gathered, lax.ppermute(gathered, 'row', swap))]
    ppermute x24 -> x16, waiting for transfers between devices: 99.5 us -> 91.9 us  [passed_along(): lax.ppermute(value, axis, [(source, source + steps) for source in range(i...]
  transfers between devices with their start and end apart: 82 -> 60, of which waited for: 35 -> 42; matrix products, arithmetic and copies ran while one was open for 6% -> 6% of each run, Pallas kernels for 46% -> 37%
where the time goes in v4:
time: 915 us; the launch traced here: 904 us
  Pallas kernels  368 us (40%)
  waiting for transfers between devices  345 us (38%)
  local copies, waits for them, and re-layouts  127 us (14%)
  starting transfers between devices  45.8 us (5%)
  between operations  15.1 us (2%)
    pallas_call x30, Pallas kernels, apply_operator(): pl.pallas_call(kernel, grid_spec=spec, out_shape=[jax.ShapeDtypeStruct((g...  310 us
    all_gather x20, waiting for transfers between devices, gather(): gathered = lax.all_gather(piece, 'col', axis=0)  195 us
    unnamed x217, local copies, waits for them, and re-layouts  103 us
    ppermute x16, waiting for transfers between devices, passed_along(): lax.ppermute(value, axis, [(source, source + steps) for source in range(i...  91.9 us
    ppermute x20, waiting for transfers between devices, gather(): return (gathered, lax.ppermute(gathered, 'row', swap))  54.1 us
    ppermute x16, starting transfers between devices, passed_along(): lax.ppermute(value, axis, [(source, source + steps) for source in range(i...  42.6 us
    pallas_call x2, Pallas kernels, split_operator(): pl.pallas_call(split_kernel, grid_spec=spec, out_shape=jax.ShapeDtypeStru...  34 us
    pallas_call x16, Pallas kernels, sum_with(): pl.pallas_call(sum_kernel, grid_spec=spec, out_shape=[jax.ShapeDtypeStruc...  20.9 us
  transfers between devices with their start and end apart: 60, of which 42 were waited for; matrix products, arithmetic and copies ran while one was open for 6% of the time, Pallas kernels for 37%

profile of v4, /device:TPU:0, one launch (start us, length us, event | category | flops | bytes accessed | tf_op | source)
XLA Modules:
  0.0 904.4 jit_solution(5988513391420874341)
XLA Ops:
  27.2 39.0 %all-gather.37.cloned.1.call-done.refs_2_ = f32[4,6,128,128]{3,2,1,0:T(8,128)} async-done(((f32[1,6,128,128]{3,2,1,0:T(8,128)}), f32[4,6,128,128]{3,2,1,0:T(8,128)}) %all-gather.37.cloned.1.call-update) | async-done | bytes 1572880 | tf_op jit(solution)/shard_map/all_gather | solution.py:238
  69.9 17.2 %split_operator.2.refs_1_ = bf16[12,24,256,128]{3,2,1,0:T(8,128)(2,1)} custom-call(s32[1]{0:T(128)} %bitcast.2.place_ref, f32[24,12,128,128]{3,2,1,0:T(8,128)} %bitcast.146, f32[12,12,128,128]{3,2,1,0:T(8,128)} %collective-permute-done.1.other_ref), custom_call_target="tpu_custom_call" | custom-call | tf_op jit(solution)/shard_map/split_operator/pallas_call | solution.py:89
  87.0 11.4 %apply_operator.30 = (f32[6,128,128]{2,1,0:T(8,128)S(1)}, f32[8,128]{1,0:T(8,128)S(1)}) custom-call(s32[288]{0:T(512)S(1)} %reshape.64.refs_0_, bf16[12,24,256,128]{3,2,1,0:T(8,128)(2,1)} %split_operator.2.refs_1_, f32[4,6,128,128]{3,2,1,0:T(8,128)S(1)} %copy-done.9, f32[4,6,128,128]{3,2,1,0:T(8,128)} %collective-permute-done.2.refs_3_), custom_call_target="tpu_custom_call" | custom-call | bytes 393216 | tf_op jit(solution)/shard_map/apply_operator/pallas_call | solution.py:172
  107.0 16.9 %split_operator.3.refs_1_ = bf16[12,24,256,128]{3,2,1,0:T(8,128)(2,1)} custom-call(s32[1]{0:T(128)} %bitcast.2.place_ref, f32[24,12,128,128]{3,2,1,0:T(8,128)} %bitcast.147, f32[12,12,128,128]{3,2,1,0:T(8,128)} %collective-permute-done.5.other_ref), custom_call_target="tpu_custom_call" | custom-call | tf_op jit(solution)/shard_map/split_operator/pallas_call | solution.py:89
  123.9 11.4 %apply_operator.31 = (f32[6,128,128]{2,1,0:T(8,128)S(1)}, f32[8,128]{1,0:T(8,128)S(1)}) custom-call(s32[288]{0:T(512)S(1)} %reshape.66.refs_0_, bf16[12,24,256,128]{3,2,1,0:T(8,128)(2,1)} %split_operator.3.refs_1_, f32[4,6,128,128]{3,2,1,0:T(8,128)S(1)} %copy-done.9, f32[4,6,128,128]{3,2,1,0:T(8,128)} %collective-permute-done.2.refs_3_, ...), custom_call_target="tpu_custom_call" | custom-call | bytes 393216 | tf_op jit(solution)/shard_map/apply_operator/pallas_call | solution.py:172
  254.0 10.8 %apply_operator.38 = (f32[6,128,128]{2,1,0:T(8,128)}, f32[8,128]{1,0:T(8,128)S(1)}) custom-call(s32[288]{0:T(512)S(1)} %reshape.64.refs_0_, bf16[12,24,256,128]{3,2,1,0:T(8,128)(2,1)} %split_operator.2.refs_1_, f32[4,6,128,128]{3,2,1,0:T(8,128)S(1)} %bitcast.118, f32[4,6,128,128]{3,2,1,0:T(8,128)S(1)} %collective-permute-done.11.refs_3_, ...), custom_call_target="tpu_custom_call" | custom-call | bytes 393216 | tf_op jit(solution)/shard_map/apply_operator/pallas_call | solution.py:172
  291.4 10.8 %apply_operator.40 = (f32[6,128,128]{2,1,0:T(8,128)}, f32[8,128]{1,0:T(8,128)S(1)}) custom-call(s32[288]{0:T(512)S(1)} %reshape.64.refs_0_, bf16[12,24,256,128]{3,2,1,0:T(8,128)(2,1)} %split_operator.2.refs_1_, f32[4,6,128,128]{3,2,1,0:T(8,128)S(1)} %bitcast.121, f32[4,6,128,128]{3,2,1,0:T(8,128)S(1)} %collective-permute-done.13.refs_3_, ...), custom_call_target="tpu_custom_call" | custom-call | bytes 393216 | tf_op jit(solution)/shard_map/apply_operator/pallas_call | solution.py:172
  329.0 10.8 %apply_operator.42 = (f32[6,128,128]{2,1,0:T(8,128)}, f32[8,128]{1,0:T(8,128)S(1)}) custom-call(s32[288]{0:T(512)S(1)} %reshape.64.refs_0_, bf16[12,24,256,128]{3,2,1,0:T(8,128)(2,1)} %split_operator.2.refs_1_, f32[4,6,128,128]{3,2,1,0:T(8,128)S(1)} %bitcast.124, f32[4,6,128,128]{3,2,1,0:T(8,128)S(1)} %collective-permute-done.15.refs_3_, ...), custom_call_target="tpu_custom_call" | custom-call | bytes 393216 | tf_op jit(solution)/shard_map/apply_operator/pallas_call | solution.py:172
  366.6 10.8 %apply_operator.44 = (f32[6,128,128]{2,1,0:T(8,128)}, f32[8,128]{1,0:T(8,128)S(1)}) custom-call(s32[288]{0:T(512)S(1)} %reshape.64.refs_0_, bf16[12,24,256,128]{3,2,1,0:T(8,128)(2,1)} %split_operator.2.refs_1_, f32[4,6,128,128]{3,2,1,0:T(8,128)S(1)} %bitcast.127, f32[4,6,128,128]{3,2,1,0:T(8,128)S(1)} %collective-permute-done.17.refs_3_, ...), custom_call_target="tpu_custom_call" | custom-call | bytes 393216 | tf_op jit(solution)/shard_map/apply_operator/pallas_call | solution.py:172
  399.7 35.5 %all-gather.59.cloned.1.call-done = f32[24,128,128]{2,1,0:T(8,128)} async-done(((f32[6,128,128]{2,1,0:T(8,128)}), f32[24,128,128]{2,1,0:T(8,128)}) %all-gather.59.cloned.1.call-update) | async-done | bytes 1572880 | tf_op jit(solution)/shard_map/all_gather | solution.py:238
  490.3 35.6 %all-gather.41.cloned.1.call-done.refs_2_ = f32[4,6,128,128]{3,2,1,0:T(8,128)} async-done(((f32[1,6,128,128]{3,2,1,0:T(8,128)}), f32[4,6,128,128]{3,2,1,0:T(8,128)}) %all-gather.41.cloned.1.call-update) | async-done | bytes 1572880 | tf_op jit(solution)/shard_map/all_gather | solution.py:238
  530.9 10.3 %apply_operator.50 = (f32[6,128,128]{2,1,0:T(8,128)S(1)}, f32[8,128]{1,0:T(8,128)}) custom-call(s32[288]{0:T(512)S(1)} %reshape.64.refs_0_, bf16[12,24,256,128]{3,2,1,0:T(8,128)(2,1)} %split_operator.2.refs_1_, f32[4,6,128,128]{3,2,1,0:T(8,128)S(1)} %copy-done.48, f32[4,6,128,128]{3,2,1,0:T(8,128)S(1)} %collective-permute-done.22.refs_3_), custom_call_target="tpu_custom_call" | custom-call | bytes 393216 | tf_op jit(solution)/shard_map/apply_operator/pallas_call | solution.py:172
  542.5 11.7 %collective-permute-done.24.arrived_ref = f32[6,128,128]{2,1,0:T(8,128)S(1)} collective-permute-done((f32[6,128,128]{2,1,0:T(8,128)S(1)}, f32[6,128,128]{2,1,0:T(8,128)S(1)}, u32[]{:S(2)}, u32[]{:S(2)}) %collective-permute-start.24) | collective-permute-done | bytes 393248 | tf_op jit(solution)/shard_map/ppermute | solution.py:19
  579.8 11.7 %collective-permute-done.26.arrived_ref = f32[6,128,128]{2,1,0:T(8,128)S(1)} collective-permute-done((f32[6,128,128]{2,1,0:T(8,128)S(1)}, f32[6,128,128]{2,1,0:T(8,128)S(1)}, u32[]{:S(2)}, u32[]{:S(2)}) %collective-permute-start.26) | collective-permute-done | bytes 393248 | tf_op jit(solution)/shard_map/ppermute | solution.py:19
  605.9 10.3 %apply_operator.52 = (f32[6,128,128]{2,1,0:T(8,128)S(1)}, f32[8,128]{1,0:T(8,128)}) custom-call(s32[288]{0:T(512)S(1)} %reshape.64.refs_0_, bf16[12,24,256,128]{3,2,1,0:T(8,128)(2,1)} %split_operator.2.refs_1_, f32[4,6,128,128]{3,2,1,0:T(8,128)S(1)} %bitcast.144, f32[4,6,128,128]{3,2,1,0:T(8,128)S(1)} %collective-permute-done.25.refs_3_, ...), custom_call_target="tpu_custom_call" | custom-call | bytes 393216 | tf_op jit(solution)/shard_map/apply_operator/pallas_call | solution.py:172
  617.5 11.7 %collective-permute-done.28.arrived_ref = f32[6,128,128]{2,1,0:T(8,128)S(1)} collective-permute-done((f32[6,128,128]{2,1,0:T(8,128)S(1)}, f32[6,128,128]{2,1,0:T(8,128)S(1)}, u32[]{:S(2)}, u32[]{:S(2)}) %collective-permute-start.28) | collective-permute-done | bytes 393248 | tf_op jit(solution)/shard_map/ppermute | solution.py:19
  654.9 11.7 %collective-permute-done.30.arrived_ref = f32[6,128,128]{2,1,0:T(8,128)S(1)} collective-permute-done((f32[6,128,128]{2,1,0:T(8,128)S(1)}, f32[6,128,128]{2,1,0:T(8,128)S(1)}, u32[]{:S(2)}, u32[]{:S(2)}) %collective-permute-start.30) | collective-permute-done | bytes 393248 | tf_op jit(solution)/shard_map/ppermute | solution.py:19
  680.8 10.3 %apply_operator.54 = (f32[6,128,128]{2,1,0:T(8,128)S(1)}, f32[8,128]{1,0:T(8,128)}) custom-call(s32[288]{0:T(512)S(1)} %reshape.64.refs_0_, bf16[12,24,256,128]{3,2,1,0:T(8,128)(2,1)} %split_operator.2.refs_1_, f32[4,6,128,128]{3,2,1,0:T(8,128)S(1)} %bitcast.138, f32[4,6,128,128]{3,2,1,0:T(8,128)S(1)} %collective-permute-done.29.refs_3_, ...), custom_call_target="tpu_custom_call" | custom-call | bytes 393216 | tf_op jit(solution)/shard_map/apply_operator/pallas_call | solution.py:172
  692.4 11.7 %collective-permute-done.32.arrived_ref = f32[6,128,128]{2,1,0:T(8,128)S(1)} collective-permute-done((f32[6,128,128]{2,1,0:T(8,128)S(1)}, f32[6,128,128]{2,1,0:T(8,128)S(1)}, u32[]{:S(2)}, u32[]{:S(2)}) %collective-permute-start.32) | collective-permute-done | bytes 393248 | tf_op jit(solution)/shard_map/ppermute | solution.py:19
  729.8 11.7 %collective-permute-done.34.arrived_ref = f32[6,128,128]{2,1,0:T(8,128)S(1)} collective-permute-done((f32[6,128,128]{2,1,0:T(8,128)S(1)}, f32[6,128,128]{2,1,0:T(8,128)S(1)}, u32[]{:S(2)}, u32[]{:S(2)}) %collective-permute-start.34) | collective-permute-done | bytes 393248 | tf_op jit(solution)/shard_map/ppermute | solution.py:19
  767.3 11.7 %collective-permute-done.36.arrived_ref = f32[6,128,128]{2,1,0:T(8,128)S(1)} collective-permute-done((f32[6,128,128]{2,1,0:T(8,128)S(1)}, f32[6,128,128]{2,1,0:T(8,128)S(1)}, u32[]{:S(2)}, u32[]{:S(2)}) %collective-permute-start.36) | collective-permute-done | bytes 393248 | tf_op jit(solution)/shard_map/ppermute | solution.py:19
  793.1 10.6 %apply_operator.57 = (f32[6,128,128]{2,1,0:T(8,128)S(1)}, f32[8,128]{1,0:T(8,128)}) custom-call(s32[288]{0:T(512)S(1)} %reshape.64.refs_0_, bf16[12,24,256,128]{3,2,1,0:T(8,128)(2,1)} %split_operator.2.refs_1_, f32[4,6,128,128]{3,2,1,0:T(8,128)S(1)} %bitcast.132, f32[4,6,128,128]{3,2,1,0:T(8,128)S(1)} %collective-permute-done.35.refs_3_, ...), custom_call_target="tpu_custom_call" | custom-call | bytes 393216 | tf_op jit(solution)/shard_map/apply_operator/pallas_call | solution.py:172
  830.7 32.3 %all-gather.75.cloned.1.call-done = f32[24,128,128]{2,1,0:T(8,128)} async-done(((f32[6,128,128]{2,1,0:T(8,128)}), f32[24,128,128]{2,1,0:T(8,128)}) %all-gather.75.cloned.1.call-update) | async-done | bytes 1572880 | tf_op jit(solution)/shard_map/all_gather | solution.py:238
  871.9 10.5 %apply_operator.58 = (f32[6,128,128]{2,1,0:T(8,128)S(1)}, f32[8,128]{1,0:T(8,128)}) custom-call(s32[288]{0:T(512)S(1)} %reshape.64.refs_0_, bf16[12,24,256,128]{3,2,1,0:T(8,128)(2,1)} %split_operator.2.refs_1_, f32[4,6,128,128]{3,2,1,0:T(8,128)S(1)} %bitcast.130, f32[4,6,128,128]{3,2,1,0:T(8,128)S(1)} %collective-permute-done.37.refs_3_, ...), custom_call_target="tpu_custom_call" | custom-call | bytes 393216 | tf_op jit(solution)/shard_map/apply_operator/pallas_call | solution.py:172
  (398 shorter events, 512.8 us)
Async XLA Ops:
  6.5 59.7 %all-gather.37.cloned.1.call-start = ((), (), s32[]{:S(2)}) async-start(), calls=%async_computation | async-start | bytes 1966080 | tf_op jit(solution)/shard_map/all_gather | solution.py:238
  15.2 54.7 %collective-permute-start.1 = (f32[12,12,128,128]{3,2,1,0:T(8,128)}, f32[12,12,128,128]{3,2,1,0:T(8,128)}, u32[]{:S(2)}, u32[]{:S(2)}) collective-permute-start(f32[12,12,128,128]{3,2,1,0:T(8,128)} %dynamic-slice_bitcast_fusion.1), channel_id=1, source_target_pairs={{0,4},{4,0},{1,5},{5,1},{2,6},{6,2},{3,7},{7,3},{8,12},{12,8},{9,1... | collective-permute-start | bytes 28311560 | tf_op jit(solution)/shard_map/ppermute | solution.py:228
  24.4 82.6 %collective-permute-start.5 = (f32[12,12,128,128]{3,2,1,0:T(8,128)}, f32[12,12,128,128]{3,2,1,0:T(8,128)}, u32[]{:S(2)}, u32[]{:S(2)}) collective-permute-start(f32[12,12,128,128]{3,2,1,0:T(8,128)} %dynamic-slice_bitcast_fusion), channel_id=1, source_target_pairs={{0,4},{4,0},{1,5},{5,1},{2,6},{6,2},{3,7},{7,3},{8,12},{12,8},{9,1... | collective-permute-start | bytes 28311560 | tf_op jit(solution)/shard_map/ppermute | solution.py:228
  26.4 112.1 %all-gather.39.cloned.1.call-start = ((), (), s32[]{:S(2)}) async-start(), calls=%async_computation.1 | async-start | bytes 1966080 | tf_op jit(solution)/shard_map/all_gather | solution.py:238
  27.2 146.1 %all-gather.45.cloned.1.call-start = ((), (), s32[]{:S(2)}) async-start(), calls=%async_computation.4 | async-start | bytes 1966080 | tf_op jit(solution)/shard_map/all_gather | solution.py:238
  138.5 71.9 %all-gather.47.cloned.1.call-start = ((), (), s32[]{:S(2)}) async-start(), calls=%async_computation.5 | async-start | bytes 1966080 | tf_op jit(solution)/shard_map/all_gather | solution.py:238
  173.0 74.7 %all-gather.49.cloned.1.call-start = ((), (), s32[]{:S(2)}) async-start(), calls=%async_computation.6 | async-start | bytes 1966080 | tf_op jit(solution)/shard_map/all_gather | solution.py:238
  208.1 77.1 %all-gather.51.cloned.1.call-start = ((), (), s32[]{:S(2)}) async-start(), calls=%async_computation.7 | async-start | bytes 1966080 | tf_op jit(solution)/shard_map/all_gather | solution.py:238
  245.5 77.2 %all-gather.53.cloned.1.call-start = ((), (), s32[]{:S(2)}) async-start(), calls=%async_computation.8 | async-start | bytes 1966080 | tf_op jit(solution)/shard_map/all_gather | solution.py:238
  283.6 76.6 %all-gather.55.cloned.1.call-start = ((), (), s32[]{:S(2)}) async-start(), calls=%async_computation.9 | async-start | bytes 1966080 | tf_op jit(solution)/shard_map/all_gather | solution.py:238
  321.0 76.8 %all-gather.57.cloned.1.call-start = ((), (), s32[]{:S(2)}) async-start(), calls=%async_computation.10 | async-start | bytes 1966080 | tf_op jit(solution)/shard_map/all_gather | solution.py:238
  358.6 76.7 %all-gather.59.cloned.1.call-start = ((), (), s32[]{:S(2)}) async-start(), calls=%async_computation.11 | async-start | bytes 1966080 | tf_op jit(solution)/shard_map/all_gather | solution.py:238
  395.0 130.8 %all-gather.41.cloned.1.call-start = ((), (), s32[]{:S(2)}) async-start(), calls=%async_computation.2 | async-start | bytes 1966080 | tf_op jit(solution)/shard_map/all_gather | solution.py:238
  397.8 47.1 %collective-permute-start.19 = (f32[4,6,128,128]{3,2,1,0:T(8,128)}, f32[4,6,128,128]{3,2,1,0:T(8,128)S(1)}, u32[]{:S(2)}, u32[]{:S(2)}) collective-permute-start(f32[4,6,128,128]{3,2,1,0:T(8,128)} %bitcast.108), channel_id=1, source_target_pairs={{0,4},{4,0},{1,5},{5,1},{2,6},{6,2},{3,7},{7,3},{8,12},{12,8},{9,1... | collective-permute-start | bytes 4718600 | tf_op jit(solution)/shard_map/ppermute | solution.py:239
  489.6 73.6 %all-gather.43.cloned.1.call-start = ((), (), s32[]{:S(2)}) async-start(), calls=%async_computation.3 | async-start | bytes 1966080 | tf_op jit(solution)/shard_map/all_gather | solution.py:238
  490.2 110.6 %all-gather.61.cloned.1.call-start = ((), (), s32[]{:S(2)}) async-start(), calls=%async_computation.12 | async-start | bytes 1966080 | tf_op jit(solution)/shard_map/all_gather | solution.py:238
  557.1 81.2 %all-gather.63.cloned.1.call-start = ((), (), s32[]{:S(2)}) async-start(), calls=%async_computation.13 | async-start | bytes 1966080 | tf_op jit(solution)/shard_map/all_gather | solution.py:238
  594.5 81.2 %all-gather.65.cloned.1.call-start = ((), (), s32[]{:S(2)}) async-start(), calls=%async_computation.14 | async-start | bytes 1966080 | tf_op jit(solution)/shard_map/all_gather | solution.py:238
  632.2 81.0 %all-gather.67.cloned.1.call-start = ((), (), s32[]{:S(2)}) async-start(), calls=%async_computation.15 | async-start | bytes 1966080 | tf_op jit(solution)/shard_map/all_gather | solution.py:238
  669.6 81.1 %all-gather.69.cloned.1.call-start = ((), (), s32[]{:S(2)}) async-start(), calls=%async_computation.16 | async-start | bytes 1966080 | tf_op jit(solution)/shard_map/all_gather | solution.py:238
  707.0 81.0 %all-gather.71.cloned.1.call-start = ((), (), s32[]{:S(2)}) async-start(), calls=%async_computation.17 | async-start | bytes 1966080 | tf_op jit(solution)/shard_map/all_gather | solution.py:238
  744.5 84.4 %all-gather.73.cloned.1.call-start = ((), (), s32[]{:S(2)}) async-start(), calls=%async_computation.18 | async-start | bytes 1966080 | tf_op jit(solution)/shard_map/all_gather | solution.py:238
  781.9 81.1 %all-gather.75.cloned.1.call-start = ((), (), s32[]{:S(2)}) async-start(), calls=%async_computation.19 | async-start | bytes 1966080 | tf_op jit(solution)/shard_map/all_gather | solution.py:238
  828.8 43.0 %collective-permute-start.37 = (f32[4,6,128,128]{3,2,1,0:T(8,128)}, f32[4,6,128,128]{3,2,1,0:T(8,128)S(1)}, u32[]{:S(2)}, u32[]{:S(2)}) collective-permute-start(f32[4,6,128,128]{3,2,1,0:T(8,128)} %bitcast.129), channel_id=1, source_target_pairs={{0,4},{4,0},{1,5},{5,1},{2,6},{6,2},{3,7},{7,3},{8,12},{12,8},{9,1... | collective-permute-start | bytes 4718600 | tf_op jit(solution)/shard_map/ppermute | solution.py:239
  (129 other events, 1307.1 us)
Sparse Core Ops, SparseCore 0:
  26.6 39.6 all-gather.36
  67.8 35.9 all-gather.38
  138.6 34.2 all-gather.44
  174.4 35.9 all-gather.46
  211.8 35.9 all-gather.48
  249.2 35.9 all-gather.50
  286.7 35.9 all-gather.52
  324.3 35.9 all-gather.54
  361.8 35.9 all-gather.56
  399.3 35.9 all-gather.58
  489.8 36.0 all-gather.40
  527.3 35.9 all-gather.42
  564.8 36.0 all-gather.60
  602.3 35.9 all-gather.62
  639.7 36.0 all-gather.64
  677.2 35.9 all-gather.66
  714.6 35.9 all-gather.68
  752.1 35.9 all-gather.70
  789.6 35.9 all-gather.72
  827.1 35.9 all-gather.74

commit v5 on v4

v5 whole, which is shorter than its diff:
```python
import jax
import jax.numpy as jnp
from jax import lax
from jax.experimental import pallas as pl
from jax.experimental.pallas import tpu as pltpu
from jax.sharding import PartitionSpec as P

LANES = 128
DELAY = 2
SLOTS = 8
FRACTION = 3
VMEM_BYTES = 44 * 2**20
TOKEN = jax.ShapeDtypeStruct((8, LANES), jnp.float32)
TOKEN_SPEC = pl.BlockSpec(TOKEN.shape, lambda *_: (0, 0))


def divisor_up_to(number, limit):
    return max(n for n in range(1, limit + 1) if number % n == 0)


def passed_along(value, axis, steps):
    count = lax.axis_size(axis)
    initial, last = (max(0, -steps), min(count, count - steps))
    return lax.ppermute(value, axis, [(source, source + steps) for source in range(initial, last)])


def pack_kernel(rows_ref, packed_ref):
    batches, _, size, lanes = packed_ref.shape
    pack = rows_ref.shape[0] // size
    span = lanes // pack
    for batch in range(batches):
        found = [rows_ref[q * size : (q + 1) * size, batch * span : (batch + 1) * span] for q in range(pack)]
        packed_ref[batch, 0] = jnp.concatenate(found, axis=1)


def unpack_kernel(*refs):
    rows_ref = refs[-1]
    _, size, lanes = refs[0].shape
    pack = rows_ref.shape[0] // size
    span = lanes // pack
    for q in range(pack):
        found = [ref[0, :, q * span : (q + 1) * span] for ref in refs[:-1]]
        rows_ref[q * size : (q + 1) * size, :] = jnp.concatenate(found, axis=1)


def packed_trace(rows, batches, pack, size):
    groups = rows.shape[0] // (pack * size)
    return pl.pallas_call(
        pack_kernel,
        grid=(groups,),
        in_specs=[pl.BlockSpec((pack * size, rows.shape[1]), lambda i: (i, 0))],
        out_specs=pl.BlockSpec((batches, 1, size, LANES), lambda i: (0, i, 0, 0)),
        out_shape=jax.ShapeDtypeStruct((batches, groups, size, LANES), rows.dtype),
        compiler_params=pltpu.CompilerParams(vmem_limit_bytes=VMEM_BYTES),
        name="pack_trace",
    )(rows)


def unpacked_trace(packed, pack):
    groups, size, lanes = packed[0].shape
    columns = len(packed) * (lanes // pack)
    return pl.pallas_call(
        unpack_kernel,
        grid=(groups,),
        in_specs=[pl.BlockSpec((1, size, lanes), lambda i: (i, 0, 0))] * len(packed),
        out_specs=pl.BlockSpec((pack * size, columns), lambda i: (i, 0)),
        out_shape=jax.ShapeDtypeStruct((groups * pack * size, columns), jnp.float32),
        compiler_params=pltpu.CompilerParams(vmem_limit_bytes=VMEM_BYTES),
        name="unpack_trace",
    )(*packed)


def in_hbm(array):
    return pltpu.with_memory_space_constraint(array, pltpu.HBM)


def half_kernel(place_ref, values_ref, *refs):
    refs[-1][...] = values_ref[...]


def other_half(values, place, after):
    rows = values.shape[0] // 2
    step = divisor_up_to(rows, 3)
    block = (step,) + values.shape[1:]
    spec = pltpu.PrefetchScalarGridSpec(
        num_scalar_prefetch=1,
        grid=(rows // step,),
        in_specs=[
            pl.BlockSpec(block, lambda i, place_ref: ((1 - place_ref[0]) * (rows // step) + i, 0, 0, 0)),
            pl.BlockSpec(memory_space=pl.ANY),
        ],
        out_specs=pl.BlockSpec(block, lambda i, place_ref: (i, 0, 0, 0)),
    )
    return pl.pallas_call(
        half_kernel,
        grid_spec=spec,
        out_shape=jax.ShapeDtypeStruct((rows,) + values.shape[1:], values.dtype),
        compiler_params=pltpu.CompilerParams(vmem_limit_bytes=VMEM_BYTES),
        name="other_half",
    )(place, values, after)


def split_kernel(place_ref, own_ref, other_ref, *refs):
    parts_ref = refs[-1]
    picks, size = own_ref.shape[1:3]
    for start, values_ref in ((0, own_ref), (picks, other_ref)):
        for k in range(picks):
            value = values_ref[0, k]
            high = value.astype(jnp.bfloat16)
            parts_ref[0, start + k, :size] = high
            parts_ref[0, start + k, size:] = (value - high.astype(jnp.float32)).astype(jnp.bfloat16)


def split_operator(values, other, place, after):
    _, picks, size, depth = values.shape
    rows = other.shape[0]
    spec = pltpu.PrefetchScalarGridSpec(
        num_scalar_prefetch=1,
        grid=(rows,),
        in_specs=[
            pl.BlockSpec((1, picks, size, depth), lambda i, place_ref: (place_ref[0] * rows + i, 0, 0, 0)),
            pl.BlockSpec((1, picks, size, depth), lambda i, place_ref: (i, 0, 0, 0)),
            pl.BlockSpec(memory_space=pltpu.HBM),
        ],
        out_specs=pl.BlockSpec((1, 2 * picks, 2 * size, depth), lambda i, place_ref: (i, 0, 0, 0)),
    )
    return pl.pallas_call(
        split_kernel,
        grid_spec=spec,
        out_shape=jax.ShapeDtypeStruct((rows, 2 * picks, 2 * size, depth), jnp.bfloat16),
        compiler_params=pltpu.CompilerParams(vmem_limit_bytes=VMEM_BYTES),
        name="split_operator",
    )(place, values, other, in_hbm(after))


def apply_kernel(pack, counts, index_ref, parts_ref, *refs):
    sources = refs[: 2 * len(counts)]
    result_ref, token_ref, slots, tiles, held, arrived, landed = refs[-7:]
    row, rows = pl.program_id(0), pl.num_programs(0)
    count, picks, twice, _ = slots.shape
    size = twice // 2
    _, pieces, groups, _, lanes = held.shape
    span = lanes // pack

    def fetch(which):
        slot = lax.rem(which, count)
        return pltpu.make_async_copy(parts_ref.at[which], slots.at[slot], arrived.at[slot])

    def bring(half, part):
        place = held.at[half, :, pl.ds(sum(counts[:part]), counts[part])]
        number = half * len(counts) + part
        return pltpu.make_async_copy(sources[number], place, landed.at[number])

    @pl.when(row == 0)
    def _():
        for half in range(2):
            for part in range(len(counts)):
                bring(half, part).start()
        for ahead in range(min(count - 1, parts_ref.shape[0])):
            fetch(ahead).start()

    @pl.when(row + count - 1 < rows)
    def _():
        fetch(row + count - 1).start()

    @pl.when(row == 0)
    def _():
        token_ref[...] = jnp.zeros_like(token_ref)
        left = lax.broadcasted_iota(jnp.int32, (size, lanes), 1) < span
        for half in range(2):
            for part in range(len(counts)):
                bring(half, part).wait()
            for piece in range(pieces):
                for group in range(groups):
                    tile = held[half, piece, group]
                    high = tile.astype(jnp.bfloat16).astype(jnp.float32)
                    low = tile - high
                    base = ((half * pieces + piece) * groups + group) * pack
                    if pack == 1:
                        tiles[base] = jnp.concatenate([high, low], axis=1).astype(jnp.bfloat16)
                    else:
                        first = jnp.where(left, high, pltpu.roll(low, span, 1))
                        second = jnp.where(left, pltpu.roll(high, span, 1), low)
                        tiles[base] = first.astype(jnp.bfloat16)
                        tiles[base + 1] = second.astype(jnp.bfloat16)

    fetch(row).wait()
    slot = lax.rem(row, count)
    picked = jnp.concatenate([tiles[index_ref[row * picks + k]] for k in range(picks)], axis=0)
    block = jnp.concatenate([slots[slot, k] for k in range(picks)], axis=1)
    product = jnp.dot(block, picked, preferred_element_type=jnp.float32)
    total = product[:size] + product[size:]
    if pack == 1:
        result_ref[0] = total[:, :lanes] + total[:, lanes:]
    else:
        total = total + pltpu.roll(total, span, 1)
        lane = lax.broadcasted_iota(jnp.int32, total.shape, 1)
        result_ref[0] = jnp.where(lane < lax.rem(row, pack) * span, result_ref[0], total)


def apply_operator(parts, index, pack, own, other, after):
    rows, picks, twice, depth = parts.shape
    pieces, _, size, lanes = own[0].shape
    counts = [part.shape[1] for part in own]
    groups = sum(counts)
    spec = pltpu.PrefetchScalarGridSpec(
        num_scalar_prefetch=1,
        grid=(rows,),
        in_specs=[pl.BlockSpec(memory_space=pltpu.HBM)] * (1 + 2 * len(own))
        + [pl.BlockSpec(memory_space=pl.ANY)] * len(after),
        out_specs=[pl.BlockSpec((1, size, lanes), lambda row, *_: (row // pack, 0, 0)), TOKEN_SPEC],
        scratch_shapes=[
            pltpu.VMEM((SLOTS, picks, twice, depth), jnp.bfloat16),
            pltpu.VMEM((2 * pieces * groups * pack, size, 2 * lanes // pack), jnp.bfloat16),
            pltpu.VMEM((2, pieces, groups, size, lanes), jnp.float32),
            pltpu.SemaphoreType.DMA((SLOTS,)),
            pltpu.SemaphoreType.DMA((2 * len(own),)),
        ],
    )

    def kernel(*refs):
        apply_kernel(pack, counts, *refs)

    return pl.pallas_call(
        kernel,
        grid_spec=spec,
        out_shape=[jax.ShapeDtypeStruct((groups, size, lanes), jnp.float32), TOKEN],
        compiler_params=pltpu.CompilerParams(vmem_limit_bytes=VMEM_BYTES),
        cost_estimate=pl.CostEstimate(flops=0, bytes_accessed=own[0].size, transcendentals=0),
        name="apply_operator",
    )(index, *map(in_hbm, (parts, *own, *other)), *after)


def sum_kernel(terms, *refs):
    first_ref, rest_ref, token_ref = refs[-3:]
    count = first_ref.shape[0]
    first_ref[...] = sum(ref[:count] for ref in refs[:terms])
    rest = sum(ref[count:] for ref in refs[:terms])
    for copy in range(rest_ref.shape[0]):
        rest_ref[copy] = rest
    token_ref[...] = jnp.zeros_like(token_ref)


def sum_of(terms, first, copies, after):
    groups, size, lanes = terms[0].shape
    shapes = [(first, size, lanes), (copies, groups - first, size, lanes)]

    def kernel(*refs):
        sum_kernel(len(terms), *refs)

    return pl.pallas_call(
        kernel,
        grid=(1,),
        in_specs=[pl.BlockSpec((groups, size, lanes), lambda i: (0, 0, 0))] * len(terms)
        + [pl.BlockSpec(memory_space=pl.ANY)] * len(after),
        out_specs=[
            pl.BlockSpec(shapes[0], lambda i: (0, 0, 0)),
            pl.BlockSpec(shapes[1], lambda i: (0, 0, 0, 0)),
            TOKEN_SPEC,
        ],
        out_shape=[jax.ShapeDtypeStruct(shape, jnp.float32) for shape in shapes] + [TOKEN],
        compiler_params=pltpu.CompilerParams(vmem_limit_bytes=VMEM_BYTES),
        name="sum_of",
    )(*terms, *after)


def shards(sources, tr_vals, tr_cols, rf_vals, rf_cols):
    source = sources[0, 0, 0]
    piece_rows, columns = source.shape
    size = tr_vals.shape[-1]
    blocks = piece_rows // size
    pack = 2 if blocks % 2 == 0 else 1
    batches, delay = columns // (LANES // pack), DELAY
    length, pieces = lax.axis_size("slab"), lax.axis_size("col")
    last = length - 1
    position = lax.axis_index("slab")
    place = lax.axis_index("row")
    swap = [(0, 1), (1, 0)]
    source = packed_trace(source, batches, pack, size)
    groups = source.shape[1]
    first = groups - groups // FRACTION

    def operator(values, columns, copy_after, split_after):
        half = values.shape[0] // 2
        own = lax.dynamic_slice_in_dim(columns, place * half, half, 0)
        other = lax.dynamic_slice_in_dim(columns, (1 - place) * half, half, 0)
        index = jnp.concatenate([own, lax.ppermute(other, "row", swap) + pieces * blocks], axis=1)
        traded = lax.ppermute(other_half(values, place.reshape(1), copy_after), "row", swap)
        return split_operator(values, traded, place.reshape(1), split_after), index.reshape(-1), pack

    def by_position(choices):
        known = [choice for choice in choices if choice is not None]
        chosen = known[-1]
        for slab, choice in enumerate(choices):
            if choice is not None and choice is not chosen:
                chosen = jnp.where(position == slab, choice, chosen)
        return chosen

    def held(results, batch_of, shift):
        return by_position(
            [
                results[batch_of(slab) + shift(slab)] if 0 <= batch_of(slab) < batches else None
                for slab in range(length)
            ]
        )

    def gather(part, copies):
        own = (lax.all_gather(part, "col", axis=0), lax.all_to_all(copies, "col", 0, 0))
        return own, tuple(lax.ppermute(array, "row", swap) for array in own)

    moments = batches + delay * last
    downs, refls, ups, tokens = [], [], [], []

    def incident_of(moment):
        after = tokens[moment - delay : moment - delay + 1]
        if moment < moments:
            which = jnp.clip(moment - delay * position, 0, batches - 1)
            terms = [lax.dynamic_index_in_dim(source, which, 0, keepdims=False)]
            if moment >= delay:
                terms.append(passed_along(downs[moment - delay], "slab", 1))
        else:
            at = moment - moments
            terms = [held(refls, lambda slab: at - delay * (last - slab), lambda slab: delay * slab)]
            if at >= delay:
                terms.append(passed_along(ups[at - delay], "slab", -1))
        return sum_of(terms, first, pieces, after)

    part, copies, _ = incident_of(0)
    gathered = [gather(part, copies)]
    trans = operator(tr_vals[0, 0, 0], tr_cols[0, 0, 0], part, gathered[0][0][0])
    lag = max(0, min(delay, batches - 2))
    copied_after = part
    for moment in range(2 * moments):
        after = tokens[-1:]
        if moment + 1 < 2 * moments:
            part, copies, token = incident_of(moment + 1)
            gathered.append(gather(part, copies))
            after = after + [token]
        if moment == 0:
            after = after + [in_hbm(gathered[1][0][0])]
        product, token = apply_operator(*trans, *gathered[moment], after)
        (downs if moment < moments else ups).append(product)
        if moment == max(0, lag - 1):
            refl = operator(rf_vals[0, 0, 0], rf_cols[0, 0, 0], copied_after, token)
        if lag <= moment < moments + lag:
            product, token = apply_operator(*refl, *gathered[moment - lag], [token])
            refls.append(product)
        tokens.append(token)
    totals = [
        held(downs, lambda slab: batch, lambda slab: delay * slab)
        + held(ups, lambda slab: batch, lambda slab: delay * (last - slab))
        for batch in range(batches)
    ]
    return unpacked_trace(totals, pack)[None, None, None]


def solution(mesh):
    placed = (
        P("slab", "col", "row", None, None),
        P("slab", "col", "row", None, None, None, None),
        P("slab", "col", "row", None, None),
        P("slab", "col", "row", None, None, None, None),
        P("slab", "col", "row", None, None),
    )
    return jax.shard_map(
        shards,
        mesh=mesh,
        in_specs=placed,
        out_specs=P("slab", "col", "row", None, None),
        check_vma=False,
    )
```

time: 915 us -> 971 us (1.061)
  Pallas kernels: 368 us -> 507 us
  local copies, waits for them, and re-layouts: 127 us -> 22.6 us
  starting transfers between devices: 45.8 us -> 131 us
  waiting for transfers between devices: 345 us -> 282 us
    all_gather x20, waiting for transfers between devices: 195 us -> 44.9 us  [gather(): lax.all_gather(part, 'col', axis=0)]
    all_to_all x0 -> x20, waiting for transfers between devices: none -> 128 us  [gather(): lax.all_to_all(copies, 'col', 0, 0)]
    pallas_call x30, Pallas kernels: 310 us -> 429 us  [apply_operator(): pl.pallas_call(kernel, grid_spec=spec, out_shape=[jax.ShapeDtypeStruct((g...]
    all_to_all x0 -> x20, starting transfers between devices: none -> 91.4 us  [gather(): lax.all_to_all(copies, 'col', 0, 0)]
    unnamed x217 -> x128, local copies, waits for them, and re-layouts: 103 us -> 20.3 us
    ppermute x16, waiting for transfers between devices: 91.9 us -> 65 us  [passed_along(): lax.ppermute(value, axis, [(source, source + steps) for source in range(i...]
    dynamic_slice x5 -> x1, local copies, waits for them, and re-layouts: 21.1 us -> 0.69 us  [operator(): own = lax.dynamic_slice_in_dim(columns, place * half, half, 0)]
    pallas_call x17 -> x23, Pallas kernels: 23.7 us -> 43.5 us  [the longest x20 25.3 us: sum_of(): pl.pallas_call(kernel, grid=(1,), in_specs=[pl.BlockSpec((groups, size, l...]
  transfers between devices with their start and end apart: 60 -> 100, of which waited for: 42 -> 41; matrix products, arithmetic and copies ran while one was open for 6% -> 0% of each run, Pallas kernels for 37% -> 50%
where the time goes in v5:
time: 971 us; the launch traced here: 961 us
  Pallas kernels  507 us (52%)
  waiting for transfers between devices  282 us (29%)
  starting transfers between devices  131 us (13%)
  local copies, waits for them, and re-layouts  22.6 us (2%)
  between operations  15.6 us (2%)
    pallas_call x30, Pallas kernels, apply_operator(): pl.pallas_call(kernel, grid_spec=spec, out_shape=[jax.ShapeDtypeStruct((g...  429 us
    all_to_all x20, waiting for transfers between devices, gather(): lax.all_to_all(copies, 'col', 0, 0)  128 us
    all_to_all x20, starting transfers between devices, gather(): lax.all_to_all(copies, 'col', 0, 0)  91.4 us
    ppermute x16, waiting for transfers between devices, passed_along(): lax.ppermute(value, axis, [(source, source + steps) for source in range(i...  65 us
    all_gather x20, waiting for transfers between devices, gather(): lax.all_gather(part, 'col', axis=0)  44.9 us
    ppermute x40, waiting for transfers between devices, gather(): return (own, tuple((lax.ppermute(array, 'row', swap) for array in own)))  41.5 us
    pallas_call x2, Pallas kernels, split_operator(): pl.pallas_call(split_kernel, grid_spec=spec, out_shape=jax.ShapeDtypeStru...  33.9 us
    ppermute x16, starting transfers between devices, passed_along(): lax.ppermute(value, axis, [(source, source + steps) for source in range(i...  30.8 us
  transfers between devices with their start and end apart: 100, of which 41 were waited for; matrix products, arithmetic and copies ran while one was open for 0% of the time, Pallas kernels for 50%

profile of v5, /device:TPU:0, one launch (start us, length us, event | category | flops | bytes accessed | tf_op | source)
XLA Modules:
  0.0 961.1 jit_solution(17495359074120057942)
XLA Ops:
  34.6 31.9 %all-gather.41.cloned.1.call-done = f32[16,128,128]{2,1,0:T(8,128)} async-done(((f32[4,128,128]{2,1,0:T(8,128)}), f32[16,128,128]{2,1,0:T(8,128)}) %all-gather.41.cloned.1.call-update) | async-done | bytes 1048592 | tf_op jit(solution)/shard_map/all_gather | solution.py:308
  70.0 17.0 %split_operator.2.refs_1_ = bf16[12,24,256,128]{3,2,1,0:T(8,128)(2,1)} custom-call(s32[1]{0:T(128)} %bitcast.2.place_ref, f32[24,12,128,128]{3,2,1,0:T(8,128)} %bitcast.51, f32[12,12,128,128]{3,2,1,0:T(8,128)} %collective-permute-done.1.other_ref, f32[4,4,128,128]{3,2,1,0:T(8,128)} %bitcast.55), custom_call_target="tpu_custom_call" | custom-call | tf_op jit(solution)/shard_map/split_operator/pallas_call | solution.py:127
  134.2 14.2 %apply_operator.31 = (f32[6,128,128]{2,1,0:T(8,128)S(1)}, f32[8,128]{1,0:T(8,128)S(1)}) custom-call(s32[288]{0:T(512)S(1)} %reshape.16.refs_0_, bf16[12,24,256,128]{3,2,1,0:T(8,128)(2,1)} %split_operator.2.refs_1_, f32[4,4,128,128]{3,2,1,0:T(8,128)} %bitcast.60, f32[4,2,128,128]{3,2,1,0:T(8,128)} %all-to-all-done.2.refs_3_, ...), custom_call_target="tpu_custom_call" | custom-call | bytes 262144 | tf_op jit(solution)/shard_map/apply_operator/pallas_call | solution.py:224
  173.8 14.2 %apply_operator.32 = (f32[6,128,128]{2,1,0:T(8,128)S(1)}, f32[8,128]{1,0:T(8,128)S(1)}) custom-call(s32[288]{0:T(512)S(1)} %reshape.16.refs_0_, bf16[12,24,256,128]{3,2,1,0:T(8,128)(2,1)} %split_operator.2.refs_1_, f32[4,4,128,128]{3,2,1,0:T(8,128)} %bitcast.69, f32[4,2,128,128]{3,2,1,0:T(8,128)} %all-to-all-done.1.refs_3_, ...), custom_call_target="tpu_custom_call" | custom-call | bytes 262144 | tf_op jit(solution)/shard_map/apply_operator/pallas_call | solution.py:224
  195.6 16.9 %split_operator.3.refs_1_ = bf16[12,24,256,128]{3,2,1,0:T(8,128)(2,1)} custom-call(s32[1]{0:T(128)} %bitcast.2.place_ref, f32[24,12,128,128]{3,2,1,0:T(8,128)} %bitcast.53, f32[12,12,128,128]{3,2,1,0:T(8,128)} %collective-permute-done.12.other_ref, f32[8,128]{1,0:T(8,128)} %copy-done.34), custom_call_target="tpu_custom_call" | custom-call | tf_op jit(solution)/shard_map/split_operator/pallas_call | solution.py:127
  232.2 14.4 %apply_operator.34 = (f32[6,128,128]{2,1,0:T(8,128)S(1)}, f32[8,128]{1,0:T(8,128)S(1)}) custom-call(s32[288]{0:T(512)S(1)} %reshape.16.refs_0_, bf16[12,24,256,128]{3,2,1,0:T(8,128)(2,1)} %split_operator.2.refs_1_, f32[4,4,128,128]{3,2,1,0:T(8,128)} %bitcast.63, f32[4,2,128,128]{3,2,1,0:T(8,128)} %copy-done.36, ...), custom_call_target="tpu_custom_call" | custom-call | bytes 262144 | tf_op jit(solution)/shard_map/apply_operator/pallas_call | solution.py:224
  273.3 14.4 %apply_operator.36 = (f32[6,128,128]{2,1,0:T(8,128)S(1)}, f32[8,128]{1,0:T(8,128)S(1)}) custom-call(s32[288]{0:T(512)S(1)} %reshape.16.refs_0_, bf16[12,24,256,128]{3,2,1,0:T(8,128)(2,1)} %split_operator.2.refs_1_, f32[4,4,128,128]{3,2,1,0:T(8,128)} %bitcast.72, f32[4,2,128,128]{3,2,1,0:T(8,128)} %copy-done.37, ...), custom_call_target="tpu_custom_call" | custom-call | bytes 262144 | tf_op jit(solution)/shard_map/apply_operator/pallas_call | solution.py:224
  314.5 14.4 %apply_operator.38 = (f32[6,128,128]{2,1,0:T(8,128)S(1)}, f32[8,128]{1,0:T(8,128)S(1)}) custom-call(s32[288]{0:T(512)S(1)} %reshape.16.refs_0_, bf16[12,24,256,128]{3,2,1,0:T(8,128)(2,1)} %split_operator.2.refs_1_, f32[4,4,128,128]{3,2,1,0:T(8,128)} %bitcast.78, f32[4,2,128,128]{3,2,1,0:T(8,128)} %all-to-all-done.6.refs_3_, ...), custom_call_target="tpu_custom_call" | custom-call | bytes 262144 | tf_op jit(solution)/shard_map/apply_operator/pallas_call | solution.py:224
  356.0 14.4 %apply_operator.40 = (f32[6,128,128]{2,1,0:T(8,128)S(1)}, f32[8,128]{1,0:T(8,128)S(1)}) custom-call(s32[288]{0:T(512)S(1)} %reshape.16.refs_0_, bf16[12,24,256,128]{3,2,1,0:T(8,128)(2,1)} %split_operator.2.refs_1_, f32[4,4,128,128]{3,2,1,0:T(8,128)} %bitcast.81, f32[4,2,128,128]{3,2,1,0:T(8,128)} %all-to-all-done.5.refs_3_, ...), custom_call_target="tpu_custom_call" | custom-call | bytes 262144 | tf_op jit(solution)/shard_map/apply_operator/pallas_call | solution.py:224
  397.2 14.4 %apply_operator.42 = (f32[6,128,128]{2,1,0:T(8,128)S(1)}, f32[8,128]{1,0:T(8,128)S(1)}) custom-call(s32[288]{0:T(512)S(1)} %reshape.16.refs_0_, bf16[12,24,256,128]{3,2,1,0:T(8,128)(2,1)} %split_operator.2.refs_1_, f32[4,4,128,128]{3,2,1,0:T(8,128)} %bitcast.84, f32[4,2,128,128]{3,2,1,0:T(8,128)} %all-to-all-done.8.refs_3_, ...), custom_call_target="tpu_custom_call" | custom-call | bytes 262144 | tf_op jit(solution)/shard_map/apply_operator/pallas_call | solution.py:224
  413.6 14.2 %apply_operator.43 = (f32[6,128,128]{2,1,0:T(8,128)S(1)}, f32[8,128]{1,0:T(8,128)S(1)}) custom-call(s32[288]{0:T(512)S(1)} %reshape.18.refs_0_, bf16[12,24,256,128]{3,2,1,0:T(8,128)(2,1)} %split_operator.3.refs_1_, f32[4,4,128,128]{3,2,1,0:T(8,128)} %bitcast.79, f32[4,2,128,128]{3,2,1,0:T(8,128)} %all-to-all-done.6.refs_3_, ...), custom_call_target="tpu_custom_call" | custom-call | bytes 262144 | tf_op jit(solution)/shard_map/apply_operator/pallas_call | solution.py:224
  434.2 26.3 %all-to-all-done.7.refs_3_ = f32[4,2,128,128]{3,2,1,0:T(8,128)S(1)} async-done(((f32[4,2,128,128]{3,2,1,0:T(8,128)}), f32[4,2,128,128]{3,2,1,0:T(8,128)S(1)}, u32[]{:S(2)}, u32[]{:S(2)}) %all-to-all-start.7) | async-done | bytes 524320 | tf_op jit(solution)/shard_map/all_to_all | solution.py:308
  463.3 14.2 %apply_operator.44 = (f32[6,128,128]{2,1,0:T(8,128)S(1)}, f32[8,128]{1,0:T(8,128)S(1)}) custom-call(s32[288]{0:T(512)S(1)} %reshape.16.refs_0_, bf16[12,24,256,128]{3,2,1,0:T(8,128)(2,1)} %split_operator.2.refs_1_, f32[4,4,128,128]{3,2,1,0:T(8,128)} %bitcast.75, f32[4,2,128,128]{3,2,1,0:T(8,128)} %copy-done.39, ...), custom_call_target="tpu_custom_call" | custom-call | bytes 262144 | tf_op jit(solution)/shard_map/apply_operator/pallas_call | solution.py:224
  497.1 27.4 %all-to-all-done.10.refs_3_ = f32[4,2,128,128]{3,2,1,0:T(8,128)S(1)} async-done(((f32[4,2,128,128]{3,2,1,0:T(8,128)}), f32[4,2,128,128]{3,2,1,0:T(8,128)S(1)}, u32[]{:S(2)}, u32[]{:S(2)}) %all-to-all-start.10) | async-done | bytes 524320 | tf_op jit(solution)/shard_map/all_to_all | solution.py:308
  563.4 14.4 %apply_operator.48 = (f32[6,128,128]{2,1,0:T(8,128)S(1)}, f32[8,128]{1,0:T(8,128)S(1)}) custom-call(s32[288]{0:T(512)S(1)} %reshape.16.refs_0_, bf16[12,24,256,128]{3,2,1,0:T(8,128)(2,1)} %split_operator.2.refs_1_, f32[4,4,128,128]{3,2,1,0:T(8,128)} %bitcast.101, f32[4,2,128,128]{3,2,1,0:T(8,128)} %all-to-all-done.9.refs_3_, ...), custom_call_target="tpu_custom_call" | custom-call | bytes 262144 | tf_op jit(solution)/shard_map/apply_operator/pallas_call | solution.py:224
  605.0 15.2 %apply_operator.50 = (f32[6,128,128]{2,1,0:T(8,128)}, f32[8,128]{1,0:T(8,128)S(1)}) custom-call(s32[288]{0:T(512)S(1)} %reshape.16.refs_0_, bf16[12,24,256,128]{3,2,1,0:T(8,128)(2,1)} %split_operator.2.refs_1_, f32[4,4,128,128]{3,2,1,0:T(8,128)} %bitcast.89, f32[4,2,128,128]{3,2,1,0:T(8,128)} %all-to-all-done.12.refs_3_, ...), custom_call_target="tpu_custom_call" | custom-call | bytes 262144 | tf_op jit(solution)/shard_map/apply_operator/pallas_call | solution.py:224
  648.0 15.0 %apply_operator.52 = (f32[6,128,128]{2,1,0:T(8,128)}, f32[8,128]{1,0:T(8,128)S(1)}) custom-call(s32[288]{0:T(512)S(1)} %reshape.16.refs_0_, bf16[12,24,256,128]{3,2,1,0:T(8,128)(2,1)} %split_operator.2.refs_1_, f32[4,4,128,128]{3,2,1,0:T(8,128)} %bitcast.93, f32[4,2,128,128]{3,2,1,0:T(8,128)} %all-to-all-done.11.refs_3_, ...), custom_call_target="tpu_custom_call" | custom-call | bytes 262144 | tf_op jit(solution)/shard_map/apply_operator/pallas_call | solution.py:224
  689.8 14.2 %apply_operator.53 = (f32[6,128,128]{2,1,0:T(8,128)S(1)}, f32[8,128]{1,0:T(8,128)S(1)}) custom-call(s32[288]{0:T(512)S(1)} %reshape.16.refs_0_, bf16[12,24,256,128]{3,2,1,0:T(8,128)(2,1)} %split_operator.2.refs_1_, f32[4,4,128,128]{3,2,1,0:T(8,128)} %bitcast.95, f32[4,2,128,128]{3,2,1,0:T(8,128)} %all-to-all-done.14.refs_3_, ...), custom_call_target="tpu_custom_call" | custom-call | bytes 262144 | tf_op jit(solution)/shard_map/apply_operator/pallas_call | solution.py:224
  727.5 14.2 %apply_operator.54 = (f32[6,128,128]{2,1,0:T(8,128)S(1)}, f32[8,128]{1,0:T(8,128)S(1)}) custom-call(s32[288]{0:T(512)S(1)} %reshape.16.refs_0_, bf16[12,24,256,128]{3,2,1,0:T(8,128)(2,1)} %split_operator.2.refs_1_, f32[4,4,128,128]{3,2,1,0:T(8,128)} %bitcast.97, f32[4,2,128,128]{3,2,1,0:T(8,128)} %all-to-all-done.13.refs_3_, ...), custom_call_target="tpu_custom_call" | custom-call | bytes 262144 | tf_op jit(solution)/shard_map/apply_operator/pallas_call | solution.py:224
  765.2 14.2 %apply_operator.55 = (f32[6,128,128]{2,1,0:T(8,128)S(1)}, f32[8,128]{1,0:T(8,128)S(1)}) custom-call(s32[288]{0:T(512)S(1)} %reshape.16.refs_0_, bf16[12,24,256,128]{3,2,1,0:T(8,128)(2,1)} %split_operator.2.refs_1_, f32[4,4,128,128]{3,2,1,0:T(8,128)} %bitcast.103, f32[4,2,128,128]{3,2,1,0:T(8,128)} %all-to-all-done.16.refs_3_, ...), custom_call_target="tpu_custom_call" | custom-call | bytes 262144 | tf_op jit(solution)/shard_map/apply_operator/pallas_call | solution.py:224
  803.0 14.3 %apply_operator.56 = (f32[6,128,128]{2,1,0:T(8,128)S(1)}, f32[8,128]{1,0:T(8,128)S(1)}) custom-call(s32[288]{0:T(512)S(1)} %reshape.16.refs_0_, bf16[12,24,256,128]{3,2,1,0:T(8,128)(2,1)} %split_operator.2.refs_1_, f32[4,4,128,128]{3,2,1,0:T(8,128)} %bitcast.105, f32[4,2,128,128]{3,2,1,0:T(8,128)} %all-to-all-done.15.refs_3_, ...), custom_call_target="tpu_custom_call" | custom-call | bytes 262144 | tf_op jit(solution)/shard_map/apply_operator/pallas_call | solution.py:224
  840.8 14.3 %apply_operator.57 = (f32[6,128,128]{2,1,0:T(8,128)S(1)}, f32[8,128]{1,0:T(8,128)S(1)}) custom-call(s32[288]{0:T(512)S(1)} %reshape.16.refs_0_, bf16[12,24,256,128]{3,2,1,0:T(8,128)(2,1)} %split_operator.2.refs_1_, f32[4,4,128,128]{3,2,1,0:T(8,128)} %bitcast.99, f32[4,2,128,128]{3,2,1,0:T(8,128)} %all-to-all-done.17.refs_3_, ...), custom_call_target="tpu_custom_call" | custom-call | bytes 262144 | tf_op jit(solution)/shard_map/apply_operator/pallas_call | solution.py:224
  876.3 25.1 %all-to-all-done.18.refs_3_ = f32[4,2,128,128]{3,2,1,0:T(8,128)} async-done(((f32[4,2,128,128]{3,2,1,0:T(8,128)}), f32[4,2,128,128]{3,2,1,0:T(8,128)}, u32[]{:S(2)}, u32[]{:S(2)}) %all-to-all-start.18) | async-done | bytes 524320 | tf_op jit(solution)/shard_map/all_to_all | solution.py:308
  935.3 14.4 %apply_operator.59 = (f32[6,128,128]{2,1,0:T(8,128)S(1)}, f32[8,128]{1,0:T(8,128)}) custom-call(s32[288]{0:T(512)S(1)} %reshape.16.refs_0_, bf16[12,24,256,128]{3,2,1,0:T(8,128)(2,1)} %split_operator.2.refs_1_, f32[4,4,128,128]{3,2,1,0:T(8,128)} %bitcast.87, f32[4,2,128,128]{3,2,1,0:T(8,128)} %all-to-all-done.19.refs_3_, ...), custom_call_target="tpu_custom_call" | custom-call | bytes 262144 | tf_op jit(solution)/shard_map/apply_operator/pallas_call | solution.py:224
  (394 shorter events, 541.7 us)
Async XLA Ops:
  6.5 60.0 %all-gather.41.cloned.1.call-start = ((), (), s32[]{:S(2)}) async-start(), calls=%async_computation.20 | async-start | bytes 1310720 | tf_op jit(solution)/shard_map/all_gather | solution.py:308
  19.0 51.1 %collective-permute-start.1 = (f32[12,12,128,128]{3,2,1,0:T(8,128)}, f32[12,12,128,128]{3,2,1,0:T(8,128)}, u32[]{:S(2)}, u32[]{:S(2)}) collective-permute-start(f32[12,12,128,128]{3,2,1,0:T(8,128)} %other_half.2), channel_id=1, source_target_pairs={{0,4},{4,0},{1,5},{5,1},{2,6},{6,2},{3,7},{7,3},{8,12},{12,8},{9,1... | collective-permute-start | bytes 28311560 | tf_op jit(solution)/shard_map/ppermute | solution.py:288
  27.2 168.4 %collective-permute-start.12 = (f32[12,12,128,128]{3,2,1,0:T(8,128)}, f32[12,12,128,128]{3,2,1,0:T(8,128)}, u32[]{:S(2)}, u32[]{:S(2)}) collective-permute-start(f32[12,12,128,128]{3,2,1,0:T(8,128)} %other_half.3), channel_id=1, source_target_pairs={{0,4},{4,0},{1,5},{5,1},{2,6},{6,2},{3,7},{7,3},{8,12},{12,8},{9,1... | collective-permute-start | bytes 28311560 | tf_op jit(solution)/shard_map/ppermute | solution.py:288
  27.3 67.9 %all-gather.43.cloned.1.call-start = ((), (), s32[]{:S(2)}) async-start(), calls=%async_computation.21 | async-start | bytes 1310720 | tf_op jit(solution)/shard_map/all_gather | solution.py:308
  116.9 44.6 %all-gather.45.cloned.1.call-start = ((), (), s32[]{:S(2)}) async-start(), calls=%async_computation.22 | async-start | bytes 1310720 | tf_op jit(solution)/shard_map/all_gather | solution.py:308
  156.0 71.8 %all-gather.49.cloned.1.call-start = ((), (), s32[]{:S(2)}) async-start(), calls=%async_computation.24 | async-start | bytes 1310720 | tf_op jit(solution)/shard_map/all_gather | solution.py:308
  188.0 38.7 %collective-permute-start.10 = (f32[6,128,128]{2,1,0:T(8,128)S(1)}, f32[6,128,128]{2,1,0:T(8,128)S(1)}, u32[]{:S(2)}, u32[]{:S(2)}) collective-permute-start(f32[6,128,128]{2,1,0:T(8,128)S(1)} %get-tuple-element.136), channel_id=1, source_target_pairs={{0,8},{8,16},{16,24},{1,9},{9,17},{17,25},{2,10},{10,18},{18,26},{... | collective-permute-start | bytes 1179656 | tf_op jit(solution)/shard_map/ppermute | solution.py:24
  195.1 73.8 %all-gather.47.cloned.1.call-start = ((), (), s32[]{:S(2)}) async-start(), calls=%async_computation.23 | async-start | bytes 1310720 | tf_op jit(solution)/shard_map/all_gather | solution.py:308
  253.7 56.2 %all-gather.53.cloned.1.call-start = ((), (), s32[]{:S(2)}) async-start(), calls=%async_computation.26 | async-start | bytes 1310720 | tf_op jit(solution)/shard_map/all_gather | solution.py:308
  294.8 56.7 %all-gather.51.cloned.1.call-start = ((), (), s32[]{:S(2)}) async-start(), calls=%async_computation.25 | async-start | bytes 1310720 | tf_op jit(solution)/shard_map/all_gather | solution.py:308
  336.3 56.4 %all-gather.57.cloned.1.call-start = ((), (), s32[]{:S(2)}) async-start(), calls=%async_computation.28 | async-start | bytes 1310720 | tf_op jit(solution)/shard_map/all_gather | solution.py:308
  377.5 56.7 %all-gather.55.cloned.1.call-start = ((), (), s32[]{:S(2)}) async-start(), calls=%async_computation.27 | async-start | bytes 1310720 | tf_op jit(solution)/shard_map/all_gather | solution.py:308
  392.7 104.2 %all-gather.61.cloned.1.call-start = ((), (), s32[]{:S(2)}) async-start(), calls=%async_computation.30 | async-start | bytes 1310720 | tf_op jit(solution)/shard_map/all_gather | solution.py:308
  434.0 124.9 %all-gather.59.cloned.1.call-start = ((), (), s32[]{:S(2)}) async-start(), calls=%async_computation.29 | async-start | bytes 1310720 | tf_op jit(solution)/shard_map/all_gather | solution.py:308
  528.7 71.9 %all-gather.65.cloned.1.call-start = ((), (), s32[]{:S(2)}) async-start(), calls=%async_computation.32 | async-start | bytes 1310720 | tf_op jit(solution)/shard_map/all_gather | solution.py:308
  584.1 59.5 %all-gather.63.cloned.1.call-start = ((), (), s32[]{:S(2)}) async-start(), calls=%async_computation.31 | async-start | bytes 1310720 | tf_op jit(solution)/shard_map/all_gather | solution.py:308
  626.7 53.4 %all-gather.69.cloned.1.call-start = ((), (), s32[]{:S(2)}) async-start(), calls=%async_computation.34 | async-start | bytes 1310720 | tf_op jit(solution)/shard_map/all_gather | solution.py:308
  669.4 49.8 %all-gather.67.cloned.1.call-start = ((), (), s32[]{:S(2)}) async-start(), calls=%async_computation.33 | async-start | bytes 1310720 | tf_op jit(solution)/shard_map/all_gather | solution.py:308
  709.5 48.7 %all-gather.73.cloned.1.call-start = ((), (), s32[]{:S(2)}) async-start(), calls=%async_computation.36 | async-start | bytes 1310720 | tf_op jit(solution)/shard_map/all_gather | solution.py:308
  747.2 49.3 %all-gather.71.cloned.1.call-start = ((), (), s32[]{:S(2)}) async-start(), calls=%async_computation.35 | async-start | bytes 1310720 | tf_op jit(solution)/shard_map/all_gather | solution.py:308
  784.9 49.9 %all-gather.75.cloned.1.call-start = ((), (), s32[]{:S(2)}) async-start(), calls=%async_computation.37 | async-start | bytes 1310720 | tf_op jit(solution)/shard_map/all_gather | solution.py:308
  822.8 53.4 %all-gather.77.cloned.1.call-start = ((), (), s32[]{:S(2)}) async-start(), calls=%async_computation.38 | async-start | bytes 1310720 | tf_op jit(solution)/shard_map/all_gather | solution.py:308
  834.8 75.6 %all-gather.79.cloned.1.call-start = ((), (), s32[]{:S(2)}) async-start(), calls=%async_computation.39 | async-start | bytes 1310720 | tf_op jit(solution)/shard_map/all_gather | solution.py:308
  876.2 42.7 %collective-permute-start.55 = (f32[4,4,128,128]{3,2,1,0:T(8,128)}, f32[4,4,128,128]{3,2,1,0:T(8,128)}, u32[]{:S(2)}, u32[]{:S(2)}) collective-permute-start(f32[4,4,128,128]{3,2,1,0:T(8,128)} %bitcast.90), channel_id=1, source_target_pairs={{0,4},{4,0},{1,5},{5,1},{2,6},{6,2},{3,7},{7,3},{8,12},{12,8},{9,1... | collective-permute-start | bytes 3145736 | tf_op jit(solution)/shard_map/ppermute | solution.py:309
  (138 other events, 1675.9 us)
Sparse Core Ops, SparseCore 0:
  27.4 39.0 all-gather.40
  68.1 27.0 all-gather.42
  122.0 28.7 all-gather.44
  161.5 27.9 all-gather.48
  227.9 27.4 all-gather.46
  269.1 27.5 all-gather.52
  310.1 27.5 all-gather.50
  351.6 27.5 all-gather.56
  392.8 27.5 all-gather.54
  429.0 36.6 all-gather.60
  493.5 35.5 all-gather.58
  558.9 27.4 all-gather.64
  600.7 29.5 all-gather.62
  643.6 36.2 all-gather.68
  681.4 29.0 all-gather.66
  719.3 27.7 all-gather.72
  758.2 27.8 all-gather.70
  796.6 27.9 all-gather.74
  834.9 28.0 all-gather.76
  872.1 38.2 all-gather.78

commit v6 on v5

--- a/solution.py
+++ b/solution.py
@@ -8,7 +8,6 @@
 LANES = 128
 DELAY = 2
 SLOTS = 8
-FRACTION = 3
 VMEM_BYTES = 44 * 2**20
 TOKEN = jax.ShapeDtypeStruct((8, LANES), jnp.float32)
 TOKEN_SPEC = pl.BlockSpec(TOKEN.shape, lambda *_: (0, 0))
@@ -133,29 +132,20 @@
     )(place, values, other, in_hbm(after))
 
 
-def apply_kernel(pack, counts, index_ref, parts_ref, *refs):
-    sources = refs[: 2 * len(counts)]
-    result_ref, token_ref, slots, tiles, held, arrived, landed = refs[-7:]
+def apply_kernel(pack, index_ref, parts_ref, gathered_ref, *refs):
+    result_ref, token_ref, slots, tiles, arrived = refs[-5:]
     row, rows = pl.program_id(0), pl.num_programs(0)
     count, picks, twice, _ = slots.shape
     size = twice // 2
-    _, pieces, groups, _, lanes = held.shape
+    pieces, halves, groups, _, lanes = gathered_ref.shape
     span = lanes // pack
 
     def fetch(which):
         slot = lax.rem(which, count)
         return pltpu.make_async_copy(parts_ref.at[which], slots.at[slot], arrived.at[slot])
 
-    def bring(half, part):
-        place = held.at[half, :, pl.ds(sum(counts[:part]), counts[part])]
-        number = half * len(counts) + part
-        return pltpu.make_async_copy(sources[number], place, landed.at[number])
-
     @pl.when(row == 0)
     def _():
-        for half in range(2):
-            for part in range(len(counts)):
-                bring(half, part).start()
         for ahead in range(min(count - 1, parts_ref.shape[0])):
             fetch(ahead).start()
 
@@ -166,23 +156,25 @@
     @pl.when(row == 0)
     def _():
         token_ref[...] = jnp.zeros_like(token_ref)
-        left = lax.broadcasted_iota(jnp.int32, (size, lanes), 1) < span
-        for half in range(2):
-            for part in range(len(counts)):
-                bring(half, part).wait()
+        lane = lax.broadcasted_iota(jnp.int32, (size, lanes), 1)
+        left = lane < lanes // 2
+        masks = [lane // span % max(1, pack // 2) == q for q in range(pack // 2)]
+        for half in range(halves):
             for piece in range(pieces):
                 for group in range(groups):
-                    tile = held[half, piece, group]
+                    tile = gathered_ref[piece, half, group]
                     high = tile.astype(jnp.bfloat16).astype(jnp.float32)
                     low = tile - high
                     base = ((half * pieces + piece) * groups + group) * pack
                     if pack == 1:
                         tiles[base] = jnp.concatenate([high, low], axis=1).astype(jnp.bfloat16)
-                    else:
-                        first = jnp.where(left, high, pltpu.roll(low, span, 1))
-                        second = jnp.where(left, pltpu.roll(high, span, 1), low)
-                        tiles[base] = first.astype(jnp.bfloat16)
-                        tiles[base + 1] = second.astype(jnp.bfloat16)
+                        continue
+                    first = jnp.where(left, high, pltpu.roll(low, lanes // 2, 1))
+                    second = jnp.where(left, pltpu.roll(high, lanes // 2, 1), low)
+                    for start, both in ((base, first), (base + pack // 2, second)):
+                        for q, mask in enumerate(masks):
+                            alone = both if pack == 2 else jnp.where(mask, both, 0.0)
+                            tiles[start + q] = alone.astype(jnp.bfloat16)
 
     fetch(row).wait()
     slot = lax.rem(row, count)
@@ -193,57 +185,55 @@
     if pack == 1:
         result_ref[0] = total[:, :lanes] + total[:, lanes:]
     else:
-        total = total + pltpu.roll(total, span, 1)
+        shift = span
+        while shift < lanes:
+            total = total + pltpu.roll(total, shift, 1)
+            shift *= 2
         lane = lax.broadcasted_iota(jnp.int32, total.shape, 1)
         result_ref[0] = jnp.where(lane < lax.rem(row, pack) * span, result_ref[0], total)
 
 
-def apply_operator(parts, index, pack, own, other, after):
+def apply_operator(parts, index, pack, gathered, after):
     rows, picks, twice, depth = parts.shape
-    pieces, _, size, lanes = own[0].shape
-    counts = [part.shape[1] for part in own]
-    groups = sum(counts)
+    pieces, halves, groups, size, lanes = gathered.shape
     spec = pltpu.PrefetchScalarGridSpec(
         num_scalar_prefetch=1,
         grid=(rows,),
-        in_specs=[pl.BlockSpec(memory_space=pltpu.HBM)] * (1 + 2 * len(own))
+        in_specs=[
+            pl.BlockSpec(memory_space=pltpu.HBM),
+            pl.BlockSpec(gathered.shape, lambda row, *_: (0, 0, 0, 0, 0)),
+        ]
         + [pl.BlockSpec(memory_space=pl.ANY)] * len(after),
         out_specs=[pl.BlockSpec((1, size, lanes), lambda row, *_: (row // pack, 0, 0)), TOKEN_SPEC],
         scratch_shapes=[
             pltpu.VMEM((SLOTS, picks, twice, depth), jnp.bfloat16),
-            pltpu.VMEM((2 * pieces * groups * pack, size, 2 * lanes // pack), jnp.bfloat16),
-            pltpu.VMEM((2, pieces, groups, size, lanes), jnp.float32),
+            pltpu.VMEM((halves * pieces * groups * pack, size, lanes * (2 if pack == 1 else 1)), jnp.bfloat16),
             pltpu.SemaphoreType.DMA((SLOTS,)),
-            pltpu.SemaphoreType.DMA((2 * len(own),)),
         ],
     )
 
     def kernel(*refs):
-        apply_kernel(pack, counts, *refs)
+        apply_kernel(pack, *refs)
 
     return pl.pallas_call(
         kernel,
         grid_spec=spec,
         out_shape=[jax.ShapeDtypeStruct((groups, size, lanes), jnp.float32), TOKEN],
         compiler_params=pltpu.CompilerParams(vmem_limit_bytes=VMEM_BYTES),
-        cost_estimate=pl.CostEstimate(flops=0, bytes_accessed=own[0].size, transcendentals=0),
+        cost_estimate=pl.CostEstimate(flops=0, bytes_accessed=gathered.size, transcendentals=0),
         name="apply_operator",
-    )(index, *map(in_hbm, (parts, *own, *other)), *after)
+    )(index, in_hbm(parts), in_hbm(gathered), *after)
 
 
 def sum_kernel(terms, *refs):
-    first_ref, rest_ref, token_ref = refs[-3:]
-    count = first_ref.shape[0]
-    first_ref[...] = sum(ref[:count] for ref in refs[:terms])
-    rest = sum(ref[count:] for ref in refs[:terms])
-    for copy in range(rest_ref.shape[0]):
-        rest_ref[copy] = rest
+    total_ref, token_ref = refs[-2:]
+    total_ref[...] = sum(ref[...] for ref in refs[:terms])
     token_ref[...] = jnp.zeros_like(token_ref)
 
 
-def sum_of(terms, first, copies, after):
-    groups, size, lanes = terms[0].shape
-    shapes = [(first, size, lanes), (copies, groups - first, size, lanes)]
+def sum_of(terms, after):
+    shape = terms[0].shape
+    whole = pl.BlockSpec(shape, lambda i: (0, 0, 0))
 
     def kernel(*refs):
         sum_kernel(len(terms), *refs)
@@ -251,14 +241,9 @@
     return pl.pallas_call(
         kernel,
         grid=(1,),
-        in_specs=[pl.BlockSpec((groups, size, lanes), lambda i: (0, 0, 0))] * len(terms)
-        + [pl.BlockSpec(memory_space=pl.ANY)] * len(after),
-        out_specs=[
-            pl.BlockSpec(shapes[0], lambda i: (0, 0, 0)),
-            pl.BlockSpec(shapes[1], lambda i: (0, 0, 0, 0)),
-            TOKEN_SPEC,
-        ],
-        out_shape=[jax.ShapeDtypeStruct(shape, jnp.float32) for shape in shapes] + [TOKEN],
+        in_specs=[whole] * len(terms) + [pl.BlockSpec(memory_space=pl.ANY)] * len(after),
+        out_specs=[whole, TOKEN_SPEC],
+        out_shape=[jax.ShapeDtypeStruct(shape, jnp.float32), TOKEN],
         compiler_params=pltpu.CompilerParams(vmem_limit_bytes=VMEM_BYTES),
         name="sum_of",
     )(*terms, *after)
@@ -269,7 +254,7 @@
     piece_rows, columns = source.shape
     size = tr_vals.shape[-1]
     blocks = piece_rows // size
-    pack = 2 if blocks % 2 == 0 else 1
+    pack = 4 if blocks % 4 == 0 else 1
     batches, delay = columns // (LANES // pack), DELAY
     length, pieces = lax.axis_size("slab"), lax.axis_size("col")
     last = length - 1
@@ -277,14 +262,14 @@
     place = lax.axis_index("row")
     swap = [(0, 1), (1, 0)]
     source = packed_trace(source, batches, pack, size)
-    groups = source.shape[1]
-    first = groups - groups // FRACTION
 
     def operator(values, columns, copy_after, split_after):
         half = values.shape[0] // 2
         own = lax.dynamic_slice_in_dim(columns, place * half, half, 0)
         other = lax.dynamic_slice_in_dim(columns, (1 - place) * half, half, 0)
-        index = jnp.concatenate([own, lax.ppermute(other, "row", swap) + pieces * blocks], axis=1)
+        group_blocks = pieces * blocks
+        other = lax.ppermute(other, "row", swap) + (1 - place) * group_blocks
+        index = jnp.concatenate([own + place * group_blocks, other], axis=1)
         traded = lax.ppermute(other_half(values, place.reshape(1), copy_after), "row", swap)
         return split_operator(values, traded, place.reshape(1), split_after), index.reshape(-1), pack
 
@@ -304,9 +289,9 @@
             ]
         )
 
-    def gather(part, copies):
-        own = (lax.all_gather(part, "col", axis=0), lax.all_to_all(copies, "col", 0, 0))
-        return own, tuple(lax.ppermute(array, "row", swap) for array in own)
+    def gather(piece):
+        gathered = lax.all_gather(piece, ("col", "row"), axis=0)
+        return gathered.reshape((pieces, 2) + piece.shape)
 
     moments = batches + delay * last
     downs, refls, ups, tokens = [], [], [], []
@@ -323,27 +308,27 @@
             terms = [held(refls, lambda slab: at - delay * (last - slab), lambda slab: delay * slab)]
             if at >= delay:
                 terms.append(passed_along(ups[at - delay], "slab", -1))
-        return sum_of(terms, first, pieces, after)
-
-    part, copies, _ = incident_of(0)
-    gathered = [gather(part, copies)]
-    trans = operator(tr_vals[0, 0, 0], tr_cols[0, 0, 0], part, gathered[0][0][0])
+        return sum_of(terms, after)
+
+    piece, _ = incident_of(0)
+    gathered = [gather(piece)]
+    trans = operator(tr_vals[0, 0, 0], tr_cols[0, 0, 0], piece, gathered[0])
     lag = max(0, min(delay, batches - 2))
-    copied_after = part
+    copied_after = piece
     for moment in range(2 * moments):
         after = tokens[-1:]
         if moment + 1 < 2 * moments:
-            part, copies, token = incident_of(moment + 1)
-            gathered.append(gather(part, copies))
+            piece, token = incident_of(moment + 1)
+            gathered.append(gather(piece))
             after = after + [token]
         if moment == 0:
-            after = after + [in_hbm(gathered[1][0][0])]
-        product, token = apply_operator(*trans, *gathered[moment], after)
+            after = after + [in_hbm(gathered[1])]
+        product, token = apply_operator(*trans, gathered[moment], after)
         (downs if moment < moments else ups).append(product)
         if moment == max(0, lag - 1):
             refl = operator(rf_vals[0, 0, 0], rf_cols[0, 0, 0], copied_after, token)
         if lag <= moment < moments + lag:
-            product, token = apply_operator(*refl, *gathered[moment - lag], [token])
+            product, token = apply_operator(*refl, gathered[moment - lag], [token])
             refls.append(product)
         tokens.append(token)
     totals = [

time: 971 us -> 858 us (0.88)
  waiting for transfers between devices: 282 us -> 184 us
  starting transfers between devices: 131 us -> 50.1 us
  Pallas kernels: 507 us -> 587 us
  local copies, waits for them, and re-layouts: 22.6 us -> 10.4 us
    all_to_all x20 -> x0, waiting for transfers between devices: 128 us -> none  [gather(): lax.all_to_all(copies, 'col', 0, 0)]
    all_to_all x20 -> x0, starting transfers between devices: 91.4 us -> none  [gather(): lax.all_to_all(copies, 'col', 0, 0)]
    pallas_call x30 -> x42, Pallas kernels: 429 us -> 515 us  [apply_operator(): pl.pallas_call(kernel, grid_spec=spec, out_shape=[jax.ShapeDtypeStruct((g...]
    ppermute x42 -> x2, waiting for transfers between devices: 43.4 us -> 4.74 us  [operator(): other = lax.ppermute(other, 'row', swap) + (1 - place) * group_blocks]
    all_gather x20 -> x28, waiting for transfers between devices: 44.9 us -> 82.2 us  [gather(): gathered = lax.all_gather(piece, ('col', 'row'), axis=0)]
    ppermute x16 -> x24, waiting for transfers between devices: 65 us -> 96.1 us  [passed_along(): lax.ppermute(value, axis, [(source, source + steps) for source in range(i...]
    ppermute x16 -> x24, starting transfers between devices: 30.8 us -> 46.6 us  [passed_along(): lax.ppermute(value, axis, [(source, source + steps) for source in range(i...]
    unnamed x128 -> x95, local copies, waits for them, and re-layouts: 20.3 us -> 8.92 us
  transfers between devices with their start and end apart: 100 -> 56, of which waited for: 41 -> 29; matrix products, arithmetic and copies ran while one was open for 0% -> 0% of each run, Pallas kernels for 50% -> 66%
where the time goes in v6:
time: 858 us; the launch traced here: 848 us
  Pallas kernels  587 us (68%)
  waiting for transfers between devices  184 us (21%)
  starting transfers between devices  50.1 us (6%)
  between operations  15.6 us (2%)
  local copies, waits for them, and re-layouts  10.4 us (1%)
    pallas_call x42, Pallas kernels, apply_operator(): pl.pallas_call(kernel, grid_spec=spec, out_shape=[jax.ShapeDtypeStruct((g...  515 us
    ppermute x24, waiting for transfers between devices, passed_along(): lax.ppermute(value, axis, [(source, source + steps) for source in range(i...  96.1 us
    all_gather x28, waiting for transfers between devices, gather(): gathered = lax.all_gather(piece, ('col', 'row'), axis=0)  82.2 us
    ppermute x24, starting transfers between devices, passed_along(): lax.ppermute(value, axis, [(source, source + steps) for source in range(i...  46.6 us
    pallas_call x2, Pallas kernels, split_operator(): pl.pallas_call(split_kernel, grid_spec=spec, out_shape=jax.ShapeDtypeStru...  33.9 us
    pallas_call x28, Pallas kernels, sum_of(): pl.pallas_call(kernel, grid=(1,), in_specs=[whole] * len(terms) + [pl.Blo...  19 us
  transfers between devices with their start and end apart: 56, of which 29 were waited for; matrix products, arithmetic and copies ran while one was open for 0% of the time, Pallas kernels for 66%

profile of v6, /device:TPU:0, one launch (start us, length us, event | category | flops | bytes accessed | tf_op | source)
XLA Modules:
  0.0 847.6 jit_solution(9974496133562220044)
XLA Ops:
  33.9 14.6 %all-gather.57.cloned.1.call-done = f32[24,128,128]{2,1,0:T(8,128)} async-done(((f32[3,128,128]{2,1,0:T(8,128)}), f32[24,128,128]{2,1,0:T(8,128)}) %all-gather.57.cloned.1.call-update) | async-done | bytes 1572880 | tf_op jit(solution)/shard_map/all_gather | solution.py:293
  48.6 17.0 %split_operator.2.refs_1_ = bf16[12,24,256,128]{3,2,1,0:T(8,128)(2,1)} custom-call(s32[1]{0:T(128)} %bitcast.1.place_ref, f32[24,12,128,128]{3,2,1,0:T(8,128)} %bitcast.74, f32[12,12,128,128]{3,2,1,0:T(8,128)} %collective-permute-done.1.other_ref, f32[4,2,3,128,128]{4,3,2,1,0:T(8,128)} %bitcast.77), custom_call_target="tpu_custom_call" | custom-call | tf_op jit(solution)/shard_map/split_operator/pallas_call | solution.py:126
  65.6 12.3 %all-gather.59.cloned.1.call-done = f32[24,128,128]{2,1,0:T(8,128)} async-done(((f32[3,128,128]{2,1,0:T(8,128)}), f32[24,128,128]{2,1,0:T(8,128)}) %all-gather.59.cloned.1.call-update) | async-done | bytes 1572880 | tf_op jit(solution)/shard_map/all_gather | solution.py:293
  140.3 16.9 %split_operator.3.refs_1_ = bf16[12,24,256,128]{3,2,1,0:T(8,128)(2,1)} custom-call(s32[1]{0:T(128)} %bitcast.1.place_ref, f32[24,12,128,128]{3,2,1,0:T(8,128)} %bitcast.76, f32[12,12,128,128]{3,2,1,0:T(8,128)} %collective-permute-done.6.other_ref, f32[8,128]{1,0:T(8,128)} %copy-done.43), custom_call_target="tpu_custom_call" | custom-call | tf_op jit(solution)/shard_map/split_operator/pallas_call | solution.py:126
  186.0 12.3 %apply_operator.47 = (f32[3,128,128]{2,1,0:T(8,128)S(1)}, f32[8,128]{1,0:T(8,128)S(1)}) custom-call(s32[288]{0:T(512)S(1)} %reshape.109.refs_0_, bf16[12,24,256,128]{3,2,1,0:T(8,128)(2,1)} %split_operator.3.refs_1_, f32[4,2,3,128,128]{4,3,2,1,0:T(8,128)} %bitcast.82, f32[8,128]{1,0:T(8,128)S(1)} %get-tuple-element.159.refs_3_), custom_call_target="tpu_custom_call" | custom-call | bytes 393216 | tf_op jit(solution)/shard_map/apply_operator/pallas_call | solution.py:218
  199.3 12.2 %apply_operator.48 = (f32[3,128,128]{2,1,0:T(8,128)S(1)}, f32[8,128]{1,0:T(8,128)S(1)}) custom-call(s32[288]{0:T(512)S(1)} %reshape.104.refs_0_, bf16[12,24,256,128]{3,2,1,0:T(8,128)(2,1)} %split_operator.2.refs_1_, f32[4,2,3,128,128]{4,3,2,1,0:T(8,128)} %bitcast.89, f32[8,128]{1,0:T(8,128)S(1)} %get-tuple-element.160.refs_2_.refs_3_, ...), custom_call_target="tpu_custom_call" | custom-call | bytes 393216 | tf_op jit(solution)/shard_map/apply_operator/pallas_call | solution.py:218
  214.9 12.3 %apply_operator.49 = (f32[3,128,128]{2,1,0:T(8,128)S(1)}, f32[8,128]{1,0:T(8,128)S(1)}) custom-call(s32[288]{0:T(512)S(1)} %reshape.109.refs_0_, bf16[12,24,256,128]{3,2,1,0:T(8,128)(2,1)} %split_operator.3.refs_1_, f32[4,2,3,128,128]{4,3,2,1,0:T(8,128)} %bitcast.86, f32[8,128]{1,0:T(8,128)S(1)} %get-tuple-element.164.refs_3_), custom_call_target="tpu_custom_call" | custom-call | bytes 393216 | tf_op jit(solution)/shard_map/apply_operator/pallas_call | solution.py:218
  242.1 12.3 %apply_operator.51 = (f32[3,128,128]{2,1,0:T(8,128)S(1)}, f32[8,128]{1,0:T(8,128)S(1)}) custom-call(s32[288]{0:T(512)S(1)} %reshape.109.refs_0_, bf16[12,24,256,128]{3,2,1,0:T(8,128)(2,1)} %split_operator.3.refs_1_, f32[4,2,3,128,128]{4,3,2,1,0:T(8,128)} %bitcast.84, f32[8,128]{1,0:T(8,128)S(1)} %get-tuple-element.169.refs_3_), custom_call_target="tpu_custom_call" | custom-call | bytes 393216 | tf_op jit(solution)/shard_map/apply_operator/pallas_call | solution.py:218
  255.2 12.2 %apply_operator.52 = (f32[3,128,128]{2,1,0:T(8,128)S(1)}, f32[8,128]{1,0:T(8,128)S(1)}) custom-call(s32[288]{0:T(512)S(1)} %reshape.104.refs_0_, bf16[12,24,256,128]{3,2,1,0:T(8,128)(2,1)} %split_operator.2.refs_1_, f32[4,2,3,128,128]{4,3,2,1,0:T(8,128)} %bitcast.93, f32[8,128]{1,0:T(8,128)S(1)} %get-tuple-element.170.refs_2_.refs_3_, ...), custom_call_target="tpu_custom_call" | custom-call | bytes 393216 | tf_op jit(solution)/shard_map/apply_operator/pallas_call | solution.py:218
  269.4 12.3 %apply_operator.53 = (f32[3,128,128]{2,1,0:T(8,128)S(1)}, f32[8,128]{1,0:T(8,128)S(1)}) custom-call(s32[288]{0:T(512)S(1)} %reshape.109.refs_0_, bf16[12,24,256,128]{3,2,1,0:T(8,128)(2,1)} %split_operator.3.refs_1_, f32[4,2,3,128,128]{4,3,2,1,0:T(8,128)} %bitcast.90, f32[8,128]{1,0:T(8,128)S(1)} %get-tuple-element.174.refs_3_), custom_call_target="tpu_custom_call" | custom-call | bytes 393216 | tf_op jit(solution)/shard_map/apply_operator/pallas_call | solution.py:218
  296.7 12.3 %apply_operator.55 = (f32[3,128,128]{2,1,0:T(8,128)S(1)}, f32[8,128]{1,0:T(8,128)S(1)}) custom-call(s32[288]{0:T(512)S(1)} %reshape.109.refs_0_, bf16[12,24,256,128]{3,2,1,0:T(8,128)(2,1)} %split_operator.3.refs_1_, f32[4,2,3,128,128]{4,3,2,1,0:T(8,128)} %bitcast.92, f32[8,128]{1,0:T(8,128)S(1)} %get-tuple-element.179.refs_3_), custom_call_target="tpu_custom_call" | custom-call | bytes 393216 | tf_op jit(solution)/shard_map/apply_operator/pallas_call | solution.py:218
  325.0 12.3 %apply_operator.57 = (f32[3,128,128]{2,1,0:T(8,128)S(1)}, f32[8,128]{1,0:T(8,128)S(1)}) custom-call(s32[288]{0:T(512)S(1)} %reshape.109.refs_0_, bf16[12,24,256,128]{3,2,1,0:T(8,128)(2,1)} %split_operator.3.refs_1_, f32[4,2,3,128,128]{4,3,2,1,0:T(8,128)} %bitcast.94, f32[8,128]{1,0:T(8,128)S(1)} %get-tuple-element.183.refs_3_), custom_call_target="tpu_custom_call" | custom-call | bytes 393216 | tf_op jit(solution)/shard_map/apply_operator/pallas_call | solution.py:218
  352.3 12.3 %apply_operator.59 = (f32[3,128,128]{2,1,0:T(8,128)S(1)}, f32[8,128]{1,0:T(8,128)S(1)}) custom-call(s32[288]{0:T(512)S(1)} %reshape.109.refs_0_, bf16[12,24,256,128]{3,2,1,0:T(8,128)(2,1)} %split_operator.3.refs_1_, f32[4,2,3,128,128]{4,3,2,1,0:T(8,128)} %bitcast.96, f32[8,128]{1,0:T(8,128)S(1)} %get-tuple-element.190.refs_3_), custom_call_target="tpu_custom_call" | custom-call | bytes 393216 | tf_op jit(solution)/shard_map/apply_operator/pallas_call | solution.py:218
  379.6 12.3 %apply_operator.61 = (f32[3,128,128]{2,1,0:T(8,128)S(1)}, f32[8,128]{1,0:T(8,128)S(1)}) custom-call(s32[288]{0:T(512)S(1)} %reshape.109.refs_0_, bf16[12,24,256,128]{3,2,1,0:T(8,128)(2,1)} %split_operator.3.refs_1_, f32[4,2,3,128,128]{4,3,2,1,0:T(8,128)} %bitcast.98, f32[8,128]{1,0:T(8,128)S(1)} %get-tuple-element.195.refs_3_), custom_call_target="tpu_custom_call" | custom-call | bytes 393216 | tf_op jit(solution)/shard_map/apply_operator/pallas_call | solution.py:218
  392.7 12.2 %apply_operator.62 = (f32[3,128,128]{2,1,0:T(8,128)S(1)}, f32[8,128]{1,0:T(8,128)S(1)}) custom-call(s32[288]{0:T(512)S(1)} %reshape.104.refs_0_, bf16[12,24,256,128]{3,2,1,0:T(8,128)(2,1)} %split_operator.2.refs_1_, f32[4,2,3,128,128]{4,3,2,1,0:T(8,128)} %bitcast.105, f32[8,128]{1,0:T(8,128)S(1)} %get-tuple-element.196.refs_2_.refs_3_, ...), custom_call_target="tpu_custom_call" | custom-call | bytes 393216 | tf_op jit(solution)/shard_map/apply_operator/pallas_call | solution.py:218
  406.8 12.3 %apply_operator.63 = (f32[3,128,128]{2,1,0:T(8,128)S(1)}, f32[8,128]{1,0:T(8,128)S(1)}) custom-call(s32[288]{0:T(512)S(1)} %reshape.109.refs_0_, bf16[12,24,256,128]{3,2,1,0:T(8,128)(2,1)} %split_operator.3.refs_1_, f32[4,2,3,128,128]{4,3,2,1,0:T(8,128)} %bitcast.100, f32[8,128]{1,0:T(8,128)S(1)} %get-tuple-element.200.refs_3_), custom_call_target="tpu_custom_call" | custom-call | bytes 393216 | tf_op jit(solution)/shard_map/apply_operator/pallas_call | solution.py:218
  432.4 12.3 %apply_operator.65 = (f32[3,128,128]{2,1,0:T(8,128)S(1)}, f32[8,128]{1,0:T(8,128)S(1)}) custom-call(s32[288]{0:T(512)S(1)} %reshape.109.refs_0_, bf16[12,24,256,128]{3,2,1,0:T(8,128)(2,1)} %split_operator.3.refs_1_, f32[4,2,3,128,128]{4,3,2,1,0:T(8,128)} %bitcast.102, f32[8,128]{1,0:T(8,128)S(1)} %get-tuple-element.204.refs_3_), custom_call_target="tpu_custom_call" | custom-call | bytes 393216 | tf_op jit(solution)/shard_map/apply_operator/pallas_call | solution.py:218
  458.4 12.2 %apply_operator.67 = (f32[3,128,128]{2,1,0:T(8,128)S(1)}, f32[8,128]{1,0:T(8,128)S(1)}) custom-call(s32[288]{0:T(512)S(1)} %reshape.109.refs_0_, bf16[12,24,256,128]{3,2,1,0:T(8,128)(2,1)} %split_operator.3.refs_1_, f32[4,2,3,128,128]{4,3,2,1,0:T(8,128)} %bitcast.106, f32[8,128]{1,0:T(8,128)S(1)} %get-tuple-element.209.refs_3_), custom_call_target="tpu_custom_call" | custom-call | bytes 393216 | tf_op jit(solution)/shard_map/apply_operator/pallas_call | solution.py:218
  484.3 12.3 %apply_operator.69 = (f32[3,128,128]{2,1,0:T(8,128)S(1)}, f32[8,128]{1,0:T(8,128)S(1)}) custom-call(s32[288]{0:T(512)S(1)} %reshape.109.refs_0_, bf16[12,24,256,128]{3,2,1,0:T(8,128)(2,1)} %split_operator.3.refs_1_, f32[4,2,3,128,128]{4,3,2,1,0:T(8,128)} %bitcast.104, f32[8,128]{1,0:T(8,128)S(1)} %get-tuple-element.216.refs_3_), custom_call_target="tpu_custom_call" | custom-call | bytes 393216 | tf_op jit(solution)/shard_map/apply_operator/pallas_call | solution.py:218
  517.8 12.3 %apply_operator.71 = (f32[3,128,128]{2,1,0:T(8,128)S(1)}, f32[8,128]{1,0:T(8,128)S(1)}) custom-call(s32[288]{0:T(512)S(1)} %reshape.109.refs_0_, bf16[12,24,256,128]{3,2,1,0:T(8,128)(2,1)} %split_operator.3.refs_1_, f32[4,2,3,128,128]{4,3,2,1,0:T(8,128)} %bitcast.88, f32[8,128]{1,0:T(8,128)S(1)} %get-tuple-element.221.refs_3_), custom_call_target="tpu_custom_call" | custom-call | bytes 393216 | tf_op jit(solution)/shard_map/apply_operator/pallas_call | solution.py:218
  538.6 12.2 %apply_operator.72 = (f32[3,128,128]{2,1,0:T(8,128)S(1)}, f32[8,128]{1,0:T(8,128)S(1)}) custom-call(s32[288]{0:T(512)S(1)} %reshape.104.refs_0_, bf16[12,24,256,128]{3,2,1,0:T(8,128)(2,1)} %split_operator.2.refs_1_, f32[4,2,3,128,128]{4,3,2,1,0:T(8,128)} %bitcast.108, f32[8,128]{1,0:T(8,128)S(1)} %get-tuple-element.222.refs_2_.refs_3_, ...), custom_call_target="tpu_custom_call" | custom-call | bytes 393216 | tf_op jit(solution)/shard_map/apply_operator/pallas_call | solution.py:218
  798.8 12.3 %apply_operator.82 = (f32[3,128,128]{2,1,0:T(8,128)S(1)}, f32[8,128]{1,0:T(8,128)S(1)}) custom-call(s32[288]{0:T(512)S(1)} %reshape.104.refs_0_, bf16[12,24,256,128]{3,2,1,0:T(8,128)(2,1)} %split_operator.2.refs_1_, f32[4,2,3,128,128]{4,3,2,1,0:T(8,128)} %bitcast.119, f32[8,128]{1,0:T(8,128)S(1)} %get-tuple-element.274.refs_2_.refs_3_, ...), custom_call_target="tpu_custom_call" | custom-call | bytes 393216 | tf_op jit(solution)/shard_map/apply_operator/pallas_call | solution.py:218
  811.5 13.6 %all-gather.111.cloned.1.call-done = f32[24,128,128]{2,1,0:T(8,128)} async-done(((f32[3,128,128]{2,1,0:T(8,128)}), f32[24,128,128]{2,1,0:T(8,128)}) %all-gather.111.cloned.1.call-update) | async-done | bytes 1572880 | tf_op jit(solution)/shard_map/all_gather | solution.py:293
  825.1 12.4 %apply_operator.83 = (f32[3,128,128]{2,1,0:T(8,128)S(1)}, f32[8,128]{1,0:T(8,128)}) custom-call(s32[288]{0:T(512)S(1)} %reshape.104.refs_0_, bf16[12,24,256,128]{3,2,1,0:T(8,128)(2,1)} %split_operator.2.refs_1_, f32[4,2,3,128,128]{4,3,2,1,0:T(8,128)} %bitcast.120, f32[8,128]{1,0:T(8,128)S(1)} %get-tuple-element.279.refs_3_), custom_call_target="tpu_custom_call" | custom-call | bytes 393216 | tf_op jit(solution)/shard_map/apply_operator/pallas_call | solution.py:218
  (304 shorter events, 524.5 us)
Async XLA Ops:
  19.4 58.4 %all-gather.59.cloned.1.call-start = ((), (), s32[]{:S(2)}) async-start(), calls=%async_computation.1 | async-start | bytes 1769472 | tf_op jit(solution)/shard_map/all_gather | solution.py:293
  27.3 113.0 %collective-permute-start.6 = (f32[12,12,128,128]{3,2,1,0:T(8,128)}, f32[12,12,128,128]{3,2,1,0:T(8,128)}, u32[]{:S(2)}, u32[]{:S(2)}) collective-permute-start(f32[12,12,128,128]{3,2,1,0:T(8,128)} %other_half.3), channel_id=1, source_target_pairs={{0,4},{4,0},{1,5},{5,1},{2,6},{6,2},{3,7},{7,3},{8,12},{12,8},{9,1... | collective-permute-start | bytes 28311560 | tf_op jit(solution)/shard_map/ppermute | solution.py:273
  28.1 96.4 %all-gather.61.cloned.1.call-start = ((), (), s32[]{:S(2)}) async-start(), calls=%async_computation.2 | async-start | bytes 1769472 | tf_op jit(solution)/shard_map/all_gather | solution.py:293
  98.8 71.5 %all-gather.65.cloned.1.call-start = ((), (), s32[]{:S(2)}) async-start(), calls=%async_computation.4 | async-start | bytes 1769472 | tf_op jit(solution)/shard_map/all_gather | solution.py:293
  120.6 78.7 %all-gather.63.cloned.1.call-start = ((), (), s32[]{:S(2)}) async-start(), calls=%async_computation.3 | async-start | bytes 1769472 | tf_op jit(solution)/shard_map/all_gather | solution.py:293
  170.2 57.8 %all-gather.69.cloned.1.call-start = ((), (), s32[]{:S(2)}) async-start(), calls=%async_computation.6 | async-start | bytes 1769472 | tf_op jit(solution)/shard_map/all_gather | solution.py:293
  199.0 56.2 %all-gather.67.cloned.1.call-start = ((), (), s32[]{:S(2)}) async-start(), calls=%async_computation.5 | async-start | bytes 1769472 | tf_op jit(solution)/shard_map/all_gather | solution.py:293
  227.9 54.6 %all-gather.73.cloned.1.call-start = ((), (), s32[]{:S(2)}) async-start(), calls=%async_computation.8 | async-start | bytes 1769472 | tf_op jit(solution)/shard_map/all_gather | solution.py:293
  255.2 55.7 %all-gather.71.cloned.1.call-start = ((), (), s32[]{:S(2)}) async-start(), calls=%async_computation.7 | async-start | bytes 1769472 | tf_op jit(solution)/shard_map/all_gather | solution.py:293
  282.4 55.7 %all-gather.77.cloned.1.call-start = ((), (), s32[]{:S(2)}) async-start(), calls=%async_computation.10 | async-start | bytes 1769472 | tf_op jit(solution)/shard_map/all_gather | solution.py:293
  310.4 55.0 %all-gather.75.cloned.1.call-start = ((), (), s32[]{:S(2)}) async-start(), calls=%async_computation.9 | async-start | bytes 1769472 | tf_op jit(solution)/shard_map/all_gather | solution.py:293
  365.3 54.8 %all-gather.79.cloned.1.call-start = ((), (), s32[]{:S(2)}) async-start(), calls=%async_computation.11 | async-start | bytes 1769472 | tf_op jit(solution)/shard_map/all_gather | solution.py:293
  446.0 59.5 %all-gather.89.cloned.1.call-start = ((), (), s32[]{:S(2)}) async-start(), calls=%async_computation.16 | async-start | bytes 1769472 | tf_op jit(solution)/shard_map/all_gather | solution.py:293
  472.0 66.6 %all-gather.87.cloned.1.call-start = ((), (), s32[]{:S(2)}) async-start(), calls=%async_computation.15 | async-start | bytes 1769472 | tf_op jit(solution)/shard_map/all_gather | solution.py:293
  505.4 57.3 %all-gather.93.cloned.1.call-start = ((), (), s32[]{:S(2)}) async-start(), calls=%async_computation.18 | async-start | bytes 1769472 | tf_op jit(solution)/shard_map/all_gather | solution.py:293
  559.3 55.9 %all-gather.97.cloned.1.call-start = ((), (), s32[]{:S(2)}) async-start(), calls=%async_computation.20 | async-start | bytes 1769472 | tf_op jit(solution)/shard_map/all_gather | solution.py:293
  584.7 56.8 %all-gather.95.cloned.1.call-start = ((), (), s32[]{:S(2)}) async-start(), calls=%async_computation.19 | async-start | bytes 1769472 | tf_op jit(solution)/shard_map/all_gather | solution.py:293
  611.6 56.1 %all-gather.99.cloned.1.call-start = ((), (), s32[]{:S(2)}) async-start(), calls=%async_computation.21 | async-start | bytes 1769472 | tf_op jit(solution)/shard_map/all_gather | solution.py:293
  637.2 56.9 %all-gather.101.cloned.1.call-start = ((), (), s32[]{:S(2)}) async-start(), calls=%async_computation.22 | async-start | bytes 1769472 | tf_op jit(solution)/shard_map/all_gather | solution.py:293
  664.0 56.2 %all-gather.103.cloned.1.call-start = ((), (), s32[]{:S(2)}) async-start(), calls=%async_computation.23 | async-start | bytes 1769472 | tf_op jit(solution)/shard_map/all_gather | solution.py:293
  689.7 56.8 %all-gather.105.cloned.1.call-start = ((), (), s32[]{:S(2)}) async-start(), calls=%async_computation.24 | async-start | bytes 1769472 | tf_op jit(solution)/shard_map/all_gather | solution.py:293
  716.6 56.0 %all-gather.107.cloned.1.call-start = ((), (), s32[]{:S(2)}) async-start(), calls=%async_computation.25 | async-start | bytes 1769472 | tf_op jit(solution)/shard_map/all_gather | solution.py:293
  742.8 55.9 %all-gather.109.cloned.1.call-start = ((), (), s32[]{:S(2)}) async-start(), calls=%async_computation.26 | async-start | bytes 1769472 | tf_op jit(solution)/shard_map/all_gather | solution.py:293
  769.0 56.0 %all-gather.111.cloned.1.call-start = ((), (), s32[]{:S(2)}) async-start(), calls=%async_computation.27 | async-start | bytes 1769472 | tf_op jit(solution)/shard_map/all_gather | solution.py:293
  (78 other events, 1036.7 us)
Sparse Core Ops, SparseCore 0:
  19.5 28.9 all-gather.56
  50.2 27.5 all-gather.58
  98.9 25.5 all-gather.60
  126.0 24.4 all-gather.64
  170.3 24.0 all-gather.62
  199.2 23.5 all-gather.68
  282.6 22.8 all-gather.70
  310.5 22.9 all-gather.76
  365.5 22.7 all-gather.80
  420.0 22.8 all-gather.84
  446.1 22.8 all-gather.82
  472.1 23.0 all-gather.88
  505.6 23.4 all-gather.86
  538.5 24.2 all-gather.92
  564.4 24.5 all-gather.90
  590.5 24.6 all-gather.96
  616.9 24.5 all-gather.94
  643.1 24.6 all-gather.98
  669.4 24.6 all-gather.100
  695.5 24.6 all-gather.102
  721.9 24.5 all-gather.104
  748.0 24.6 all-gather.106
  774.1 24.5 all-gather.108
  800.4 24.5 all-gather.110
  (4 shorter events, 90.8 us)

commit v7 on v6

--- a/solution.py
+++ b/solution.py
@@ -156,25 +156,24 @@
     @pl.when(row == 0)
     def _():
         token_ref[...] = jnp.zeros_like(token_ref)
-        lane = lax.broadcasted_iota(jnp.int32, (size, lanes), 1)
-        left = lane < lanes // 2
-        masks = [lane // span % max(1, pack // 2) == q for q in range(pack // 2)]
+        middle = lanes // 2
+        lane = lax.broadcasted_iota(jnp.int32, (size, lanes), 1) // span % max(1, pack // 2)
+        masks = [(lane == q).astype(jnp.float32).astype(jnp.bfloat16) for q in range(pack // 2)]
         for half in range(halves):
             for piece in range(pieces):
                 for group in range(groups):
                     tile = gathered_ref[piece, half, group]
-                    high = tile.astype(jnp.bfloat16).astype(jnp.float32)
-                    low = tile - high
+                    high = tile.astype(jnp.bfloat16)
+                    low = (tile - high.astype(jnp.float32)).astype(jnp.bfloat16)
                     base = ((half * pieces + piece) * groups + group) * pack
                     if pack == 1:
-                        tiles[base] = jnp.concatenate([high, low], axis=1).astype(jnp.bfloat16)
+                        tiles[base] = jnp.concatenate([high, low], axis=1)
                         continue
-                    first = jnp.where(left, high, pltpu.roll(low, lanes // 2, 1))
-                    second = jnp.where(left, pltpu.roll(high, lanes // 2, 1), low)
+                    first = jnp.concatenate([high[:, :middle], low[:, :middle]], axis=1)
+                    second = jnp.concatenate([high[:, middle:], low[:, middle:]], axis=1)
                     for start, both in ((base, first), (base + pack // 2, second)):
                         for q, mask in enumerate(masks):
-                            alone = both if pack == 2 else jnp.where(mask, both, 0.0)
-                            tiles[start + q] = alone.astype(jnp.bfloat16)
+                            tiles[start + q] = both if pack == 2 else both * mask
 
     fetch(row).wait()
     slot = lax.rem(row, count)
@@ -296,8 +295,8 @@
     moments = batches + delay * last
     downs, refls, ups, tokens = [], [], [], []
 
-    def incident_of(moment):
-        after = tokens[moment - delay : moment - delay + 1]
+    def incident_of(moment, ready=()):
+        after = [*tokens[moment - delay : moment - delay + 1], *ready]
         if moment < moments:
             which = jnp.clip(moment - delay * position, 0, batches - 1)
             terms = [lax.dynamic_index_in_dim(source, which, 0, keepdims=False)]
@@ -314,11 +313,11 @@
     gathered = [gather(piece)]
     trans = operator(tr_vals[0, 0, 0], tr_cols[0, 0, 0], piece, gathered[0])
     lag = max(0, min(delay, batches - 2))
-    copied_after = piece
+    copied_after, ready = in_hbm(gathered[0]), []
     for moment in range(2 * moments):
         after = tokens[-1:]
         if moment + 1 < 2 * moments:
-            piece, token = incident_of(moment + 1)
+            piece, token = incident_of(moment + 1, ready if moment == lag else [])
             gathered.append(gather(piece))
             after = after + [token]
         if moment == 0:
@@ -327,6 +326,7 @@
         (downs if moment < moments else ups).append(product)
         if moment == max(0, lag - 1):
             refl = operator(rf_vals[0, 0, 0], rf_cols[0, 0, 0], copied_after, token)
+            ready = [in_hbm(refl[0])]
         if lag <= moment < moments + lag:
             product, token = apply_operator(*refl, gathered[moment - lag], [token])
             refls.append(product)

time: 858 us -> 858 us (level)
  transfers between devices with their start and end apart: 56 -> 56, of which waited for: 29 -> 26; matrix products, arithmetic and copies ran while one was open for 0% -> 0% of each run, Pallas kernels for 66% -> 66%
where the time goes in v7:
time: 858 us; the launch traced here: 847 us
  Pallas kernels  587 us (68%)
  waiting for transfers between devices  184 us (21%)
  starting transfers between devices  49 us (6%)
  between operations  15.6 us (2%)
  local copies, waits for them, and re-layouts  11 us (1%)
    pallas_call x42, Pallas kernels, apply_operator(): pl.pallas_call(kernel, grid_spec=spec, out_shape=[jax.ShapeDtypeStruct((g...  515 us
    ppermute x24, waiting for transfers between devices, passed_along(): lax.ppermute(value, axis, [(source, source + steps) for source in range(i...  92.4 us
    all_gather x28, waiting for transfers between devices, gather(): gathered = lax.all_gather(piece, ('col', 'row'), axis=0)  79.3 us
    ppermute x24, starting transfers between devices, passed_along(): lax.ppermute(value, axis, [(source, source + steps) for source in range(i...  45.3 us
    pallas_call x2, Pallas kernels, split_operator(): pl.pallas_call(split_kernel, grid_spec=spec, out_shape=jax.ShapeDtypeStru...  33.9 us
    pallas_call x28, Pallas kernels, sum_of(): pl.pallas_call(kernel, grid=(1,), in_specs=[whole] * len(terms) + [pl.Blo...  19 us
  transfers between devices with their start and end apart: 56, of which 26 were waited for; matrix products, arithmetic and copies ran while one was open for 0% of the time, Pallas kernels for 66%

profile of v7, /device:TPU:0, one launch (start us, length us, event | category | flops | bytes accessed | tf_op | source)
XLA Modules:
  0.0 847.3 jit_solution(13974991210009941156)
XLA Ops:
  19.5 27.6 %all-gather.57.cloned.1.call-done = f32[24,128,128]{2,1,0:T(8,128)} async-done(((f32[3,128,128]{2,1,0:T(8,128)}), f32[24,128,128]{2,1,0:T(8,128)}) %all-gather.57.cloned.1.call-update) | async-done | bytes 1572880 | tf_op jit(solution)/shard_map/all_gather | solution.py:292
  68.4 17.0 %split_operator.2.refs_1_ = bf16[12,24,256,128]{3,2,1,0:T(8,128)(2,1)} custom-call(s32[1]{0:T(128)} %bitcast.1.place_ref, f32[24,12,128,128]{3,2,1,0:T(8,128)} %bitcast.76, f32[12,12,128,128]{3,2,1,0:T(8,128)} %collective-permute-done.1.other_ref, f32[4,2,3,128,128]{4,3,2,1,0:T(8,128)} %bitcast.78), custom_call_target="tpu_custom_call" | custom-call | tf_op jit(solution)/shard_map/split_operator/pallas_call | solution.py:126
  123.8 16.9 %split_operator.3.refs_3_.refs_1_ = bf16[12,24,256,128]{3,2,1,0:T(8,128)(2,1)} custom-call(s32[1]{0:T(128)} %bitcast.1.place_ref, f32[24,12,128,128]{3,2,1,0:T(8,128)} %bitcast.74, f32[12,12,128,128]{3,2,1,0:T(8,128)} %collective-permute-done.4.other_ref, f32[8,128]{1,0:T(8,128)} %copy-done.43), custom_call_target="tpu_custom_call" | custom-call | tf_op jit(solution)/shard_map/split_operator/pallas_call | solution.py:126
  141.5 12.2 %apply_operator.44 = (f32[3,128,128]{2,1,0:T(8,128)S(1)}, f32[8,128]{1,0:T(8,128)S(1)}) custom-call(s32[288]{0:T(512)S(1)} %reshape.104.refs_0_, bf16[12,24,256,128]{3,2,1,0:T(8,128)(2,1)} %split_operator.2.refs_1_, f32[4,2,3,128,128]{4,3,2,1,0:T(8,128)} %bitcast.86, f32[8,128]{1,0:T(8,128)S(1)} %copy-done.44, f32[8,128]{1,0:T(8,128)S(1)} %get-tuple-element.152.refs_4_), custom_call_target="tpu_custom_call" | custom-call | bytes 393216 | tf_op jit(solution)/shard_map/apply_operator/pallas_call | solution.py:217
  158.3 12.3 %apply_operator.45 = (f32[3,128,128]{2,1,0:T(8,128)S(1)}, f32[8,128]{1,0:T(8,128)S(1)}) custom-call(s32[288]{0:T(512)S(1)} %reshape.109.refs_0_, bf16[12,24,256,128]{3,2,1,0:T(8,128)(2,1)} %split_operator.3.refs_3_.refs_1_, f32[4,2,3,128,128]{4,3,2,1,0:T(8,128)} %bitcast.80, f32[8,128]{1,0:T(8,128)S(1)} %get-tuple-element.154.refs_3_), custom_call_target="tpu_custom_call" | custom-call | bytes 393216 | tf_op jit(solution)/shard_map/apply_operator/pallas_call | solution.py:217
  186.2 12.3 %apply_operator.47 = (f32[3,128,128]{2,1,0:T(8,128)S(1)}, f32[8,128]{1,0:T(8,128)S(1)}) custom-call(s32[288]{0:T(512)S(1)} %reshape.109.refs_0_, bf16[12,24,256,128]{3,2,1,0:T(8,128)(2,1)} %split_operator.3.refs_3_.refs_1_, f32[4,2,3,128,128]{4,3,2,1,0:T(8,128)} %bitcast.83, f32[8,128]{1,0:T(8,128)S(1)} %get-tuple-element.159.refs_3_), custom_call_target="tpu_custom_call" | custom-call | bytes 393216 | tf_op jit(solution)/shard_map/apply_operator/pallas_call | solution.py:217
  213.7 12.3 %apply_operator.49 = (f32[3,128,128]{2,1,0:T(8,128)S(1)}, f32[8,128]{1,0:T(8,128)S(1)}) custom-call(s32[288]{0:T(512)S(1)} %reshape.109.refs_0_, bf16[12,24,256,128]{3,2,1,0:T(8,128)(2,1)} %split_operator.3.refs_3_.refs_1_, f32[4,2,3,128,128]{4,3,2,1,0:T(8,128)} %bitcast.87, f32[8,128]{1,0:T(8,128)S(1)} %get-tuple-element.164.refs_3_), custom_call_target="tpu_custom_call" | custom-call | bytes 393216 | tf_op jit(solution)/shard_map/apply_operator/pallas_call | solution.py:217
  226.8 12.2 %apply_operator.50 = (f32[3,128,128]{2,1,0:T(8,128)S(1)}, f32[8,128]{1,0:T(8,128)S(1)}) custom-call(s32[288]{0:T(512)S(1)} %reshape.104.refs_0_, bf16[12,24,256,128]{3,2,1,0:T(8,128)(2,1)} %split_operator.2.refs_1_, f32[4,2,3,128,128]{4,3,2,1,0:T(8,128)} %bitcast.92, f32[8,128]{1,0:T(8,128)S(1)} %get-tuple-element.165.refs_2_.refs_3_, ...), custom_call_target="tpu_custom_call" | custom-call | bytes 393216 | tf_op jit(solution)/shard_map/apply_operator/pallas_call | solution.py:217
  240.9 12.3 %apply_operator.51 = (f32[3,128,128]{2,1,0:T(8,128)S(1)}, f32[8,128]{1,0:T(8,128)S(1)}) custom-call(s32[288]{0:T(512)S(1)} %reshape.109.refs_0_, bf16[12,24,256,128]{3,2,1,0:T(8,128)(2,1)} %split_operator.3.refs_3_.refs_1_, f32[4,2,3,128,128]{4,3,2,1,0:T(8,128)} %bitcast.85, f32[8,128]{1,0:T(8,128)S(1)} %get-tuple-element.169.refs_3_), custom_call_target="tpu_custom_call" | custom-call | bytes 393216 | tf_op jit(solution)/shard_map/apply_operator/pallas_call | solution.py:217
  254.1 12.2 %apply_operator.52 = (f32[3,128,128]{2,1,0:T(8,128)S(1)}, f32[8,128]{1,0:T(8,128)S(1)}) custom-call(s32[288]{0:T(512)S(1)} %reshape.104.refs_0_, bf16[12,24,256,128]{3,2,1,0:T(8,128)(2,1)} %split_operator.2.refs_1_, f32[4,2,3,128,128]{4,3,2,1,0:T(8,128)} %bitcast.94, f32[8,128]{1,0:T(8,128)S(1)} %get-tuple-element.170.refs_2_.refs_3_, ...), custom_call_target="tpu_custom_call" | custom-call | bytes 393216 | tf_op jit(solution)/shard_map/apply_operator/pallas_call | solution.py:217
  268.3 12.3 %apply_operator.53 = (f32[3,128,128]{2,1,0:T(8,128)S(1)}, f32[8,128]{1,0:T(8,128)S(1)}) custom-call(s32[288]{0:T(512)S(1)} %reshape.109.refs_0_, bf16[12,24,256,128]{3,2,1,0:T(8,128)(2,1)} %split_operator.3.refs_3_.refs_1_, f32[4,2,3,128,128]{4,3,2,1,0:T(8,128)} %bitcast.91, f32[8,128]{1,0:T(8,128)S(1)} %get-tuple-element.174.refs_3_), custom_call_target="tpu_custom_call" | custom-call | bytes 393216 | tf_op jit(solution)/shard_map/apply_operator/pallas_call | solution.py:217
  295.5 12.3 %apply_operator.55 = (f32[3,128,128]{2,1,0:T(8,128)S(1)}, f32[8,128]{1,0:T(8,128)S(1)}) custom-call(s32[288]{0:T(512)S(1)} %reshape.109.refs_0_, bf16[12,24,256,128]{3,2,1,0:T(8,128)(2,1)} %split_operator.3.refs_3_.refs_1_, f32[4,2,3,128,128]{4,3,2,1,0:T(8,128)} %bitcast.93, f32[8,128]{1,0:T(8,128)S(1)} %get-tuple-element.179.refs_3_), custom_call_target="tpu_custom_call" | custom-call | bytes 393216 | tf_op jit(solution)/shard_map/apply_operator/pallas_call | solution.py:217
  323.9 12.3 %apply_operator.57 = (f32[3,128,128]{2,1,0:T(8,128)S(1)}, f32[8,128]{1,0:T(8,128)S(1)}) custom-call(s32[288]{0:T(512)S(1)} %reshape.109.refs_0_, bf16[12,24,256,128]{3,2,1,0:T(8,128)(2,1)} %split_operator.3.refs_3_.refs_1_, f32[4,2,3,128,128]{4,3,2,1,0:T(8,128)} %bitcast.95, f32[8,128]{1,0:T(8,128)S(1)} %get-tuple-element.183.refs_3_), custom_call_target="tpu_custom_call" | custom-call | bytes 393216 | tf_op jit(solution)/shard_map/apply_operator/pallas_call | solution.py:217
  351.2 12.3 %apply_operator.59 = (f32[3,128,128]{2,1,0:T(8,128)S(1)}, f32[8,128]{1,0:T(8,128)S(1)}) custom-call(s32[288]{0:T(512)S(1)} %reshape.109.refs_0_, bf16[12,24,256,128]{3,2,1,0:T(8,128)(2,1)} %split_operator.3.refs_3_.refs_1_, f32[4,2,3,128,128]{4,3,2,1,0:T(8,128)} %bitcast.97, f32[8,128]{1,0:T(8,128)S(1)} %get-tuple-element.190.refs_3_), custom_call_target="tpu_custom_call" | custom-call | bytes 393216 | tf_op jit(solution)/shard_map/apply_operator/pallas_call | solution.py:217
  378.4 12.3 %apply_operator.61 = (f32[3,128,128]{2,1,0:T(8,128)S(1)}, f32[8,128]{1,0:T(8,128)S(1)}) custom-call(s32[288]{0:T(512)S(1)} %reshape.109.refs_0_, bf16[12,24,256,128]{3,2,1,0:T(8,128)(2,1)} %split_operator.3.refs_3_.refs_1_, f32[4,2,3,128,128]{4,3,2,1,0:T(8,128)} %bitcast.99, f32[8,128]{1,0:T(8,128)S(1)} %get-tuple-element.195.refs_3_), custom_call_target="tpu_custom_call" | custom-call | bytes 393216 | tf_op jit(solution)/shard_map/apply_operator/pallas_call | solution.py:217
  405.7 12.3 %apply_operator.63 = (f32[3,128,128]{2,1,0:T(8,128)S(1)}, f32[8,128]{1,0:T(8,128)S(1)}) custom-call(s32[288]{0:T(512)S(1)} %reshape.109.refs_0_, bf16[12,24,256,128]{3,2,1,0:T(8,128)(2,1)} %split_operator.3.refs_3_.refs_1_, f32[4,2,3,128,128]{4,3,2,1,0:T(8,128)} %bitcast.101, f32[8,128]{1,0:T(8,128)S(1)} %get-tuple-element.200.refs_3_), custom_call_target="tpu_custom_call" | custom-call | bytes 393216 | tf_op jit(solution)/shard_map/apply_operator/pallas_call | solution.py:217
  431.9 12.3 %apply_operator.65 = (f32[3,128,128]{2,1,0:T(8,128)S(1)}, f32[8,128]{1,0:T(8,128)S(1)}) custom-call(s32[288]{0:T(512)S(1)} %reshape.109.refs_0_, bf16[12,24,256,128]{3,2,1,0:T(8,128)(2,1)} %split_operator.3.refs_3_.refs_1_, f32[4,2,3,128,128]{4,3,2,1,0:T(8,128)} %bitcast.103, f32[8,128]{1,0:T(8,128)S(1)} %get-tuple-element.204.refs_3_), custom_call_target="tpu_custom_call" | custom-call | bytes 393216 | tf_op jit(solution)/shard_map/apply_operator/pallas_call | solution.py:217
  457.9 12.2 %apply_operator.67 = (f32[3,128,128]{2,1,0:T(8,128)S(1)}, f32[8,128]{1,0:T(8,128)S(1)}) custom-call(s32[288]{0:T(512)S(1)} %reshape.109.refs_0_, bf16[12,24,256,128]{3,2,1,0:T(8,128)(2,1)} %split_operator.3.refs_3_.refs_1_, f32[4,2,3,128,128]{4,3,2,1,0:T(8,128)} %bitcast.107, f32[8,128]{1,0:T(8,128)S(1)} %get-tuple-element.209.refs_3_), custom_call_target="tpu_custom_call" | custom-call | bytes 393216 | tf_op jit(solution)/shard_map/apply_operator/pallas_call | solution.py:217
  471.6 12.2 %apply_operator.68 = (f32[3,128,128]{2,1,0:T(8,128)S(1)}, f32[8,128]{1,0:T(8,128)S(1)}) custom-call(s32[288]{0:T(512)S(1)} %reshape.104.refs_0_, bf16[12,24,256,128]{3,2,1,0:T(8,128)(2,1)} %split_operator.2.refs_1_, f32[4,2,3,128,128]{4,3,2,1,0:T(8,128)} %bitcast.112, f32[8,128]{1,0:T(8,128)S(1)} %get-tuple-element.210.refs_1_.refs_3_, ...), custom_call_target="tpu_custom_call" | custom-call | bytes 393216 | tf_op jit(solution)/shard_map/apply_operator/pallas_call | solution.py:217
  483.9 12.3 %apply_operator.69 = (f32[3,128,128]{2,1,0:T(8,128)S(1)}, f32[8,128]{1,0:T(8,128)S(1)}) custom-call(s32[288]{0:T(512)S(1)} %reshape.109.refs_0_, bf16[12,24,256,128]{3,2,1,0:T(8,128)(2,1)} %split_operator.3.refs_3_.refs_1_, f32[4,2,3,128,128]{4,3,2,1,0:T(8,128)} %bitcast.105, f32[8,128]{1,0:T(8,128)S(1)} %get-tuple-element.216.refs_3_), custom_call_target="tpu_custom_call" | custom-call | bytes 393216 | tf_op jit(solution)/shard_map/apply_operator/pallas_call | solution.py:217
  517.3 12.3 %apply_operator.71 = (f32[3,128,128]{2,1,0:T(8,128)S(1)}, f32[8,128]{1,0:T(8,128)S(1)}) custom-call(s32[288]{0:T(512)S(1)} %reshape.109.refs_0_, bf16[12,24,256,128]{3,2,1,0:T(8,128)(2,1)} %split_operator.3.refs_3_.refs_1_, f32[4,2,3,128,128]{4,3,2,1,0:T(8,128)} %bitcast.89, f32[8,128]{1,0:T(8,128)S(1)} %get-tuple-element.221.refs_3_), custom_call_target="tpu_custom_call" | custom-call | bytes 393216 | tf_op jit(solution)/shard_map/apply_operator/pallas_call | solution.py:217
  798.5 12.3 %apply_operator.82 = (f32[3,128,128]{2,1,0:T(8,128)S(1)}, f32[8,128]{1,0:T(8,128)S(1)}) custom-call(s32[288]{0:T(512)S(1)} %reshape.104.refs_0_, bf16[12,24,256,128]{3,2,1,0:T(8,128)(2,1)} %split_operator.2.refs_1_, f32[4,2,3,128,128]{4,3,2,1,0:T(8,128)} %bitcast.120, f32[8,128]{1,0:T(8,128)S(1)} %get-tuple-element.274.refs_2_.refs_3_, ...), custom_call_target="tpu_custom_call" | custom-call | bytes 393216 | tf_op jit(solution)/shard_map/apply_operator/pallas_call | solution.py:217
  811.2 13.6 %all-gather.111.cloned.1.call-done = f32[24,128,128]{2,1,0:T(8,128)} async-done(((f32[3,128,128]{2,1,0:T(8,128)}), f32[24,128,128]{2,1,0:T(8,128)}) %all-gather.111.cloned.1.call-update) | async-done | bytes 1572880 | tf_op jit(solution)/shard_map/all_gather | solution.py:292
  824.7 12.4 %apply_operator.83 = (f32[3,128,128]{2,1,0:T(8,128)S(1)}, f32[8,128]{1,0:T(8,128)}) custom-call(s32[288]{0:T(512)S(1)} %reshape.104.refs_0_, bf16[12,24,256,128]{3,2,1,0:T(8,128)(2,1)} %split_operator.2.refs_1_, f32[4,2,3,128,128]{4,3,2,1,0:T(8,128)} %bitcast.121, f32[8,128]{1,0:T(8,128)S(1)} %get-tuple-element.279.refs_3_), custom_call_target="tpu_custom_call" | custom-call | bytes 393216 | tf_op jit(solution)/shard_map/apply_operator/pallas_call | solution.py:217
  (306 shorter events, 511.3 us)
Async XLA Ops:
  19.4 66.0 %all-gather.59.cloned.1.call-start = ((), (), s32[]{:S(2)}) async-start(), calls=%async_computation.1 | async-start | bytes 1769472 | tf_op jit(solution)/shard_map/all_gather | solution.py:292
  54.8 69.0 %collective-permute-start.4 = (f32[12,12,128,128]{3,2,1,0:T(8,128)}, f32[12,12,128,128]{3,2,1,0:T(8,128)}, u32[]{:S(2)}, u32[]{:S(2)}) collective-permute-start(f32[12,12,128,128]{3,2,1,0:T(8,128)} %other_half.3), channel_id=1, source_target_pairs={{0,4},{4,0},{1,5},{5,1},{2,6},{6,2},{3,7},{7,3},{8,12},{12,8},{9,1... | collective-permute-start | bytes 28311560 | tf_op jit(solution)/shard_map/ppermute | solution.py:272
  55.8 85.8 %all-gather.61.cloned.1.call-start = ((), (), s32[]{:S(2)}) async-start(), calls=%async_computation.2 | async-start | bytes 1769472 | tf_op jit(solution)/shard_map/all_gather | solution.py:292
  106.5 64.9 %all-gather.65.cloned.1.call-start = ((), (), s32[]{:S(2)}) async-start(), calls=%async_computation.4 | async-start | bytes 1769472 | tf_op jit(solution)/shard_map/all_gather | solution.py:292
  141.5 58.0 %all-gather.63.cloned.1.call-start = ((), (), s32[]{:S(2)}) async-start(), calls=%async_computation.3 | async-start | bytes 1769472 | tf_op jit(solution)/shard_map/all_gather | solution.py:292
  171.3 55.4 %all-gather.69.cloned.1.call-start = ((), (), s32[]{:S(2)}) async-start(), calls=%async_computation.6 | async-start | bytes 1769472 | tf_op jit(solution)/shard_map/all_gather | solution.py:292
  199.2 54.9 %all-gather.67.cloned.1.call-start = ((), (), s32[]{:S(2)}) async-start(), calls=%async_computation.5 | async-start | bytes 1769472 | tf_op jit(solution)/shard_map/all_gather | solution.py:292
  226.7 54.7 %all-gather.73.cloned.1.call-start = ((), (), s32[]{:S(2)}) async-start(), calls=%async_computation.8 | async-start | bytes 1769472 | tf_op jit(solution)/shard_map/all_gather | solution.py:292
  254.0 55.7 %all-gather.71.cloned.1.call-start = ((), (), s32[]{:S(2)}) async-start(), calls=%async_computation.7 | async-start | bytes 1769472 | tf_op jit(solution)/shard_map/all_gather | solution.py:292
  281.3 55.7 %all-gather.77.cloned.1.call-start = ((), (), s32[]{:S(2)}) async-start(), calls=%async_computation.10 | async-start | bytes 1769472 | tf_op jit(solution)/shard_map/all_gather | solution.py:292
  309.2 55.0 %all-gather.75.cloned.1.call-start = ((), (), s32[]{:S(2)}) async-start(), calls=%async_computation.9 | async-start | bytes 1769472 | tf_op jit(solution)/shard_map/all_gather | solution.py:292
  364.2 55.4 %all-gather.79.cloned.1.call-start = ((), (), s32[]{:S(2)}) async-start(), calls=%async_computation.11 | async-start | bytes 1769472 | tf_op jit(solution)/shard_map/all_gather | solution.py:292
  445.5 59.5 %all-gather.89.cloned.1.call-start = ((), (), s32[]{:S(2)}) async-start(), calls=%async_computation.16 | async-start | bytes 1769472 | tf_op jit(solution)/shard_map/all_gather | solution.py:292
  471.5 66.6 %all-gather.87.cloned.1.call-start = ((), (), s32[]{:S(2)}) async-start(), calls=%async_computation.15 | async-start | bytes 1769472 | tf_op jit(solution)/shard_map/all_gather | solution.py:292
  505.0 57.5 %all-gather.93.cloned.1.call-start = ((), (), s32[]{:S(2)}) async-start(), calls=%async_computation.18 | async-start | bytes 1769472 | tf_op jit(solution)/shard_map/all_gather | solution.py:292
  558.8 56.2 %all-gather.97.cloned.1.call-start = ((), (), s32[]{:S(2)}) async-start(), calls=%async_computation.20 | async-start | bytes 1769472 | tf_op jit(solution)/shard_map/all_gather | solution.py:292
  584.4 56.8 %all-gather.95.cloned.1.call-start = ((), (), s32[]{:S(2)}) async-start(), calls=%async_computation.19 | async-start | bytes 1769472 | tf_op jit(solution)/shard_map/all_gather | solution.py:292
  611.3 56.3 %all-gather.99.cloned.1.call-start = ((), (), s32[]{:S(2)}) async-start(), calls=%async_computation.21 | async-start | bytes 1769472 | tf_op jit(solution)/shard_map/all_gather | solution.py:292
  636.9 56.9 %all-gather.101.cloned.1.call-start = ((), (), s32[]{:S(2)}) async-start(), calls=%async_computation.22 | async-start | bytes 1769472 | tf_op jit(solution)/shard_map/all_gather | solution.py:292
  663.8 56.1 %all-gather.103.cloned.1.call-start = ((), (), s32[]{:S(2)}) async-start(), calls=%async_computation.23 | async-start | bytes 1769472 | tf_op jit(solution)/shard_map/all_gather | solution.py:292
  689.4 56.7 %all-gather.105.cloned.1.call-start = ((), (), s32[]{:S(2)}) async-start(), calls=%async_computation.24 | async-start | bytes 1769472 | tf_op jit(solution)/shard_map/all_gather | solution.py:292
  716.4 56.0 %all-gather.107.cloned.1.call-start = ((), (), s32[]{:S(2)}) async-start(), calls=%async_computation.25 | async-start | bytes 1769472 | tf_op jit(solution)/shard_map/all_gather | solution.py:292
  742.5 56.0 %all-gather.109.cloned.1.call-start = ((), (), s32[]{:S(2)}) async-start(), calls=%async_computation.26 | async-start | bytes 1769472 | tf_op jit(solution)/shard_map/all_gather | solution.py:292
  768.7 56.0 %all-gather.111.cloned.1.call-start = ((), (), s32[]{:S(2)}) async-start(), calls=%async_computation.27 | async-start | bytes 1769472 | tf_op jit(solution)/shard_map/all_gather | solution.py:292
  (79 other events, 1063.4 us)
Sparse Core Ops, SparseCore 0:
  19.6 27.4 all-gather.56
  55.9 24.5 all-gather.58
  106.6 25.5 all-gather.60
  141.6 24.5 all-gather.64
  254.1 22.7 all-gather.72
  309.4 22.8 all-gather.76
  337.0 22.8 all-gather.74
  364.3 22.8 all-gather.80
  391.6 22.8 all-gather.78
  419.5 22.8 all-gather.84
  445.7 22.8 all-gather.82
  471.6 23.0 all-gather.88
  505.1 23.4 all-gather.86
  538.0 24.4 all-gather.92
  564.1 24.5 all-gather.90
  590.2 24.6 all-gather.96
  616.6 24.6 all-gather.94
  642.9 24.5 all-gather.98
  669.2 24.5 all-gather.100
  695.3 24.6 all-gather.102
  721.6 24.5 all-gather.104
  747.6 24.6 all-gather.106
  773.9 24.5 all-gather.108
  800.1 24.5 all-gather.110
  (4 shorter events, 90.8 us)

commit v8 on v7

--- a/solution.py
+++ b/solution.py
@@ -133,19 +133,40 @@
 
 
 def apply_kernel(pack, index_ref, parts_ref, gathered_ref, *refs):
-    result_ref, token_ref, slots, tiles, arrived = refs[-5:]
+    result_ref, token_ref, slots, tiles, held, arrived, landed = refs[-7:]
     row, rows = pl.program_id(0), pl.num_programs(0)
     count, picks, twice, _ = slots.shape
     size = twice // 2
     pieces, halves, groups, _, lanes = gathered_ref.shape
     span = lanes // pack
 
+    class Copies:
+        def __init__(self, source, target, signals):
+            cut = source.shape[0] // 2
+            ends = ((0, cut), (cut, source.shape[0] - cut))
+            self.halves = [
+                pltpu.make_async_copy(source.at[pl.ds(*end)], target.at[pl.ds(*end)], signal)
+                for end, signal in zip(ends, signals)
+            ]
+
+        def start(self):
+            for priority, half in enumerate(self.halves):
+                half.start(priority=priority)
+
+        def wait(self):
+            for half in self.halves:
+                half.wait()
+
     def fetch(which):
         slot = lax.rem(which, count)
-        return pltpu.make_async_copy(parts_ref.at[which], slots.at[slot], arrived.at[slot])
+        signals = [arrived.at[slot, part] for part in range(2)]
+        return Copies(parts_ref.at[which], slots.at[slot], signals)
+
+    pieces_here = Copies(gathered_ref, held, [landed.at[part] for part in range(2)])
 
     @pl.when(row == 0)
     def _():
+        pieces_here.start()
         for ahead in range(min(count - 1, parts_ref.shape[0])):
             fetch(ahead).start()
 
@@ -156,13 +177,14 @@
     @pl.when(row == 0)
     def _():
         token_ref[...] = jnp.zeros_like(token_ref)
+        pieces_here.wait()
         middle = lanes // 2
         lane = lax.broadcasted_iota(jnp.int32, (size, lanes), 1) // span % max(1, pack // 2)
         masks = [(lane == q).astype(jnp.float32).astype(jnp.bfloat16) for q in range(pack // 2)]
         for half in range(halves):
             for piece in range(pieces):
                 for group in range(groups):
-                    tile = gathered_ref[piece, half, group]
+                    tile = held[piece, half, group]
                     high = tile.astype(jnp.bfloat16)
                     low = (tile - high.astype(jnp.float32)).astype(jnp.bfloat16)
                     base = ((half * pieces + piece) * groups + group) * pack
@@ -200,14 +222,16 @@
         grid=(rows,),
         in_specs=[
             pl.BlockSpec(memory_space=pltpu.HBM),
-            pl.BlockSpec(gathered.shape, lambda row, *_: (0, 0, 0, 0, 0)),
+            pl.BlockSpec(memory_space=pltpu.HBM),
         ]
         + [pl.BlockSpec(memory_space=pl.ANY)] * len(after),
         out_specs=[pl.BlockSpec((1, size, lanes), lambda row, *_: (row // pack, 0, 0)), TOKEN_SPEC],
         scratch_shapes=[
             pltpu.VMEM((SLOTS, picks, twice, depth), jnp.bfloat16),
             pltpu.VMEM((halves * pieces * groups * pack, size, lanes * (2 if pack == 1 else 1)), jnp.bfloat16),
-            pltpu.SemaphoreType.DMA((SLOTS,)),
+            pltpu.VMEM(gathered.shape, jnp.float32),
+            pltpu.SemaphoreType.DMA((SLOTS, 2)),
+            pltpu.SemaphoreType.DMA((2,)),
         ],
     )
 

time: 858 us -> 946 us (1.10)
  Pallas kernels: 587 us -> 711 us
  waiting for transfers between devices: 184 us -> 150 us
    pallas_call x42, Pallas kernels: 515 us -> 639 us  [apply_operator(): pl.pallas_call(kernel, grid_spec=spec, out_shape=[jax.ShapeDtypeStruct((g...]
    all_gather x28, waiting for transfers between devices: 79.3 us -> 46.2 us  [gather(): gathered = lax.all_gather(piece, ('col', 'row'), axis=0)]
  transfers between devices with their start and end apart: 56 -> 56, of which waited for: 26 -> 26; matrix products, arithmetic and copies ran while one was open for 0% -> 0% of each run, Pallas kernels for 66% -> 73%
where the time goes in v8:
time: 946 us; the launch traced here: 937 us
  Pallas kernels  711 us (75%)
  waiting for transfers between devices  150 us (16%)
  starting transfers between devices  48.1 us (5%)
  between operations  15.6 us (2%)
  local copies, waits for them, and re-layouts  11 us (1%)
    pallas_call x42, Pallas kernels, apply_operator(): pl.pallas_call(kernel, grid_spec=spec, out_shape=[jax.ShapeDtypeStruct((g...  639 us
    ppermute x24, waiting for transfers between devices, passed_along(): lax.ppermute(value, axis, [(source, source + steps) for source in range(i...  91.6 us
    all_gather x28, waiting for transfers between devices, gather(): gathered = lax.all_gather(piece, ('col', 'row'), axis=0)  46.2 us
    ppermute x24, starting transfers between devices, passed_along(): lax.ppermute(value, axis, [(source, source + steps) for source in range(i...  44.7 us
    pallas_call x2, Pallas kernels, split_operator(): pl.pallas_call(split_kernel, grid_spec=spec, out_shape=jax.ShapeDtypeStru...  33.9 us
    pallas_call x28, Pallas kernels, sum_of(): pl.pallas_call(kernel, grid=(1,), in_specs=[whole] * len(terms) + [pl.Blo...  19 us
  transfers between devices with their start and end apart: 56, of which 26 were waited for; matrix products, arithmetic and copies ran while one was open for 0% of the time, Pallas kernels for 73%

profile of v8, /device:TPU:0, one launch (start us, length us, event | category | flops | bytes accessed | tf_op | source)
XLA Modules:
  0.0 936.7 jit_solution(9253758275735527604)
XLA Ops:
  19.5 27.6 %all-gather.57.cloned.1.call-done = f32[24,128,128]{2,1,0:T(8,128)} async-done(((f32[3,128,128]{2,1,0:T(8,128)}), f32[24,128,128]{2,1,0:T(8,128)}) %all-gather.57.cloned.1.call-update) | async-done | bytes 1572880 | tf_op jit(solution)/shard_map/all_gather | solution.py:316
  68.4 17.0 %split_operator.2.refs_1_ = bf16[12,24,256,128]{3,2,1,0:T(8,128)(2,1)} custom-call(s32[1]{0:T(128)} %bitcast.1.place_ref, f32[24,12,128,128]{3,2,1,0:T(8,128)} %bitcast.76, f32[12,12,128,128]{3,2,1,0:T(8,128)} %collective-permute-done.1.other_ref, f32[4,2,3,128,128]{4,3,2,1,0:T(8,128)} %bitcast.78), custom_call_target="tpu_custom_call" | custom-call | tf_op jit(solution)/shard_map/split_operator/pallas_call | solution.py:126
  129.6 16.9 %split_operator.3.refs_3_.refs_1_ = bf16[12,24,256,128]{3,2,1,0:T(8,128)(2,1)} custom-call(s32[1]{0:T(128)} %bitcast.1.place_ref, f32[24,12,128,128]{3,2,1,0:T(8,128)} %bitcast.74, f32[12,12,128,128]{3,2,1,0:T(8,128)} %collective-permute-done.4.other_ref, f32[8,128]{1,0:T(8,128)} %copy-done.43), custom_call_target="tpu_custom_call" | custom-call | tf_op jit(solution)/shard_map/split_operator/pallas_call | solution.py:126
  183.0 15.3 %apply_operator.46 = (f32[3,128,128]{2,1,0:T(8,128)S(1)}, f32[8,128]{1,0:T(8,128)S(1)}) custom-call(s32[288]{0:T(512)S(1)} %reshape.104.refs_0_, bf16[12,24,256,128]{3,2,1,0:T(8,128)(2,1)} %split_operator.2.refs_1_, f32[4,2,3,128,128]{4,3,2,1,0:T(8,128)} %bitcast.84, f32[8,128]{1,0:T(8,128)S(1)} %get-tuple-element.155.refs_2_.refs_3_, ...), custom_call_target="tpu_custom_call" | custom-call | bytes 393216 | tf_op jit(solution)/shard_map/apply_operator/pallas_call | solution.py:241
  216.9 15.3 %apply_operator.48 = (f32[3,128,128]{2,1,0:T(8,128)S(1)}, f32[8,128]{1,0:T(8,128)S(1)}) custom-call(s32[288]{0:T(512)S(1)} %reshape.104.refs_0_, bf16[12,24,256,128]{3,2,1,0:T(8,128)(2,1)} %split_operator.2.refs_1_, f32[4,2,3,128,128]{4,3,2,1,0:T(8,128)} %bitcast.90, f32[8,128]{1,0:T(8,128)S(1)} %get-tuple-element.160.refs_2_.refs_3_, ...), custom_call_target="tpu_custom_call" | custom-call | bytes 393216 | tf_op jit(solution)/shard_map/apply_operator/pallas_call | solution.py:241
  250.1 15.3 %apply_operator.50 = (f32[3,128,128]{2,1,0:T(8,128)S(1)}, f32[8,128]{1,0:T(8,128)S(1)}) custom-call(s32[288]{0:T(512)S(1)} %reshape.104.refs_0_, bf16[12,24,256,128]{3,2,1,0:T(8,128)(2,1)} %split_operator.2.refs_1_, f32[4,2,3,128,128]{4,3,2,1,0:T(8,128)} %bitcast.92, f32[8,128]{1,0:T(8,128)S(1)} %get-tuple-element.165.refs_2_.refs_3_, ...), custom_call_target="tpu_custom_call" | custom-call | bytes 393216 | tf_op jit(solution)/shard_map/apply_operator/pallas_call | solution.py:241
  283.2 15.3 %apply_operator.52 = (f32[3,128,128]{2,1,0:T(8,128)S(1)}, f32[8,128]{1,0:T(8,128)S(1)}) custom-call(s32[288]{0:T(512)S(1)} %reshape.104.refs_0_, bf16[12,24,256,128]{3,2,1,0:T(8,128)(2,1)} %split_operator.2.refs_1_, f32[4,2,3,128,128]{4,3,2,1,0:T(8,128)} %bitcast.94, f32[8,128]{1,0:T(8,128)S(1)} %get-tuple-element.170.refs_2_.refs_3_, ...), custom_call_target="tpu_custom_call" | custom-call | bytes 393216 | tf_op jit(solution)/shard_map/apply_operator/pallas_call | solution.py:241
  300.4 15.2 %apply_operator.53 = (f32[3,128,128]{2,1,0:T(8,128)S(1)}, f32[8,128]{1,0:T(8,128)S(1)}) custom-call(s32[288]{0:T(512)S(1)} %reshape.109.refs_0_, bf16[12,24,256,128]{3,2,1,0:T(8,128)(2,1)} %split_operator.3.refs_3_.refs_1_, f32[4,2,3,128,128]{4,3,2,1,0:T(8,128)} %bitcast.91, f32[8,128]{1,0:T(8,128)S(1)} %get-tuple-element.174.refs_3_), custom_call_target="tpu_custom_call" | custom-call | bytes 393216 | tf_op jit(solution)/shard_map/apply_operator/pallas_call | solution.py:241
  316.4 15.3 %apply_operator.54 = (f32[3,128,128]{2,1,0:T(8,128)S(1)}, f32[8,128]{1,0:T(8,128)S(1)}) custom-call(s32[288]{0:T(512)S(1)} %reshape.104.refs_0_, bf16[12,24,256,128]{3,2,1,0:T(8,128)(2,1)} %split_operator.2.refs_1_, f32[4,2,3,128,128]{4,3,2,1,0:T(8,128)} %bitcast.96, f32[8,128]{1,0:T(8,128)S(1)} %get-tuple-element.175.refs_2_.refs_3_, ...), custom_call_target="tpu_custom_call" | custom-call | bytes 393216 | tf_op jit(solution)/shard_map/apply_operator/pallas_call | solution.py:241
  350.6 15.3 %apply_operator.56 = (f32[3,128,128]{2,1,0:T(8,128)S(1)}, f32[8,128]{1,0:T(8,128)S(1)}) custom-call(s32[288]{0:T(512)S(1)} %reshape.104.refs_0_, bf16[12,24,256,128]{3,2,1,0:T(8,128)(2,1)} %split_operator.2.refs_1_, f32[4,2,3,128,128]{4,3,2,1,0:T(8,128)} %bitcast.98, f32[8,128]{1,0:T(8,128)S(1)} %get-tuple-element.180.refs_2_.refs_3_, ...), custom_call_target="tpu_custom_call" | custom-call | bytes 393216 | tf_op jit(solution)/shard_map/apply_operator/pallas_call | solution.py:241
  383.8 15.3 %apply_operator.58 = (f32[3,128,128]{2,1,0:T(8,128)S(1)}, f32[8,128]{1,0:T(8,128)S(1)}) custom-call(s32[288]{0:T(512)S(1)} %reshape.104.refs_0_, bf16[12,24,256,128]{3,2,1,0:T(8,128)(2,1)} %split_operator.2.refs_1_, f32[4,2,3,128,128]{4,3,2,1,0:T(8,128)} %bitcast.100, f32[8,128]{1,0:T(8,128)S(1)} %get-tuple-element.186.refs_2_.refs_3_, ...), custom_call_target="tpu_custom_call" | custom-call | bytes 393216 | tf_op jit(solution)/shard_map/apply_operator/pallas_call | solution.py:241
  416.9 15.3 %apply_operator.60 = (f32[3,128,128]{2,1,0:T(8,128)S(1)}, f32[8,128]{1,0:T(8,128)S(1)}) custom-call(s32[288]{0:T(512)S(1)} %reshape.104.refs_0_, bf16[12,24,256,128]{3,2,1,0:T(8,128)(2,1)} %split_operator.2.refs_1_, f32[4,2,3,128,128]{4,3,2,1,0:T(8,128)} %bitcast.102, f32[8,128]{1,0:T(8,128)S(1)} %get-tuple-element.191.refs_2_.refs_3_, ...), custom_call_target="tpu_custom_call" | custom-call | bytes 393216 | tf_op jit(solution)/shard_map/apply_operator/pallas_call | solution.py:241
  434.1 15.2 %apply_operator.61 = (f32[3,128,128]{2,1,0:T(8,128)S(1)}, f32[8,128]{1,0:T(8,128)S(1)}) custom-call(s32[288]{0:T(512)S(1)} %reshape.109.refs_0_, bf16[12,24,256,128]{3,2,1,0:T(8,128)(2,1)} %split_operator.3.refs_3_.refs_1_, f32[4,2,3,128,128]{4,3,2,1,0:T(8,128)} %bitcast.99, f32[8,128]{1,0:T(8,128)S(1)} %get-tuple-element.195.refs_3_), custom_call_target="tpu_custom_call" | custom-call | bytes 393216 | tf_op jit(solution)/shard_map/apply_operator/pallas_call | solution.py:241
  450.1 15.3 %apply_operator.62 = (f32[3,128,128]{2,1,0:T(8,128)S(1)}, f32[8,128]{1,0:T(8,128)S(1)}) custom-call(s32[288]{0:T(512)S(1)} %reshape.104.refs_0_, bf16[12,24,256,128]{3,2,1,0:T(8,128)(2,1)} %split_operator.2.refs_1_, f32[4,2,3,128,128]{4,3,2,1,0:T(8,128)} %bitcast.106, f32[8,128]{1,0:T(8,128)S(1)} %get-tuple-element.196.refs_2_.refs_3_, ...), custom_call_target="tpu_custom_call" | custom-call | bytes 393216 | tf_op jit(solution)/shard_map/apply_operator/pallas_call | solution.py:241
  467.2 15.2 %apply_operator.63 = (f32[3,128,128]{2,1,0:T(8,128)S(1)}, f32[8,128]{1,0:T(8,128)S(1)}) custom-call(s32[288]{0:T(512)S(1)} %reshape.109.refs_0_, bf16[12,24,256,128]{3,2,1,0:T(8,128)(2,1)} %split_operator.3.refs_3_.refs_1_, f32[4,2,3,128,128]{4,3,2,1,0:T(8,128)} %bitcast.101, f32[8,128]{1,0:T(8,128)S(1)} %get-tuple-element.200.refs_3_), custom_call_target="tpu_custom_call" | custom-call | bytes 393216 | tf_op jit(solution)/shard_map/apply_operator/pallas_call | solution.py:241
  484.1 15.3 %apply_operator.64 = (f32[3,128,128]{2,1,0:T(8,128)S(1)}, f32[8,128]{1,0:T(8,128)S(1)}) custom-call(s32[288]{0:T(512)S(1)} %reshape.104.refs_0_, bf16[12,24,256,128]{3,2,1,0:T(8,128)(2,1)} %split_operator.2.refs_1_, f32[4,2,3,128,128]{4,3,2,1,0:T(8,128)} %bitcast.104, f32[8,128]{1,0:T(8,128)S(1)} %get-tuple-element.201.refs_2_.refs_3_, ...), custom_call_target="tpu_custom_call" | custom-call | bytes 393216 | tf_op jit(solution)/shard_map/apply_operator/pallas_call | solution.py:241
  499.4 15.2 %apply_operator.65 = (f32[3,128,128]{2,1,0:T(8,128)S(1)}, f32[8,128]{1,0:T(8,128)S(1)}) custom-call(s32[288]{0:T(512)S(1)} %reshape.109.refs_0_, bf16[12,24,256,128]{3,2,1,0:T(8,128)(2,1)} %split_operator.3.refs_3_.refs_1_, f32[4,2,3,128,128]{4,3,2,1,0:T(8,128)} %bitcast.103, f32[8,128]{1,0:T(8,128)S(1)} %get-tuple-element.204.refs_3_), custom_call_target="tpu_custom_call" | custom-call | bytes 393216 | tf_op jit(solution)/shard_map/apply_operator/pallas_call | solution.py:241
  516.1 15.3 %apply_operator.66 = (f32[3,128,128]{2,1,0:T(8,128)S(1)}, f32[8,128]{1,0:T(8,128)S(1)}) custom-call(s32[288]{0:T(512)S(1)} %reshape.104.refs_0_, bf16[12,24,256,128]{3,2,1,0:T(8,128)(2,1)} %split_operator.2.refs_1_, f32[4,2,3,128,128]{4,3,2,1,0:T(8,128)} %bitcast.88, f32[8,128]{1,0:T(8,128)S(1)} %get-tuple-element.205.refs_1_.refs_3_, ...), custom_call_target="tpu_custom_call" | custom-call | bytes 393216 | tf_op jit(solution)/shard_map/apply_operator/pallas_call | solution.py:241
  531.4 15.2 %apply_operator.67 = (f32[3,128,128]{2,1,0:T(8,128)S(1)}, f32[8,128]{1,0:T(8,128)S(1)}) custom-call(s32[288]{0:T(512)S(1)} %reshape.109.refs_0_, bf16[12,24,256,128]{3,2,1,0:T(8,128)(2,1)} %split_operator.3.refs_3_.refs_1_, f32[4,2,3,128,128]{4,3,2,1,0:T(8,128)} %bitcast.107, f32[8,128]{1,0:T(8,128)S(1)} %get-tuple-element.209.refs_3_), custom_call_target="tpu_custom_call" | custom-call | bytes 393216 | tf_op jit(solution)/shard_map/apply_operator/pallas_call | solution.py:241
  548.1 15.3 %apply_operator.68 = (f32[3,128,128]{2,1,0:T(8,128)S(1)}, f32[8,128]{1,0:T(8,128)S(1)}) custom-call(s32[288]{0:T(512)S(1)} %reshape.104.refs_0_, bf16[12,24,256,128]{3,2,1,0:T(8,128)(2,1)} %split_operator.2.refs_1_, f32[4,2,3,128,128]{4,3,2,1,0:T(8,128)} %bitcast.112, f32[8,128]{1,0:T(8,128)S(1)} %get-tuple-element.210.refs_1_.refs_3_, ...), custom_call_target="tpu_custom_call" | custom-call | bytes 393216 | tf_op jit(solution)/shard_map/apply_operator/pallas_call | solution.py:241
  563.4 15.2 %apply_operator.69 = (f32[3,128,128]{2,1,0:T(8,128)S(1)}, f32[8,128]{1,0:T(8,128)S(1)}) custom-call(s32[288]{0:T(512)S(1)} %reshape.109.refs_0_, bf16[12,24,256,128]{3,2,1,0:T(8,128)(2,1)} %split_operator.3.refs_3_.refs_1_, f32[4,2,3,128,128]{4,3,2,1,0:T(8,128)} %bitcast.105, f32[8,128]{1,0:T(8,128)S(1)} %get-tuple-element.216.refs_3_), custom_call_target="tpu_custom_call" | custom-call | bytes 393216 | tf_op jit(solution)/shard_map/apply_operator/pallas_call | solution.py:241
  587.0 15.2 %apply_operator.70 = (f32[3,128,128]{2,1,0:T(8,128)S(1)}, f32[8,128]{1,0:T(8,128)S(1)}) custom-call(s32[288]{0:T(512)S(1)} %reshape.104.refs_0_, bf16[12,24,256,128]{3,2,1,0:T(8,128)(2,1)} %split_operator.2.refs_1_, f32[4,2,3,128,128]{4,3,2,1,0:T(8,128)} %bitcast.108, f32[8,128]{1,0:T(8,128)S(1)} %get-tuple-element.217.refs_2_.refs_3_, ...), custom_call_target="tpu_custom_call" | custom-call | bytes 393216 | tf_op jit(solution)/shard_map/apply_operator/pallas_call | solution.py:241
  602.3 15.2 %apply_operator.71 = (f32[3,128,128]{2,1,0:T(8,128)S(1)}, f32[8,128]{1,0:T(8,128)S(1)}) custom-call(s32[288]{0:T(512)S(1)} %reshape.109.refs_0_, bf16[12,24,256,128]{3,2,1,0:T(8,128)(2,1)} %split_operator.3.refs_3_.refs_1_, f32[4,2,3,128,128]{4,3,2,1,0:T(8,128)} %bitcast.89, f32[8,128]{1,0:T(8,128)S(1)} %get-tuple-element.221.refs_3_), custom_call_target="tpu_custom_call" | custom-call | bytes 393216 | tf_op jit(solution)/shard_map/apply_operator/pallas_call | solution.py:241
  911.2 15.3 %apply_operator.83 = (f32[3,128,128]{2,1,0:T(8,128)S(1)}, f32[8,128]{1,0:T(8,128)}) custom-call(s32[288]{0:T(512)S(1)} %reshape.104.refs_0_, bf16[12,24,256,128]{3,2,1,0:T(8,128)(2,1)} %split_operator.2.refs_1_, f32[4,2,3,128,128]{4,3,2,1,0:T(8,128)} %bitcast.121, f32[8,128]{1,0:T(8,128)S(1)} %get-tuple-element.279.refs_3_), custom_call_target="tpu_custom_call" | custom-call | bytes 393216 | tf_op jit(solution)/shard_map/apply_operator/pallas_call | solution.py:241
  (306 shorter events, 539.2 us)
Async XLA Ops:
  19.4 66.0 %all-gather.59.cloned.1.call-start = ((), (), s32[]{:S(2)}) async-start(), calls=%async_computation.1 | async-start | bytes 1769472 | tf_op jit(solution)/shard_map/all_gather | solution.py:316
  54.8 74.8 %collective-permute-start.4 = (f32[12,12,128,128]{3,2,1,0:T(8,128)}, f32[12,12,128,128]{3,2,1,0:T(8,128)}, u32[]{:S(2)}, u32[]{:S(2)}) collective-permute-start(f32[12,12,128,128]{3,2,1,0:T(8,128)} %other_half.3), channel_id=1, source_target_pairs={{0,4},{4,0},{1,5},{5,1},{2,6},{6,2},{3,7},{7,3},{8,12},{12,8},{9,1... | collective-permute-start | bytes 28311560 | tf_op jit(solution)/shard_map/ppermute | solution.py:296
  55.8 91.5 %all-gather.61.cloned.1.call-start = ((), (), s32[]{:S(2)}) async-start(), calls=%async_computation.2 | async-start | bytes 1769472 | tf_op jit(solution)/shard_map/all_gather | solution.py:316
  109.4 73.6 %all-gather.65.cloned.1.call-start = ((), (), s32[]{:S(2)}) async-start(), calls=%async_computation.4 | async-start | bytes 1769472 | tf_op jit(solution)/shard_map/all_gather | solution.py:316
  147.2 69.7 %all-gather.63.cloned.1.call-start = ((), (), s32[]{:S(2)}) async-start(), calls=%async_computation.3 | async-start | bytes 1769472 | tf_op jit(solution)/shard_map/all_gather | solution.py:316
  182.9 67.1 %all-gather.69.cloned.1.call-start = ((), (), s32[]{:S(2)}) async-start(), calls=%async_computation.6 | async-start | bytes 1769472 | tf_op jit(solution)/shard_map/all_gather | solution.py:316
  216.6 66.6 %all-gather.67.cloned.1.call-start = ((), (), s32[]{:S(2)}) async-start(), calls=%async_computation.5 | async-start | bytes 1769472 | tf_op jit(solution)/shard_map/all_gather | solution.py:316
  250.0 66.4 %all-gather.73.cloned.1.call-start = ((), (), s32[]{:S(2)}) async-start(), calls=%async_computation.8 | async-start | bytes 1769472 | tf_op jit(solution)/shard_map/all_gather | solution.py:316
  283.2 67.5 %all-gather.71.cloned.1.call-start = ((), (), s32[]{:S(2)}) async-start(), calls=%async_computation.7 | async-start | bytes 1769472 | tf_op jit(solution)/shard_map/all_gather | solution.py:316
  316.3 67.5 %all-gather.77.cloned.1.call-start = ((), (), s32[]{:S(2)}) async-start(), calls=%async_computation.10 | async-start | bytes 1769472 | tf_op jit(solution)/shard_map/all_gather | solution.py:316
  350.2 66.8 %all-gather.75.cloned.1.call-start = ((), (), s32[]{:S(2)}) async-start(), calls=%async_computation.9 | async-start | bytes 1769472 | tf_op jit(solution)/shard_map/all_gather | solution.py:316
  383.7 66.4 %all-gather.81.cloned.1.call-start = ((), (), s32[]{:S(2)}) async-start(), calls=%async_computation.12 | async-start | bytes 1769472 | tf_op jit(solution)/shard_map/all_gather | solution.py:316
  416.9 67.2 %all-gather.79.cloned.1.call-start = ((), (), s32[]{:S(2)}) async-start(), calls=%async_computation.11 | async-start | bytes 1769472 | tf_op jit(solution)/shard_map/all_gather | solution.py:316
  450.0 66.0 %all-gather.85.cloned.1.call-start = ((), (), s32[]{:S(2)}) async-start(), calls=%async_computation.14 | async-start | bytes 1769472 | tf_op jit(solution)/shard_map/all_gather | solution.py:316
  483.8 64.2 %all-gather.83.cloned.1.call-start = ((), (), s32[]{:S(2)}) async-start(), calls=%async_computation.13 | async-start | bytes 1769472 | tf_op jit(solution)/shard_map/all_gather | solution.py:316
  516.0 71.0 %all-gather.89.cloned.1.call-start = ((), (), s32[]{:S(2)}) async-start(), calls=%async_computation.16 | async-start | bytes 1769472 | tf_op jit(solution)/shard_map/all_gather | solution.py:316
  548.0 78.0 %all-gather.87.cloned.1.call-start = ((), (), s32[]{:S(2)}) async-start(), calls=%async_computation.15 | async-start | bytes 1769472 | tf_op jit(solution)/shard_map/all_gather | solution.py:316
  586.9 62.8 %all-gather.93.cloned.1.call-start = ((), (), s32[]{:S(2)}) async-start(), calls=%async_computation.18 | async-start | bytes 1769472 | tf_op jit(solution)/shard_map/all_gather | solution.py:316
  674.5 53.9 %all-gather.95.cloned.1.call-start = ((), (), s32[]{:S(2)}) async-start(), calls=%async_computation.19 | async-start | bytes 1769472 | tf_op jit(solution)/shard_map/all_gather | solution.py:316
  701.4 53.2 %all-gather.99.cloned.1.call-start = ((), (), s32[]{:S(2)}) async-start(), calls=%async_computation.21 | async-start | bytes 1769472 | tf_op jit(solution)/shard_map/all_gather | solution.py:316
  726.9 54.0 %all-gather.101.cloned.1.call-start = ((), (), s32[]{:S(2)}) async-start(), calls=%async_computation.22 | async-start | bytes 1769472 | tf_op jit(solution)/shard_map/all_gather | solution.py:316
  753.8 53.2 %all-gather.103.cloned.1.call-start = ((), (), s32[]{:S(2)}) async-start(), calls=%async_computation.23 | async-start | bytes 1769472 | tf_op jit(solution)/shard_map/all_gather | solution.py:316
  779.4 53.6 %all-gather.105.cloned.1.call-start = ((), (), s32[]{:S(2)}) async-start(), calls=%async_computation.24 | async-start | bytes 1769472 | tf_op jit(solution)/shard_map/all_gather | solution.py:316
  858.5 52.7 %all-gather.111.cloned.1.call-start = ((), (), s32[]{:S(2)}) async-start(), calls=%async_computation.27 | async-start | bytes 1769472 | tf_op jit(solution)/shard_map/all_gather | solution.py:316
  (79 other events, 1168.4 us)
Sparse Core Ops, SparseCore 0:
  19.6 27.4 all-gather.56
  55.9 24.5 all-gather.58
  109.5 25.6 all-gather.60
  147.4 24.5 all-gather.64
  183.0 22.7 all-gather.62
  216.7 22.7 all-gather.68
  250.1 22.7 all-gather.66
  283.3 22.7 all-gather.72
  316.5 22.7 all-gather.70
  350.3 22.7 all-gather.76
  383.9 22.7 all-gather.74
  484.0 22.7 all-gather.84
  587.0 22.8 all-gather.86
  625.9 23.7 all-gather.92
  651.3 24.5 all-gather.90
  677.4 24.6 all-gather.96
  703.7 24.5 all-gather.94
  730.0 24.5 all-gather.98
  756.3 24.5 all-gather.100
  782.4 24.5 all-gather.102
  808.7 24.3 all-gather.104
  834.5 24.4 all-gather.106
  860.5 24.3 all-gather.108
  886.6 24.5 all-gather.110
  (4 shorter events, 89.9 us)

commit v9 on v7

--- a/solution.py
+++ b/solution.py
@@ -132,12 +132,12 @@
     )(place, values, other, in_hbm(after))
 
 
-def apply_kernel(pack, index_ref, parts_ref, gathered_ref, *refs):
+def apply_kernel(pack, index_ref, parts_ref, own_ref, other_ref, *refs):
     result_ref, token_ref, slots, tiles, arrived = refs[-5:]
     row, rows = pl.program_id(0), pl.num_programs(0)
     count, picks, twice, _ = slots.shape
     size = twice // 2
-    pieces, halves, groups, _, lanes = gathered_ref.shape
+    pieces, groups, _, lanes = own_ref.shape
     span = lanes // pack
 
     def fetch(which):
@@ -159,10 +159,10 @@
         middle = lanes // 2
         lane = lax.broadcasted_iota(jnp.int32, (size, lanes), 1) // span % max(1, pack // 2)
         masks = [(lane == q).astype(jnp.float32).astype(jnp.bfloat16) for q in range(pack // 2)]
-        for half in range(halves):
+        for half, ref in enumerate((own_ref, other_ref)):
             for piece in range(pieces):
                 for group in range(groups):
-                    tile = gathered_ref[piece, half, group]
+                    tile = ref[piece, group]
                     high = tile.astype(jnp.bfloat16)
                     low = (tile - high.astype(jnp.float32)).astype(jnp.bfloat16)
                     base = ((half * pieces + piece) * groups + group) * pack
@@ -194,19 +194,21 @@
 
 def apply_operator(parts, index, pack, gathered, after):
     rows, picks, twice, depth = parts.shape
-    pieces, halves, groups, size, lanes = gathered.shape
+    pieces, groups, size, lanes = gathered[0].shape
+    whole = pl.BlockSpec(gathered[0].shape, lambda row, *_: (0, 0, 0, 0))
     spec = pltpu.PrefetchScalarGridSpec(
         num_scalar_prefetch=1,
         grid=(rows,),
         in_specs=[
             pl.BlockSpec(memory_space=pltpu.HBM),
-            pl.BlockSpec(gathered.shape, lambda row, *_: (0, 0, 0, 0, 0)),
+            whole,
+            whole,
         ]
         + [pl.BlockSpec(memory_space=pl.ANY)] * len(after),
         out_specs=[pl.BlockSpec((1, size, lanes), lambda row, *_: (row // pack, 0, 0)), TOKEN_SPEC],
         scratch_shapes=[
             pltpu.VMEM((SLOTS, picks, twice, depth), jnp.bfloat16),
-            pltpu.VMEM((halves * pieces * groups * pack, size, lanes * (2 if pack == 1 else 1)), jnp.bfloat16),
+            pltpu.VMEM((2 * pieces * groups * pack, size, lanes * (2 if pack == 1 else 1)), jnp.bfloat16),
             pltpu.SemaphoreType.DMA((SLOTS,)),
         ],
     )
@@ -219,9 +221,9 @@
         grid_spec=spec,
         out_shape=[jax.ShapeDtypeStruct((groups, size, lanes), jnp.float32), TOKEN],
         compiler_params=pltpu.CompilerParams(vmem_limit_bytes=VMEM_BYTES),
-        cost_estimate=pl.CostEstimate(flops=0, bytes_accessed=gathered.size, transcendentals=0),
+        cost_estimate=pl.CostEstimate(flops=0, bytes_accessed=gathered[0].size, transcendentals=0),
         name="apply_operator",
-    )(index, in_hbm(parts), in_hbm(gathered), *after)
+    )(index, in_hbm(parts), *gathered, *after)
 
 
 def sum_kernel(terms, *refs):
@@ -253,7 +255,7 @@
     piece_rows, columns = source.shape
     size = tr_vals.shape[-1]
     blocks = piece_rows // size
-    pack = 4 if blocks % 4 == 0 else 1
+    pack = 2 if blocks % 2 == 0 else 1
     batches, delay = columns // (LANES // pack), DELAY
     length, pieces = lax.axis_size("slab"), lax.axis_size("col")
     last = length - 1
@@ -267,8 +269,7 @@
         own = lax.dynamic_slice_in_dim(columns, place * half, half, 0)
         other = lax.dynamic_slice_in_dim(columns, (1 - place) * half, half, 0)
         group_blocks = pieces * blocks
-        other = lax.ppermute(other, "row", swap) + (1 - place) * group_blocks
-        index = jnp.concatenate([own + place * group_blocks, other], axis=1)
+        index = jnp.concatenate([own, lax.ppermute(other, "row", swap) + group_blocks], axis=1)
         traded = lax.ppermute(other_half(values, place.reshape(1), copy_after), "row", swap)
         return split_operator(values, traded, place.reshape(1), split_after), index.reshape(-1), pack
 
@@ -289,8 +290,8 @@
         )
 
     def gather(piece):
-        gathered = lax.all_gather(piece, ("col", "row"), axis=0)
-        return gathered.reshape((pieces, 2) + piece.shape)
+        gathered = lax.all_gather(piece, "col", axis=0)
+        return gathered, lax.ppermute(gathered, "row", swap)
 
     moments = batches + delay * last
     downs, refls, ups, tokens = [], [], [], []
@@ -311,17 +312,15 @@
 
     piece, _ = incident_of(0)
     gathered = [gather(piece)]
-    trans = operator(tr_vals[0, 0, 0], tr_cols[0, 0, 0], piece, gathered[0])
+    trans = operator(tr_vals[0, 0, 0], tr_cols[0, 0, 0], piece, gathered[0][0])
     lag = max(0, min(delay, batches - 2))
-    copied_after, ready = in_hbm(gathered[0]), []
+    copied_after, ready = piece, []
     for moment in range(2 * moments):
         after = tokens[-1:]
         if moment + 1 < 2 * moments:
             piece, token = incident_of(moment + 1, ready if moment == lag else [])
             gathered.append(gather(piece))
             after = after + [token]
-        if moment == 0:
-            after = after + [in_hbm(gathered[1])]
         product, token = apply_operator(*trans, gathered[moment], after)
         (downs if moment < moments else ups).append(product)
         if moment == max(0, lag - 1):

time: 858 us -> 830 us (0.967)
  Pallas kernels: 587 us -> 374 us
  waiting for transfers between devices: 184 us -> 342 us
  local copies, waits for them, and re-layouts: 11 us -> 43.3 us
    pallas_call x42 -> x30, Pallas kernels: 515 us -> 305 us  [apply_operator(): pl.pallas_call(kernel, grid_spec=spec, out_shape=[jax.ShapeDtypeStruct((g...]
    all_gather x28 -> x20, waiting for transfers between devices: 79.3 us -> 197 us  [gather(): gathered = lax.all_gather(piece, 'col', axis=0)]
    ppermute x2 -> x22, waiting for transfers between devices: 11.6 us -> 64.1 us  [the longest x20 61.3 us: gather(): return (gathered, lax.ppermute(gathered, 'row', swap))]
    unnamed x97 -> x208, local copies, waits for them, and re-layouts: 9.5 us -> 40.1 us
    ppermute x24 -> x16, waiting for transfers between devices: 92.4 us -> 80.7 us  [passed_along(): lax.ppermute(value, axis, [(source, source + steps) for source in range(i...]
    ppermute x24 -> x16, starting transfers between devices: 45.3 us -> 38.9 us  [passed_along(): lax.ppermute(value, axis, [(source, source + steps) for source in range(i...]
    pallas_call x28 -> x20, Pallas kernels: 19 us -> 15.9 us  [sum_of(): pl.pallas_call(kernel, grid=(1,), in_specs=[whole] * len(terms) + [pl.Blo...]
  transfers between devices with their start and end apart: 56 -> 60, of which waited for: 26 -> 45; matrix products, arithmetic and copies ran while one was open for 0% -> 1% of each run, Pallas kernels for 66% -> 43%
where the time goes in v9:
time: 830 us; the launch traced here: 820 us
  Pallas kernels  374 us (45%)
  waiting for transfers between devices  342 us (41%)
  local copies, waits for them, and re-layouts  43.3 us (5%)
  starting transfers between devices  41.6 us (5%)
  between operations  15.6 us (2%)
    pallas_call x30, Pallas kernels, apply_operator(): pl.pallas_call(kernel, grid_spec=spec, out_shape=[jax.ShapeDtypeStruct((g...  305 us
    all_gather x20, waiting for transfers between devices, gather(): gathered = lax.all_gather(piece, 'col', axis=0)  197 us
    ppermute x16, waiting for transfers between devices, passed_along(): lax.ppermute(value, axis, [(source, source + steps) for source in range(i...  80.7 us
    ppermute x20, waiting for transfers between devices, gather(): return (gathered, lax.ppermute(gathered, 'row', swap))  61.3 us
    unnamed x208, local copies, waits for them, and re-layouts  40.1 us
    ppermute x16, starting transfers between devices, passed_along(): lax.ppermute(value, axis, [(source, source + steps) for source in range(i...  38.9 us
    pallas_call x2, Pallas kernels, split_operator(): pl.pallas_call(split_kernel, grid_spec=spec, out_shape=jax.ShapeDtypeStru...  34.1 us
  transfers between devices with their start and end apart: 60, of which 45 were waited for; matrix products, arithmetic and copies ran while one was open for 1% of the time, Pallas kernels for 43%

profile of v9, /device:TPU:0, one launch (start us, length us, event | category | flops | bytes accessed | tf_op | source)
XLA Modules:
  0.0 819.9 jit_solution(357970382270204164)
XLA Ops:
  28.1 39.0 %all-gather.41.cloned.1.call-done = f32[24,128,128]{2,1,0:T(8,128)} async-done(((f32[6,128,128]{2,1,0:T(8,128)}), f32[24,128,128]{2,1,0:T(8,128)}) %all-gather.41.cloned.1.call-update) | async-done | bytes 1572880 | tf_op jit(solution)/shard_map/all_gather | solution.py:293
  70.8 17.1 %split_operator.2.refs_1_ = bf16[12,24,256,128]{3,2,1,0:T(8,128)(2,1)} custom-call(s32[1]{0:T(128)} %bitcast.2.place_ref, f32[24,12,128,128]{3,2,1,0:T(8,128)} %bitcast.102, f32[12,12,128,128]{3,2,1,0:T(8,128)} %collective-permute-done.1.other_ref, f32[4,6,128,128]{3,2,1,0:T(8,128)} %bitcast.50), custom_call_target="tpu_custom_call" | custom-call | tf_op jit(solution)/shard_map/split_operator/pallas_call | solution.py:126
  116.5 10.1 %apply_operator.31 = (f32[6,128,128]{2,1,0:T(8,128)S(1)}, f32[8,128]{1,0:T(8,128)S(1)}) custom-call(s32[288]{0:T(512)S(1)} %reshape.16.refs_0_, bf16[12,24,256,128]{3,2,1,0:T(8,128)(2,1)} %split_operator.2.refs_1_, f32[4,6,128,128]{3,2,1,0:T(8,128)S(1)} %bitcast.54, f32[4,6,128,128]{3,2,1,0:T(8,128)S(1)} %collective-permute-done.5.refs_3_, ...), custom_call_target="tpu_custom_call" | custom-call | bytes 393216 | tf_op jit(solution)/shard_map/apply_operator/pallas_call | solution.py:219
  131.7 17.0 %split_operator.3.refs_3_.refs_1_ = bf16[12,24,256,128]{3,2,1,0:T(8,128)(2,1)} custom-call(s32[1]{0:T(128)} %bitcast.2.place_ref, f32[24,12,128,128]{3,2,1,0:T(8,128)} %bitcast.104, f32[12,12,128,128]{3,2,1,0:T(8,128)} %collective-permute-done.7.other_ref, f32[8,128]{1,0:T(8,128)} %copy-done.96), custom_call_target="tpu_custom_call" | custom-call | tf_op jit(solution)/shard_map/split_operator/pallas_call | solution.py:126
  155.3 10.8 %apply_operator.32 = (f32[6,128,128]{2,1,0:T(8,128)}, f32[8,128]{1,0:T(8,128)S(1)}) custom-call(s32[288]{0:T(512)S(1)} %reshape.16.refs_0_, bf16[12,24,256,128]{3,2,1,0:T(8,128)(2,1)} %split_operator.2.refs_1_, f32[4,6,128,128]{3,2,1,0:T(8,128)S(1)} %bitcast.57, f32[4,6,128,128]{3,2,1,0:T(8,128)S(1)} %collective-permute-done.4.refs_3_, ...), custom_call_target="tpu_custom_call" | custom-call | bytes 393216 | tf_op jit(solution)/shard_map/apply_operator/pallas_call | solution.py:219
  193.5 10.4 %apply_operator.34 = (f32[6,128,128]{2,1,0:T(8,128)S(1)}, f32[8,128]{1,0:T(8,128)S(1)}) custom-call(s32[288]{0:T(512)S(1)} %reshape.16.refs_0_, bf16[12,24,256,128]{3,2,1,0:T(8,128)(2,1)} %split_operator.2.refs_1_, f32[4,6,128,128]{3,2,1,0:T(8,128)S(1)} %bitcast.60, f32[4,6,128,128]{3,2,1,0:T(8,128)S(1)} %collective-permute-done.11.refs_3_, ...), custom_call_target="tpu_custom_call" | custom-call | bytes 393216 | tf_op jit(solution)/shard_map/apply_operator/pallas_call | solution.py:219
  228.0 10.4 %apply_operator.36 = (f32[6,128,128]{2,1,0:T(8,128)S(1)}, f32[8,128]{1,0:T(8,128)S(1)}) custom-call(s32[288]{0:T(512)S(1)} %reshape.16.refs_0_, bf16[12,24,256,128]{3,2,1,0:T(8,128)(2,1)} %split_operator.2.refs_1_, f32[4,6,128,128]{3,2,1,0:T(8,128)S(1)} %bitcast.66, f32[4,6,128,128]{3,2,1,0:T(8,128)S(1)} %collective-permute-done.10.refs_3_, ...), custom_call_target="tpu_custom_call" | custom-call | bytes 393216 | tf_op jit(solution)/shard_map/apply_operator/pallas_call | solution.py:219
  266.0 10.1 %apply_operator.38 = (f32[6,128,128]{2,1,0:T(8,128)S(1)}, f32[8,128]{1,0:T(8,128)S(1)}) custom-call(s32[288]{0:T(512)S(1)} %reshape.16.refs_0_, bf16[12,24,256,128]{3,2,1,0:T(8,128)(2,1)} %split_operator.2.refs_1_, f32[4,6,128,128]{3,2,1,0:T(8,128)S(1)} %bitcast.69, f32[4,6,128,128]{3,2,1,0:T(8,128)S(1)} %collective-permute-done.15.refs_3_, ...), custom_call_target="tpu_custom_call" | custom-call | bytes 393216 | tf_op jit(solution)/shard_map/apply_operator/pallas_call | solution.py:219
  341.1 10.5 %apply_operator.42 = (f32[6,128,128]{2,1,0:T(8,128)S(1)}, f32[8,128]{1,0:T(8,128)S(1)}) custom-call(s32[288]{0:T(512)S(1)} %reshape.16.refs_0_, bf16[12,24,256,128]{3,2,1,0:T(8,128)(2,1)} %split_operator.2.refs_1_, f32[4,6,128,128]{3,2,1,0:T(8,128)S(1)} %bitcast.78, f32[4,6,128,128]{3,2,1,0:T(8,128)S(1)} %collective-permute-done.19.refs_3_, ...), custom_call_target="tpu_custom_call" | custom-call | bytes 393216 | tf_op jit(solution)/shard_map/apply_operator/pallas_call | solution.py:219
  378.7 10.1 %apply_operator.44 = (f32[6,128,128]{2,1,0:T(8,128)S(1)}, f32[8,128]{1,0:T(8,128)S(1)}) custom-call(s32[288]{0:T(512)S(1)} %reshape.16.refs_0_, bf16[12,24,256,128]{3,2,1,0:T(8,128)(2,1)} %split_operator.2.refs_1_, f32[4,6,128,128]{3,2,1,0:T(8,128)S(1)} %bitcast.75, f32[4,6,128,128]{3,2,1,0:T(8,128)S(1)} %collective-permute-done.18.refs_3_, ...), custom_call_target="tpu_custom_call" | custom-call | bytes 393216 | tf_op jit(solution)/shard_map/apply_operator/pallas_call | solution.py:219
  400.5 10.2 %all-gather.61.cloned.1.call-done = f32[24,128,128]{2,1,0:T(8,128)} async-done(((f32[6,128,128]{2,1,0:T(8,128)}), f32[24,128,128]{2,1,0:T(8,128)}) %all-gather.61.cloned.1.call-update) | async-done | bytes 1572880 | tf_op jit(solution)/shard_map/all_gather | solution.py:293
  415.7 10.4 %apply_operator.46 = (f32[6,128,128]{2,1,0:T(8,128)S(1)}, f32[8,128]{1,0:T(8,128)S(1)}) custom-call(s32[288]{0:T(512)S(1)} %reshape.16.refs_0_, bf16[12,24,256,128]{3,2,1,0:T(8,128)(2,1)} %split_operator.2.refs_1_, f32[4,6,128,128]{3,2,1,0:T(8,128)S(1)} %bitcast.63, f32[4,6,128,128]{3,2,1,0:T(8,128)S(1)} %collective-permute-done.22.refs_3_, ...), custom_call_target="tpu_custom_call" | custom-call | bytes 393216 | tf_op jit(solution)/shard_map/apply_operator/pallas_call | solution.py:219
  453.9 10.8 %apply_operator.48 = (f32[6,128,128]{2,1,0:T(8,128)}, f32[8,128]{1,0:T(8,128)S(1)}) custom-call(s32[288]{0:T(512)S(1)} %reshape.16.refs_0_, bf16[12,24,256,128]{3,2,1,0:T(8,128)(2,1)} %split_operator.2.refs_1_, f32[4,6,128,128]{3,2,1,0:T(8,128)S(1)} %bitcast.100, f32[4,6,128,128]{3,2,1,0:T(8,128)S(1)} %collective-permute-done.21.refs_3_, ...), custom_call_target="tpu_custom_call" | custom-call | bytes 393216 | tf_op jit(solution)/shard_map/apply_operator/pallas_call | solution.py:219
  528.4 10.1 %apply_operator.52 = (f32[6,128,128]{2,1,0:T(8,128)S(1)}, f32[8,128]{1,0:T(8,128)S(1)}) custom-call(s32[288]{0:T(512)S(1)} %reshape.16.refs_0_, bf16[12,24,256,128]{3,2,1,0:T(8,128)(2,1)} %split_operator.2.refs_1_, f32[4,6,128,128]{3,2,1,0:T(8,128)S(1)} %bitcast.86, f32[4,6,128,128]{3,2,1,0:T(8,128)S(1)} %collective-permute-done.24.refs_3_, ...), custom_call_target="tpu_custom_call" | custom-call | bytes 393216 | tf_op jit(solution)/shard_map/apply_operator/pallas_call | solution.py:219
  539.9 11.7 %collective-permute-done.27.refs_1_ = f32[6,128,128]{2,1,0:T(8,128)S(1)} collective-permute-done((f32[6,128,128]{2,1,0:T(8,128)S(1)}, f32[6,128,128]{2,1,0:T(8,128)S(1)}, u32[]{:S(2)}, u32[]{:S(2)}) %collective-permute-start.27) | collective-permute-done | bytes 393248 | tf_op jit(solution)/shard_map/ppermute | solution.py:23
  577.2 11.7 %collective-permute-done.30.refs_1_ = f32[6,128,128]{2,1,0:T(8,128)S(1)} collective-permute-done((f32[6,128,128]{2,1,0:T(8,128)S(1)}, f32[6,128,128]{2,1,0:T(8,128)S(1)}, u32[]{:S(2)}, u32[]{:S(2)}) %collective-permute-start.30) | collective-permute-done | bytes 393248 | tf_op jit(solution)/shard_map/ppermute | solution.py:23
  614.6 11.7 %collective-permute-done.31.refs_1_ = f32[6,128,128]{2,1,0:T(8,128)S(1)} collective-permute-done((f32[6,128,128]{2,1,0:T(8,128)S(1)}, f32[6,128,128]{2,1,0:T(8,128)S(1)}, u32[]{:S(2)}, u32[]{:S(2)}) %collective-permute-start.31) | collective-permute-done | bytes 393248 | tf_op jit(solution)/shard_map/ppermute | solution.py:23
  652.0 11.7 %collective-permute-done.34.refs_1_ = f32[6,128,128]{2,1,0:T(8,128)S(1)} collective-permute-done((f32[6,128,128]{2,1,0:T(8,128)S(1)}, f32[6,128,128]{2,1,0:T(8,128)S(1)}, u32[]{:S(2)}, u32[]{:S(2)}) %collective-permute-start.34) | collective-permute-done | bytes 393248 | tf_op jit(solution)/shard_map/ppermute | solution.py:23
  678.1 10.1 %apply_operator.56 = (f32[6,128,128]{2,1,0:T(8,128)S(1)}, f32[8,128]{1,0:T(8,128)S(1)}) custom-call(s32[288]{0:T(512)S(1)} %reshape.16.refs_0_, bf16[12,24,256,128]{3,2,1,0:T(8,128)(2,1)} %split_operator.2.refs_1_, f32[4,6,128,128]{3,2,1,0:T(8,128)S(1)} %bitcast.96, f32[4,6,128,128]{3,2,1,0:T(8,128)S(1)} %collective-permute-done.32.refs_3_, ...), custom_call_target="tpu_custom_call" | custom-call | bytes 393216 | tf_op jit(solution)/shard_map/apply_operator/pallas_call | solution.py:219
  689.5 11.7 %collective-permute-done.36.refs_1_ = f32[6,128,128]{2,1,0:T(8,128)S(1)} collective-permute-done((f32[6,128,128]{2,1,0:T(8,128)S(1)}, f32[6,128,128]{2,1,0:T(8,128)S(1)}, u32[]{:S(2)}, u32[]{:S(2)}) %collective-permute-start.36) | collective-permute-done | bytes 393248 | tf_op jit(solution)/shard_map/ppermute | solution.py:23
  726.9 11.7 %collective-permute-done.38.refs_1_ = f32[6,128,128]{2,1,0:T(8,128)S(1)} collective-permute-done((f32[6,128,128]{2,1,0:T(8,128)S(1)}, f32[6,128,128]{2,1,0:T(8,128)S(1)}, u32[]{:S(2)}, u32[]{:S(2)}) %collective-permute-start.38) | collective-permute-done | bytes 393248 | tf_op jit(solution)/shard_map/ppermute | solution.py:23
  748.1 37.4 %all-gather.79.cloned.1.call-done = f32[24,128,128]{2,1,0:T(8,128)} async-done(((f32[6,128,128]{2,1,0:T(8,128)}), f32[24,128,128]{2,1,0:T(8,128)}) %all-gather.79.cloned.1.call-update) | async-done | bytes 1572880 | tf_op jit(solution)/shard_map/all_gather | solution.py:293
  787.0 10.2 %apply_operator.58 = (f32[6,128,128]{2,1,0:T(8,128)S(1)}, f32[8,128]{1,0:T(8,128)S(1)}) custom-call(s32[288]{0:T(512)S(1)} %reshape.16.refs_0_, bf16[12,24,256,128]{3,2,1,0:T(8,128)(2,1)} %split_operator.2.refs_1_, f32[4,6,128,128]{3,2,1,0:T(8,128)S(1)} %bitcast.88, f32[4,6,128,128]{3,2,1,0:T(8,128)S(1)} %collective-permute-done.37.refs_3_, ...), custom_call_target="tpu_custom_call" | custom-call | bytes 393216 | tf_op jit(solution)/shard_map/apply_operator/pallas_call | solution.py:219
  799.0 10.5 %apply_operator.59 = (f32[6,128,128]{2,1,0:T(8,128)S(1)}, f32[8,128]{1,0:T(8,128)}) custom-call(s32[288]{0:T(512)S(1)} %reshape.16.refs_0_, bf16[12,24,256,128]{3,2,1,0:T(8,128)(2,1)} %split_operator.2.refs_1_, f32[4,6,128,128]{3,2,1,0:T(8,128)S(1)} %bitcast.81, f32[4,6,128,128]{3,2,1,0:T(8,128)S(1)} %collective-permute-done.39.refs_3_, ...), custom_call_target="tpu_custom_call" | custom-call | bytes 393216 | tf_op jit(solution)/shard_map/apply_operator/pallas_call | solution.py:219
  (394 shorter events, 478.9 us)
Async XLA Ops:
  6.5 60.6 %all-gather.41.cloned.1.call-start = ((), (), s32[]{:S(2)}) async-start(), calls=%async_computation | async-start | bytes 1966080 | tf_op jit(solution)/shard_map/all_gather | solution.py:293
  18.9 51.8 %collective-permute-start.1 = (f32[12,12,128,128]{3,2,1,0:T(8,128)}, f32[12,12,128,128]{3,2,1,0:T(8,128)}, u32[]{:S(2)}, u32[]{:S(2)}) collective-permute-start(f32[12,12,128,128]{3,2,1,0:T(8,128)} %other_half.2), channel_id=1, source_target_pairs={{0,4},{4,0},{1,5},{5,1},{2,6},{6,2},{3,7},{7,3},{8,12},{12,8},{9,1... | collective-permute-start | bytes 28311560 | tf_op jit(solution)/shard_map/ppermute | solution.py:273
  27.1 104.5 %collective-permute-start.7 = (f32[12,12,128,128]{3,2,1,0:T(8,128)}, f32[12,12,128,128]{3,2,1,0:T(8,128)}, u32[]{:S(2)}, u32[]{:S(2)}) collective-permute-start(f32[12,12,128,128]{3,2,1,0:T(8,128)} %other_half.3), channel_id=1, source_target_pairs={{0,4},{4,0},{1,5},{5,1},{2,6},{6,2},{3,7},{7,3},{8,12},{12,8},{9,1... | collective-permute-start | bytes 28311560 | tf_op jit(solution)/shard_map/ppermute | solution.py:273
  27.2 83.7 %all-gather.45.cloned.1.call-start = ((), (), s32[]{:S(2)}) async-start(), calls=%async_computation.2 | async-start | bytes 1966080 | tf_op jit(solution)/shard_map/all_gather | solution.py:293
  28.1 121.5 %all-gather.43.cloned.1.call-start = ((), (), s32[]{:S(2)}) async-start(), calls=%async_computation.1 | async-start | bytes 1966080 | tf_op jit(solution)/shard_map/all_gather | solution.py:293
  110.8 77.5 %all-gather.49.cloned.1.call-start = ((), (), s32[]{:S(2)}) async-start(), calls=%async_computation.4 | async-start | bytes 1966080 | tf_op jit(solution)/shard_map/all_gather | solution.py:293
  127.3 21.4 %collective-permute-start.6 = (f32[6,128,128]{2,1,0:T(8,128)S(1)}, f32[6,128,128]{2,1,0:T(8,128)S(1)}, u32[]{:S(2)}, u32[]{:S(2)}) collective-permute-start(f32[6,128,128]{2,1,0:T(8,128)S(1)} %get-tuple-element.111), channel_id=1, source_target_pairs={{0,8},{8,16},{16,24},{1,9},{9,17},{17,25},{2,10},{10,18},{18,26},{... | collective-permute-start | bytes 1179656 | tf_op jit(solution)/shard_map/ppermute | solution.py:23
  149.5 73.5 %all-gather.47.cloned.1.call-start = ((), (), s32[]{:S(2)}) async-start(), calls=%async_computation.3 | async-start | bytes 1966080 | tf_op jit(solution)/shard_map/all_gather | solution.py:293
  188.2 72.2 %all-gather.53.cloned.1.call-start = ((), (), s32[]{:S(2)}) async-start(), calls=%async_computation.6 | async-start | bytes 1966080 | tf_op jit(solution)/shard_map/all_gather | solution.py:293
  217.0 80.9 %all-gather.51.cloned.1.call-start = ((), (), s32[]{:S(2)}) async-start(), calls=%async_computation.5 | async-start | bytes 1966080 | tf_op jit(solution)/shard_map/all_gather | solution.py:293
  252.7 82.8 %all-gather.57.cloned.1.call-start = ((), (), s32[]{:S(2)}) async-start(), calls=%async_computation.8 | async-start | bytes 1966080 | tf_op jit(solution)/shard_map/all_gather | solution.py:293
  291.2 81.9 %all-gather.55.cloned.1.call-start = ((), (), s32[]{:S(2)}) async-start(), calls=%async_computation.7 | async-start | bytes 1966080 | tf_op jit(solution)/shard_map/all_gather | solution.py:293
  327.4 83.2 %all-gather.61.cloned.1.call-start = ((), (), s32[]{:S(2)}) async-start(), calls=%async_computation.10 | async-start | bytes 1966080 | tf_op jit(solution)/shard_map/all_gather | solution.py:293
  365.9 82.3 %all-gather.59.cloned.1.call-start = ((), (), s32[]{:S(2)}) async-start(), calls=%async_computation.9 | async-start | bytes 1966080 | tf_op jit(solution)/shard_map/all_gather | solution.py:293
  400.4 85.2 %all-gather.65.cloned.1.call-start = ((), (), s32[]{:S(2)}) async-start(), calls=%async_computation.12 | async-start | bytes 1966080 | tf_op jit(solution)/shard_map/all_gather | solution.py:293
  438.3 85.1 %all-gather.63.cloned.1.call-start = ((), (), s32[]{:S(2)}) async-start(), calls=%async_computation.11 | async-start | bytes 1966080 | tf_op jit(solution)/shard_map/all_gather | solution.py:293
  479.9 80.8 %all-gather.69.cloned.1.call-start = ((), (), s32[]{:S(2)}) async-start(), calls=%async_computation.14 | async-start | bytes 1966080 | tf_op jit(solution)/shard_map/all_gather | solution.py:293
  514.5 83.6 %all-gather.67.cloned.1.call-start = ((), (), s32[]{:S(2)}) async-start(), calls=%async_computation.13 | async-start | bytes 1966080 | tf_op jit(solution)/shard_map/all_gather | solution.py:293
  552.3 83.3 %all-gather.73.cloned.1.call-start = ((), (), s32[]{:S(2)}) async-start(), calls=%async_computation.16 | async-start | bytes 1966080 | tf_op jit(solution)/shard_map/all_gather | solution.py:293
  589.7 83.4 %all-gather.71.cloned.1.call-start = ((), (), s32[]{:S(2)}) async-start(), calls=%async_computation.15 | async-start | bytes 1966080 | tf_op jit(solution)/shard_map/all_gather | solution.py:293
  627.1 83.4 %all-gather.75.cloned.1.call-start = ((), (), s32[]{:S(2)}) async-start(), calls=%async_computation.17 | async-start | bytes 1966080 | tf_op jit(solution)/shard_map/all_gather | solution.py:293
  664.6 83.5 %all-gather.77.cloned.1.call-start = ((), (), s32[]{:S(2)}) async-start(), calls=%async_computation.18 | async-start | bytes 1966080 | tf_op jit(solution)/shard_map/all_gather | solution.py:293
  702.0 83.5 %all-gather.79.cloned.1.call-start = ((), (), s32[]{:S(2)}) async-start(), calls=%async_computation.19 | async-start | bytes 1966080 | tf_op jit(solution)/shard_map/all_gather | solution.py:293
  748.1 37.4 %collective-permute-start.37 = (f32[4,6,128,128]{3,2,1,0:T(8,128)}, f32[4,6,128,128]{3,2,1,0:T(8,128)S(1)}, u32[]{:S(2)}, u32[]{:S(2)}) collective-permute-start(f32[4,6,128,128]{3,2,1,0:T(8,128)} %bitcast.87), channel_id=1, source_target_pairs={{0,4},{4,0},{1,5},{5,1},{2,6},{6,2},{3,7},{7,3},{8,12},{12,8},{9,1... | collective-permute-start | bytes 4718600 | tf_op jit(solution)/shard_map/ppermute | solution.py:294
  (138 other events, 1348.3 us)
Sparse Core Ops, SparseCore 0:
  27.3 39.7 all-gather.40
  68.7 35.9 all-gather.44
  110.9 36.9 all-gather.42
  149.6 35.9 all-gather.48
  188.3 34.5 all-gather.46
  224.4 35.9 all-gather.52
  262.0 35.9 all-gather.50
  299.5 35.9 all-gather.56
  337.1 35.9 all-gather.54
  374.5 36.0 all-gather.60
  412.2 35.9 all-gather.58
  449.6 35.9 all-gather.64
  487.2 36.1 all-gather.62
  524.8 35.8 all-gather.68
  562.1 36.0 all-gather.66
  599.6 35.9 all-gather.72
  637.0 35.9 all-gather.70
  674.5 35.9 all-gather.74
  712.1 35.9 all-gather.76
  749.5 35.9 all-gather.78
